TPU v7x, 32 devices: a whole 2x2x4 slice. The times are simulated.
32 devices in a mesh: fsdp: 16 (over z, y, core), sp: 2 (over x).
Axes of the slice: x: 2, y: 2, z: 4, core: 2. Of those that a mesh axis runs over, the one named last changes fastest.
Arguments:
- latent_tokens: bfloat16 [16, 1024, 1152], P('fsdp', 'sp'), may hold values from -6 to 6
- caption_tokens: bfloat16 [16, 120, 1152], P('fsdp', 'sp'), may hold values from -1.6953125 to 1.6953125
- caption_len: int32 [16], P('fsdp'), may hold values from 31 to 120, as said below
- time_embed: float32 [16, 6912], P('fsdp'), may hold values from -0.4 to 0.4
- mod_table: bfloat16 [6, 1152], P(None, 'fsdp'), may hold values from -0.3984375 to 0.3984375
- self_input_weight: bfloat16 [1152, 3456], P('fsdp'), may hold values from -0.1875 to 0.1875
- self_query_bias: bfloat16 [1152], P('fsdp'), may hold values from -0.5 to 0.5
- self_value_bias: bfloat16 [1152], P('fsdp'), may hold values from -0.5 to 0.5
- self_output_weight: bfloat16 [1152, 1152], P('fsdp'), may hold values from -1 to 1
- self_output_bias: bfloat16 [1152], P('fsdp'), may hold values from -0.5 to 0.5
- cross_query_weight: bfloat16 [1152, 1152], P('fsdp'), may hold values from -0.1875 to 0.1875
- cross_query_bias: bfloat16 [1152], P('fsdp'), may hold values from -0.5 to 0.5
- cross_keyval_weight: bfloat16 [1152, 2304], P('fsdp'), may hold values from -0.1875 to 0.1875
- cross_value_bias: bfloat16 [1152], P('fsdp'), may hold values from -0.5 to 0.5
- cross_output_weight: bfloat16 [1152, 1152], P('fsdp'), may hold values from -0.375 to 0.375
- cross_output_bias: bfloat16 [1152], P('fsdp'), may hold values from -0.5 to 0.5
- expand_weight: bfloat16 [1152, 4608], P('fsdp'), may hold values from -0.1875 to 0.1875
- expand_bias: bfloat16 [4608], P('fsdp'), may hold values from -0.5 to 0.5
- contract_weight: bfloat16 [4608, 1152], P('fsdp'), may hold values from -0.09375 to 0.09375
- contract_bias: bfloat16 [1152], P('fsdp'), may hold values from -0.5 to 0.5
- out_grad: bfloat16 [16, 1024, 1152], P('fsdp', 'sp'), may hold values from -6 to 6
Outputs:
- block_out: bfloat16 [16, 1024, 1152], P('fsdp', 'sp')
- latent_grad: float32 [16, 1024, 1152], P('fsdp', 'sp')
- caption_grad: float32 [16, 120, 1152], P('fsdp', 'sp')
- time_grad: float32 [16, 6912], P('fsdp')
- mod_table_grad: float32 [6, 1152], P(None, 'fsdp')
- self_input_weight_grad: float32 [1152, 3456], P('fsdp')
- self_query_bias_grad: float32 [1152], P('fsdp')
- self_value_bias_grad: float32 [1152], P('fsdp')
- self_output_weight_grad: float32 [1152, 1152], P('fsdp')
- self_output_bias_grad: float32 [1152], P('fsdp')
- cross_query_weight_grad: float32 [1152, 1152], P('fsdp')
- cross_query_bias_grad: float32 [1152], P('fsdp')
- cross_keyval_weight_grad: float32 [1152, 2304], P('fsdp')
- cross_value_bias_grad: float32 [1152], P('fsdp')
- cross_output_weight_grad: float32 [1152, 1152], P('fsdp')
- cross_output_bias_grad: float32 [1152], P('fsdp')
- expand_weight_grad: float32 [1152, 4608], P('fsdp')
- expand_bias_grad: float32 [4608], P('fsdp')
- contract_weight_grad: float32 [4608, 1152], P('fsdp')
- contract_bias_grad: float32 [1152], P('fsdp')
Inputs may be any that keep to these rules, and one draw needn't show every extreme that they name: caption_len[b] is the number of leading caption tokens of latent b that are attended to; the rest are masked out.
All inputs are finite; a program needn't handle non-finite values.
Results may differ from a plain program's by a relative error of at most 0.025.
Values may be sent and summed in bfloat16 or wider, within the bound.
No kernel may reach another device: no remote copies, remote signals or barrier semaphores. Data moves between devices by JAX's collectives and lax.ppermute only.
A program may use at most 256 MiB of HBM per device.

v0:
```python
from functools import partial

import jax
import jax.numpy as jnp
from jax import lax
from jax.sharding import PartitionSpec as P

HEADS = 16
HEAD_DIM = 72


EPS = 1e-06
NEG = -1e30


def modulated_norm(stream, shift, scale_rows):
    centre = stream - jnp.mean(stream, axis=-1, keepdims=True)
    spread = jnp.mean(centre * centre, axis=-1, keepdims=True)
    return centre * lax.rsqrt(spread + EPS) * (1.0 + scale_rows[:, None, :]) + shift[:, None, :]


def linear(inputs, weight):
    return jnp.einsum("lsd,de->lse", inputs, weight, preferred_element_type=jnp.float32)


def linear_back(grads, weight):
    return jnp.einsum("lse,de->lsd", grads, weight, preferred_element_type=jnp.float32)


def weight_grad(inputs, grads):
    return jnp.einsum("lsd,lse->de", inputs, grads, preferred_element_type=jnp.float32)


def column_sum(grads):
    return jnp.sum(grads, axis=(0, 1), dtype=jnp.float32)


def head_items(tensor, heads):
    latents, length, width = tensor.shape
    return (
        tensor.reshape(latents, length, heads, HEAD_DIM)
        .transpose(0, 2, 1, 3)
        .reshape(latents * heads, length, HEAD_DIM)
    )


def token_rows(tensor, latents):
    items, length, head_width = tensor.shape
    heads = items // latents
    return (
        tensor.reshape(latents, heads, length, head_width)
        .transpose(0, 2, 1, 3)
        .reshape(latents, length, heads * head_width)
    )


def self_forward(operands):
    queries, key_rows, value_rows = operands
    length = queries.shape[0]
    block_rows = min(512, length)
    score_scale = HEAD_DIM ** (-0.5)

    def attend_block(query_block):
        scores = (
            jnp.einsum("qe,ke->qk", query_block, key_rows, preferred_element_type=jnp.float32)
            * score_scale
        )
        row_peak = jnp.max(scores, axis=-1, keepdims=True)
        exponent = jnp.exp(scores - row_peak)
        row_total = jnp.sum(exponent, axis=-1, keepdims=True)
        weights_low = (exponent / row_total).astype(jnp.bfloat16)
        mixed_rows = jnp.einsum(
            "qk,ke->qe", weights_low, value_rows, preferred_element_type=jnp.float32
        )
        return (mixed_rows.astype(jnp.bfloat16), (row_peak + jnp.log(row_total))[:, 0])

    mixed_rows, log_total = lax.map(
        attend_block, queries.reshape(length // block_rows, block_rows, HEAD_DIM)
    )
    return (mixed_rows.reshape(length, HEAD_DIM), log_total.reshape(length))


def self_backward(operands):
    queries, key_rows, value_rows, log_total, grad_rows = operands
    length = queries.shape[0]
    block_rows = min(512, length)
    count_blocks = length // block_rows
    score_scale = HEAD_DIM ** (-0.5)

    def revisit_block(running, pieces):
        key_grad, value_grad = running
        query_block, total_block, grad_block = pieces
        scores = (
            jnp.einsum("qe,ke->qk", query_block, key_rows, preferred_element_type=jnp.float32)
            * score_scale
        )
        weights_full = jnp.exp(scores - total_block[:, None])
        weights_grad = jnp.einsum(
            "qe,ke->qk", grad_block, value_rows, preferred_element_type=jnp.float32
        )
        centred = weights_grad - jnp.sum(weights_full * weights_grad, axis=-1, keepdims=True)
        score_grad = (weights_full * centred).astype(jnp.bfloat16)
        query_grad = (
            jnp.einsum("qk,ke->qe", score_grad, key_rows, preferred_element_type=jnp.float32)
            * score_scale
        )
        key_grad = (
            key_grad
            + jnp.einsum("qk,qe->ke", score_grad, query_block, preferred_element_type=jnp.float32)
            * score_scale
        )
        value_grad = value_grad + jnp.einsum(
            "qk,qe->ke",
            weights_full.astype(jnp.bfloat16),
            grad_block,
            preferred_element_type=jnp.float32,
        )
        return ((key_grad, value_grad), query_grad.astype(jnp.bfloat16))

    zeros_rows = jnp.zeros((length, HEAD_DIM), jnp.float32)
    carried, query_grad = lax.scan(
        revisit_block,
        (zeros_rows, zeros_rows),
        (
            queries.reshape(count_blocks, block_rows, HEAD_DIM),
            log_total.reshape(count_blocks, block_rows),
            grad_rows.reshape(count_blocks, block_rows, HEAD_DIM),
        ),
    )
    return (
        query_grad.reshape(length, HEAD_DIM),
        carried[0].astype(jnp.bfloat16),
        carried[1].astype(jnp.bfloat16),
    )


def on_device(
    latent_tokens,
    caption_tokens,
    caption_len,
    time_embed,
    mod_table,
    self_input_weight,
    self_query_bias,
    self_value_bias,
    self_output_weight,
    self_output_bias,
    cross_query_weight,
    cross_query_bias,
    cross_keyval_weight,
    cross_value_bias,
    cross_output_weight,
    cross_output_bias,
    expand_weight,
    expand_bias,
    contract_weight,
    contract_bias,
    out_grad,
):
    latents, local_len, width = latent_tokens.shape
    heads_local = HEADS // lax.axis_size("sp")
    score_scale = HEAD_DIM ** (-0.5)
    gathered = (
        lax.all_gather(self_input_weight, "fsdp", axis=0, tiled=True),
        lax.all_gather(self_output_weight, "fsdp", axis=0, tiled=True),
        lax.all_gather(cross_query_weight, "fsdp", axis=0, tiled=True),
        lax.all_gather(cross_keyval_weight, "fsdp", axis=0, tiled=True),
        lax.all_gather(cross_output_weight, "fsdp", axis=0, tiled=True),
        lax.all_gather(expand_weight, "fsdp", axis=0, tiled=True),
        lax.all_gather(contract_weight, "fsdp", axis=0, tiled=True),
        lax.all_gather(self_query_bias, "fsdp", axis=0, tiled=True),
        lax.all_gather(self_value_bias, "fsdp", axis=0, tiled=True),
        lax.all_gather(self_output_bias, "fsdp", axis=0, tiled=True),
        lax.all_gather(cross_query_bias, "fsdp", axis=0, tiled=True),
        lax.all_gather(cross_value_bias, "fsdp", axis=0, tiled=True),
        lax.all_gather(cross_output_bias, "fsdp", axis=0, tiled=True),
        lax.all_gather(expand_bias, "fsdp", axis=0, tiled=True),
        lax.all_gather(contract_bias, "fsdp", axis=0, tiled=True),
        lax.all_gather(mod_table, "fsdp", axis=1, tiled=True),
    )
    (
        whole_input,
        whole_output,
        whole_xquery,
        whole_keyval,
        whole_xoutput,
        whole_expand,
        whole_contract,
    ) = gathered[:7]
    bias_query = gathered[7].astype(jnp.float32)
    bias_value = gathered[8].astype(jnp.float32)
    bias_output = gathered[9].astype(jnp.float32)
    bias_xquery = gathered[10].astype(jnp.float32)
    bias_xvalue = gathered[11].astype(jnp.float32)
    bias_xoutput = gathered[12].astype(jnp.float32)
    bias_expand = gathered[13].astype(jnp.float32)
    bias_contract = gathered[14].astype(jnp.float32)
    modulation = gathered[15].astype(jnp.float32)[None] + time_embed.reshape(latents, 6, width)
    stream = latent_tokens.astype(jnp.float32)
    normed_one, norm_one_back = jax.vjp(modulated_norm, stream, modulation[:, 0], modulation[:, 1])
    normed_one = normed_one.astype(jnp.bfloat16)
    projected = linear(normed_one, whole_input)
    queries = (projected[..., :width] + bias_query).astype(jnp.bfloat16)
    key_rows = projected[..., width : 2 * width].astype(jnp.bfloat16)
    value_rows = (projected[..., 2 * width :] + bias_value).astype(jnp.bfloat16)
    head_query, head_key, head_value = (
        lax.all_to_all(queries, "sp", split_axis=2, concat_axis=1, tiled=True),
        lax.all_to_all(key_rows, "sp", split_axis=2, concat_axis=1, tiled=True),
        lax.all_to_all(value_rows, "sp", split_axis=2, concat_axis=1, tiled=True),
    )
    items_query = head_items(head_query, heads_local)
    items_key = head_items(head_key, heads_local)
    items_value = head_items(head_value, heads_local)
    mixed_items, log_total = lax.map(self_forward, (items_query, items_key, items_value))
    mixed_tokens = lax.all_to_all(
        token_rows(mixed_items, latents), "sp", split_axis=1, concat_axis=2, tiled=True
    )
    attended = linear(mixed_tokens, whole_output) + bias_output
    after_attn = stream + modulation[:, 2][:, None, :] * attended
    attn_low = after_attn.astype(jnp.bfloat16)
    cross_queries = (linear(attn_low, whole_xquery) + bias_xquery).astype(jnp.bfloat16)
    caption_all = lax.all_gather(caption_tokens, "sp", axis=1, tiled=True)
    caption_count = caption_all.shape[1]
    keyval = linear(caption_all, whole_keyval)
    cross_keys = keyval[..., :width].astype(jnp.bfloat16)
    cross_values = (keyval[..., width:] + bias_xvalue).astype(jnp.bfloat16)
    query_split = cross_queries.reshape(latents, local_len, HEADS, HEAD_DIM)
    key_split = cross_keys.reshape(latents, caption_count, HEADS, HEAD_DIM)
    value_split = cross_values.reshape(latents, caption_count, HEADS, HEAD_DIM)
    visible = jnp.arange(caption_count)[None, :] < caption_len[:, None]

    def cross_scores():
        raw = (
            jnp.einsum(
                "lshe,lche->lhsc", query_split, key_split, preferred_element_type=jnp.float32
            )
            * score_scale
        )
        return jnp.where(visible[:, None, None, :], raw, NEG)

    scores = cross_scores()
    row_peak = jnp.max(scores, axis=-1, keepdims=True)
    exponent = jnp.exp(scores - row_peak)
    row_total = jnp.sum(exponent, axis=-1, keepdims=True)
    cross_lse = row_peak + jnp.log(row_total)
    weights_low = (exponent / row_total).astype(jnp.bfloat16)
    cross_mixed = jnp.einsum(
        "lhsc,lche->lshe", weights_low, value_split, preferred_element_type=jnp.float32
    )
    cross_mixed = cross_mixed.reshape(latents, local_len, width).astype(jnp.bfloat16)
    crossed = linear(cross_mixed, whole_xoutput) + bias_xoutput
    after_cross = after_attn + crossed
    normed_two, norm_two_back = jax.vjp(
        modulated_norm, after_cross, modulation[:, 3], modulation[:, 4]
    )
    normed_two = normed_two.astype(jnp.bfloat16)
    hidden = linear(normed_two, whole_expand) + bias_expand
    activated, gelu_back = jax.vjp(partial(jax.nn.gelu, approximate=True), hidden)
    activated = activated.astype(jnp.bfloat16)
    fed = linear(activated, whole_contract) + bias_contract
    block_out = (after_cross + modulation[:, 5][:, None, :] * fed).astype(jnp.bfloat16)
    cotangent = out_grad.astype(jnp.float32)
    fed_grad = (modulation[:, 5][:, None, :] * cotangent).astype(jnp.bfloat16)
    gate_two_grad = jnp.sum(cotangent * fed, axis=1)
    contract_wgrad = weight_grad(activated, fed_grad)
    contract_bgrad = column_sum(fed_grad)
    hidden_grad = gelu_back(linear_back(fed_grad, whole_contract))[0].astype(jnp.bfloat16)
    expand_wgrad = weight_grad(normed_two, hidden_grad)
    expand_bgrad = column_sum(hidden_grad)
    cross_stream_grad, shift_two_grad, scale_two_grad = norm_two_back(
        linear_back(hidden_grad, whole_expand)
    )
    cross_stream_grad = cross_stream_grad + cotangent
    crossed_grad = cross_stream_grad.astype(jnp.bfloat16)
    xoutput_wgrad = weight_grad(cross_mixed, crossed_grad)
    xoutput_bgrad = column_sum(crossed_grad)
    mixed_grad = linear_back(crossed_grad, whole_xoutput).astype(jnp.bfloat16)
    mixed_grad = mixed_grad.reshape(latents, local_len, HEADS, HEAD_DIM)
    weights_full = jnp.exp(cross_scores() - cross_lse)
    weights_grad = jnp.einsum(
        "lshe,lche->lhsc", mixed_grad, value_split, preferred_element_type=jnp.float32
    )
    centred = weights_grad - jnp.sum(weights_full * weights_grad, axis=-1, keepdims=True)
    score_grad = (weights_full * centred).astype(jnp.bfloat16)
    xquery_grad = (
        jnp.einsum("lhsc,lche->lshe", score_grad, key_split, preferred_element_type=jnp.float32)
        * score_scale
    )
    xquery_grad = xquery_grad.reshape(latents, local_len, width).astype(jnp.bfloat16)
    key_part = (
        jnp.einsum("lhsc,lshe->lche", score_grad, query_split, preferred_element_type=jnp.float32)
        * score_scale
    )
    value_part = jnp.einsum(
        "lhsc,lshe->lche",
        weights_full.astype(jnp.bfloat16),
        mixed_grad,
        preferred_element_type=jnp.float32,
    )
    keyval_part = jnp.concatenate(
        [
            key_part.reshape(latents, caption_count, width),
            value_part.reshape(latents, caption_count, width),
        ],
        axis=-1,
    )
    keyval_grad = lax.psum_scatter(keyval_part, "sp", scatter_dimension=1, tiled=True).astype(
        jnp.bfloat16
    )
    caption_grad = linear_back(keyval_grad, whole_keyval)
    keyval_wgrad = weight_grad(caption_tokens, keyval_grad)
    xvalue_bgrad = column_sum(keyval_grad[..., width:])
    xquery_wgrad = weight_grad(attn_low, xquery_grad)
    xquery_bgrad = column_sum(xquery_grad)
    attn_stream_grad = cross_stream_grad + linear_back(xquery_grad, whole_xquery)
    gate_one_grad = jnp.sum(attn_stream_grad * attended, axis=1)
    attended_grad = (modulation[:, 2][:, None, :] * attn_stream_grad).astype(jnp.bfloat16)
    output_wgrad = weight_grad(mixed_tokens, attended_grad)
    output_bgrad = column_sum(attended_grad)
    tokens_grad = linear_back(attended_grad, whole_output).astype(jnp.bfloat16)
    heads_grad = lax.all_to_all(tokens_grad, "sp", split_axis=2, concat_axis=1, tiled=True)
    query_items, key_items, value_items = lax.map(
        self_backward,
        (items_query, items_key, items_value, log_total, head_items(heads_grad, heads_local)),
    )
    query_tgrad, key_tgrad, value_tgrad = (
        lax.all_to_all(
            token_rows(query_items, latents), "sp", split_axis=1, concat_axis=2, tiled=True
        ),
        lax.all_to_all(
            token_rows(key_items, latents), "sp", split_axis=1, concat_axis=2, tiled=True
        ),
        lax.all_to_all(
            token_rows(value_items, latents), "sp", split_axis=1, concat_axis=2, tiled=True
        ),
    )
    projected_grad = jnp.concatenate([query_tgrad, key_tgrad, value_tgrad], axis=-1)
    input_wgrad = weight_grad(normed_one, projected_grad)
    query_bgrad = column_sum(query_tgrad)
    value_bgrad = column_sum(value_tgrad)
    stream_part, shift_one_grad, scale_one_grad = norm_one_back(
        linear_back(projected_grad, whole_input)
    )
    latent_grad = attn_stream_grad + stream_part
    embed_part = jnp.stack(
        [
            shift_one_grad,
            scale_one_grad,
            gate_one_grad,
            shift_two_grad,
            scale_two_grad,
            gate_two_grad,
        ],
        axis=1,
    )
    table_part = jnp.sum(embed_part, axis=0)
    embed_part = embed_part.reshape(latents, 6 * width)
    shards = (
        lax.psum_scatter(
            input_wgrad.astype(jnp.bfloat16), "fsdp", scatter_dimension=0, tiled=True
        ).astype(jnp.float32),
        lax.psum_scatter(
            output_wgrad.astype(jnp.bfloat16), "fsdp", scatter_dimension=0, tiled=True
        ).astype(jnp.float32),
        lax.psum_scatter(
            xquery_wgrad.astype(jnp.bfloat16), "fsdp", scatter_dimension=0, tiled=True
        ).astype(jnp.float32),
        lax.psum_scatter(
            keyval_wgrad.astype(jnp.bfloat16), "fsdp", scatter_dimension=0, tiled=True
        ).astype(jnp.float32),
        lax.psum_scatter(
            xoutput_wgrad.astype(jnp.bfloat16), "fsdp", scatter_dimension=0, tiled=True
        ).astype(jnp.float32),
        lax.psum_scatter(
            expand_wgrad.astype(jnp.bfloat16), "fsdp", scatter_dimension=0, tiled=True
        ).astype(jnp.float32),
        lax.psum_scatter(
            contract_wgrad.astype(jnp.bfloat16), "fsdp", scatter_dimension=0, tiled=True
        ).astype(jnp.float32),
        lax.psum_scatter(
            query_bgrad.astype(jnp.bfloat16), "fsdp", scatter_dimension=0, tiled=True
        ).astype(jnp.float32),
        lax.psum_scatter(
            value_bgrad.astype(jnp.bfloat16), "fsdp", scatter_dimension=0, tiled=True
        ).astype(jnp.float32),
        lax.psum_scatter(
            output_bgrad.astype(jnp.bfloat16), "fsdp", scatter_dimension=0, tiled=True
        ).astype(jnp.float32),
        lax.psum_scatter(
            xquery_bgrad.astype(jnp.bfloat16), "fsdp", scatter_dimension=0, tiled=True
        ).astype(jnp.float32),
        lax.psum_scatter(
            xvalue_bgrad.astype(jnp.bfloat16), "fsdp", scatter_dimension=0, tiled=True
        ).astype(jnp.float32),
        lax.psum_scatter(
            xoutput_bgrad.astype(jnp.bfloat16), "fsdp", scatter_dimension=0, tiled=True
        ).astype(jnp.float32),
        lax.psum_scatter(
            expand_bgrad.astype(jnp.bfloat16), "fsdp", scatter_dimension=0, tiled=True
        ).astype(jnp.float32),
        lax.psum_scatter(
            contract_bgrad.astype(jnp.bfloat16), "fsdp", scatter_dimension=0, tiled=True
        ).astype(jnp.float32),
        lax.psum_scatter(
            table_part.astype(jnp.bfloat16), "fsdp", scatter_dimension=1, tiled=True
        ).astype(jnp.float32),
    )
    totals = (
        lax.psum(shards[0].astype(jnp.bfloat16), "sp").astype(jnp.float32),
        lax.psum(shards[1].astype(jnp.bfloat16), "sp").astype(jnp.float32),
        lax.psum(shards[2].astype(jnp.bfloat16), "sp").astype(jnp.float32),
        lax.psum(shards[3].astype(jnp.bfloat16), "sp").astype(jnp.float32),
        lax.psum(shards[4].astype(jnp.bfloat16), "sp").astype(jnp.float32),
        lax.psum(shards[5].astype(jnp.bfloat16), "sp").astype(jnp.float32),
        lax.psum(shards[6].astype(jnp.bfloat16), "sp").astype(jnp.float32),
        lax.psum(shards[7].astype(jnp.bfloat16), "sp").astype(jnp.float32),
        lax.psum(shards[8].astype(jnp.bfloat16), "sp").astype(jnp.float32),
        lax.psum(shards[9].astype(jnp.bfloat16), "sp").astype(jnp.float32),
        lax.psum(shards[10].astype(jnp.bfloat16), "sp").astype(jnp.float32),
        lax.psum(shards[11].astype(jnp.bfloat16), "sp").astype(jnp.float32),
        lax.psum(shards[12].astype(jnp.bfloat16), "sp").astype(jnp.float32),
        lax.psum(shards[13].astype(jnp.bfloat16), "sp").astype(jnp.float32),
        lax.psum(shards[14].astype(jnp.bfloat16), "sp").astype(jnp.float32),
        lax.psum(shards[15].astype(jnp.bfloat16), "sp").astype(jnp.float32),
        lax.psum(embed_part.astype(jnp.bfloat16), "sp").astype(jnp.float32),
    )
    summed = tuple(totals[:16])
    time_grad = totals[16]
    return (
        block_out,
        latent_grad,
        caption_grad,
        time_grad,
        summed[15],
        summed[0],
        summed[7],
        summed[8],
        summed[1],
        summed[9],
        summed[2],
        summed[10],
        summed[3],
        summed[11],
        summed[4],
        summed[12],
        summed[5],
        summed[13],
        summed[6],
        summed[14],
    )


def solution(mesh):
    in_specs = (
        P("fsdp", "sp", None),
        P("fsdp", "sp", None),
        P("fsdp"),
        P("fsdp", None),
        P(None, "fsdp"),
        P("fsdp", None),
        P("fsdp"),
        P("fsdp"),
        P("fsdp", None),
        P("fsdp"),
        P("fsdp", None),
        P("fsdp"),
        P("fsdp", None),
        P("fsdp"),
        P("fsdp", None),
        P("fsdp"),
        P("fsdp", None),
        P("fsdp"),
        P("fsdp", None),
        P("fsdp"),
        P("fsdp", "sp", None),
    )
    out_specs = (
        P("fsdp", "sp", None),
        P("fsdp", "sp", None),
        P("fsdp", "sp", None),
        P("fsdp", None),
        P(None, "fsdp"),
        P("fsdp", None),
        P("fsdp"),
        P("fsdp"),
        P("fsdp", None),
        P("fsdp"),
        P("fsdp", None),
        P("fsdp"),
        P("fsdp", None),
        P("fsdp"),
        P("fsdp", None),
        P("fsdp"),
        P("fsdp", None),
        P("fsdp"),
        P("fsdp", None),
        P("fsdp"),
    )
    return jax.shard_map(
        on_device, mesh=mesh, in_specs=in_specs, out_specs=out_specs, check_vma=False
    )
```

profile of v0, /device:TPU:8, one launch (start us, length us, event | category | flops | bytes accessed | tf_op | source)
XLA Modules:
  0.0 1591.8 jit_solution(8860474305623939224)
XLA Ops:
  14.7 19.4 %all-gather = bf16[16,72,6]{1,2,0:T(8,128)(2,1)S(1)} all-gather(bf16[1,72,6]{1,2,0:T(8,128)(2,1)} %bitcast.446), channel_id=1, replica_groups=mesh['fsdp'=16,'sp'=2] {'fsdp'}, dimensions={0}, use_global_device_ids=true | all-gather | bytes 14688 | tf_op jit(solution)/shard_map/all_gather | solution.py:179
  36.2 53.9 %all-reduce.23 = (bf16[1152]{0:T(1024)(128)(2,1)}, bf16[1152]{0:T(1024)(128)(2,1)S(1)}, bf16[1152]{0:T(1024)(128)(2,1)S(1)}, bf16[1152]{0:T(1024)(128)(2,1)}, bf...) all-reduce(bf16[1152]{0:T(1024)(128)(2,1)S(1)} %dynamic-update-slic, ...), channel_id=1, replica_groups=mesh['fsdp'=16,'sp'=2] {'fsdp'}, use_global_device_ids=true, to_apply=%add.3 | all-reduce | flops 12672 | bytes 50688
  179.1 12.1 all_gather.57
  212.8 59.8 %while.54 = (s32[]{:T(128)}, bf16[8,1024,72]{1,2,0:T(8,128)(2,1)S(1)}, f32[8,1024]{1,0:T(8,128)}, bf16[8,1024,72]{2,1,0:T(8,128)(2,1)}, bf16[8,1024,72]{2,1,0:T(...) while((s32[]{:T(128)}, ...), condition=%wide.region_7.8_spmd, body=%wide.region_2.7_spmd.sunk | while | flops 155749888 | bytes 8827182 | solution.py:214
  276.8 9.9 reduce.54
  339.6 22.8 %all-gather.19.cloned.1.call-done = bf16[1152,4608]{1,0:T(8,128)(2,1)} async-done(((bf16[72,4608]{1,0:T(8,128)(2,1)}), bf16[1152,4608]{1,0:T(8,128)(2,1)}) %all-gather.19.cloned.1.call-update) | async-done | bytes 10616848 | tf_op jit(solution)/shard_map/all_gather | solution.py:169
  362.4 12.6 fusion.100
  375.0 76.5 %all-gather.21.cloned.1.call-done = bf16[4608,1152]{1,0:T(8,128)(2,1)} async-done(((bf16[288,1152]{1,0:T(8,128)(2,1)}), bf16[4608,1152]{1,0:T(8,128)(2,1)}) %all-gather.21.cloned.1.call-update) | async-done | bytes 10616848 | tf_op jit(solution)/shard_map/all_gather | solution.py:170
  451.6 16.1 %fusion.109 = (bf16[4608]{0:T(1024)(128)(2,1)}, bf16[512,4608]{1,0:T(8,128)(2,1)S(1)}) fusion(f32[512,4608]{1,0:T(8,128)} %fusion.100, f32[4608]{0:T(1024)S(1)} %copy-done.57, bf16[4608,1152]{1,0:T(8,128)(2,1)} %all-gather.21.cloned.1.call-done, bf16[1,512,1152]{2,1,0:T(8,128)(2,1)S(1)} %copy-done.29, f32[1152]{0:T(1024)S(1)} %copy-done.52), kind=kOutput, calls=%fused_computation.201 | convolution fusion | flops 5489487360 | bytes 25984512 | tf_op jit(solution)/shard_map/lse,de->lsd/dot_general | solution.py:27
  467.7 12.8 fusion.56
  480.5 15.5 fusion.53
  517.8 205.2 %all-reduce.30 = bf16[1,120,2304]{2,0,1:T(2,128)(2,1)} all-reduce(f32[1,120,2304]{2,0,1:T(1,128)S(1)} %pad_maximum_fusion), channel_id=2, replica_groups=mesh['fsdp'=16,'sp'=2] {'sp'}, use_global_device_ids=true, to_apply=%region_22.23.clone | all-reduce | flops 276480 | bytes 1658880
  785.1 10.4 all-to-all-done.4
  803.2 224.8 %while.56 = (s32[]{:T(128)}, bf16[8,1024,72]{1,2,0:T(8,128)(2,1)}, bf16[8,1024,72]{1,2,0:T(8,128)(2,1)}, bf16[8,1024,72]{1,2,0:T(8,128)(2,1)}, bf16[8,1024,72]{2...) while((s32[]{:T(128)}, bf16[8,1024,72]{1,2,0:T(8,128)(2,1)}, ...), condition=%wide.region_19.20_spmd, body=%wide.region_15.19_spmd.sunk | while | flops 382270976 | bytes 21449112 | solution.py:322
  809.8 17.2 %while.58 = (s32[]{:T(128)}, f32[1024,72]{0,1:T(8,128)}, f32[1024,72]{0,1:T(8,128)}, bf16[2,512,72]{1,2,0:T(8,128)(2,1)S(1)}, bf16[2,512,72]{2,1,0:T(8,128)(2,1)...) while((s32[]{:T(128)}, f32[1024,72]{0,1:T(8,128)}, ...), condition=%wide.region_18.18_spmd.clone, body=%wide.region_16.17_spmd.clone.sunk | while | flops 382123520 | bytes 18188440 | solution.py:121
  837.9 17.3 %while.58 = (s32[]{:T(128)}, f32[1024,72]{0,1:T(8,128)}, f32[1024,72]{0,1:T(8,128)}, bf16[2,512,72]{1,2,0:T(8,128)(2,1)S(1)}, bf16[2,512,72]{2,1,0:T(8,128)(2,1)...) while((s32[]{:T(128)}, f32[1024,72]{0,1:T(8,128)}, ...), condition=%wide.region_18.18_spmd.clone, body=%wide.region_16.17_spmd.clone.sunk | while | flops 382123520 | bytes 18188440 | solution.py:121
  866.1 17.2 %while.58 = (s32[]{:T(128)}, f32[1024,72]{0,1:T(8,128)}, f32[1024,72]{0,1:T(8,128)}, bf16[2,512,72]{1,2,0:T(8,128)(2,1)S(1)}, bf16[2,512,72]{2,1,0:T(8,128)(2,1)...) while((s32[]{:T(128)}, f32[1024,72]{0,1:T(8,128)}, ...), condition=%wide.region_18.18_spmd.clone, body=%wide.region_16.17_spmd.clone.sunk | while | flops 382123520 | bytes 18188440 | solution.py:121
  894.2 17.2 %while.58 = (s32[]{:T(128)}, f32[1024,72]{0,1:T(8,128)}, f32[1024,72]{0,1:T(8,128)}, bf16[2,512,72]{1,2,0:T(8,128)(2,1)S(1)}, bf16[2,512,72]{2,1,0:T(8,128)(2,1)...) while((s32[]{:T(128)}, f32[1024,72]{0,1:T(8,128)}, ...), condition=%wide.region_18.18_spmd.clone, body=%wide.region_16.17_spmd.clone.sunk | while | flops 382123520 | bytes 18188440 | solution.py:121
  922.3 17.2 %while.58 = (s32[]{:T(128)}, f32[1024,72]{0,1:T(8,128)}, f32[1024,72]{0,1:T(8,128)}, bf16[2,512,72]{1,2,0:T(8,128)(2,1)S(1)}, bf16[2,512,72]{2,1,0:T(8,128)(2,1)...) while((s32[]{:T(128)}, f32[1024,72]{0,1:T(8,128)}, ...), condition=%wide.region_18.18_spmd.clone, body=%wide.region_16.17_spmd.clone.sunk | while | flops 382123520 | bytes 18188440 | solution.py:121
  950.3 17.2 %while.58 = (s32[]{:T(128)}, f32[1024,72]{0,1:T(8,128)}, f32[1024,72]{0,1:T(8,128)}, bf16[2,512,72]{1,2,0:T(8,128)(2,1)S(1)}, bf16[2,512,72]{2,1,0:T(8,128)(2,1)...) while((s32[]{:T(128)}, f32[1024,72]{0,1:T(8,128)}, ...), condition=%wide.region_18.18_spmd.clone, body=%wide.region_16.17_spmd.clone.sunk | while | flops 382123520 | bytes 18188440 | solution.py:121
  978.5 17.2 %while.58 = (s32[]{:T(128)}, f32[1024,72]{0,1:T(8,128)}, f32[1024,72]{0,1:T(8,128)}, bf16[2,512,72]{1,2,0:T(8,128)(2,1)S(1)}, bf16[2,512,72]{2,1,0:T(8,128)(2,1)...) while((s32[]{:T(128)}, f32[1024,72]{0,1:T(8,128)}, ...), condition=%wide.region_18.18_spmd.clone, body=%wide.region_16.17_spmd.clone.sunk | while | flops 382123520 | bytes 18188440 | solution.py:121
  1006.6 17.2 %while.58 = (s32[]{:T(128)}, f32[1024,72]{0,1:T(8,128)}, f32[1024,72]{0,1:T(8,128)}, bf16[2,512,72]{1,2,0:T(8,128)(2,1)S(1)}, bf16[2,512,72]{2,1,0:T(8,128)(2,1)...) while((s32[]{:T(128)}, f32[1024,72]{0,1:T(8,128)}, ...), condition=%wide.region_18.18_spmd.clone, body=%wide.region_16.17_spmd.clone.sunk | while | flops 382123520 | bytes 18188440 | solution.py:121
  1033.1 10.1 reduce.56
  1056.3 10.1 reduce.57
  1079.7 10.1 reduce.58
  1125.5 10.1 convolution_convert_fusion.3
  1137.2 10.8 convolution_convert_fusion.2
  1149.3 13.7 convolution_convert_fusion.1
  1176.7 59.6 %reduce-scatter.25.cloned.1.call-done = bf16[72,3456]{1,0:T(8,128)(2,1)} async-done(((bf16[1152,3456]{1,0:T(8,128)(2,1)}), bf16[72,3456]{1,0:T(8,128)(2,1)}) %reduce-scatter.25.cloned.1.call-update) | async-done | bytes 497680
  1236.3 124.2 %reduce-scatter.19.cloned.1.call-done = bf16[72,4608]{1,0:T(8,128)(2,1)} async-done(((bf16[1152,4608]{1,0:T(8,128)(2,1)}), bf16[72,4608]{1,0:T(8,128)(2,1)}) %reduce-scatter.19.cloned.1.call-update) | async-done | bytes 663568 | tf_op jit(solution)/shard_map/reduce_scatter | solution.py:374
  1360.4 124.0 %reduce-scatter.21.cloned.1.call-done = bf16[288,1152]{1,0:T(8,128)(2,1)} async-done(((bf16[4608,1152]{1,0:T(8,128)(2,1)}), bf16[288,1152]{1,0:T(8,128)(2,1)}) %reduce-scatter.21.cloned.1.call-update) | async-done | bytes 663568 | tf_op jit(solution)/shard_map/reduce_scatter | solution.py:377
  1507.7 52.5 %all-reduce.22 = (bf16[6,1152]{1,0:T(8,128)(2,1)S(1)}, bf16[1152]{0:T(1024)(128)(2,1)S(1)}, bf16[1152]{0:T(1024)(128)(2,1)S(1)}, bf16[1152]{0:T(1024)(128)(2,1)S...) all-reduce(bf16[6,1152]{1,0:T(8,128)(2,1)S(1)} %bitcast.443, ...), channel_id=3, replica_groups=mesh['fsdp'=16,'sp'=2] {'fsdp'}, use_global_device_ids=true, to_apply=%region_30.31.clone | all-reduce | flops 19584 | bytes 78336
  (819 shorter events, 707.9 us)
Async XLA Ops:
  7.3 28.5 %copy-start.89 = (bf16[72]{0:T(256)(128)(2,1)S(1)}, bf16[72]{0:T(256)(128)(2,1)}, u32[]{:S(2)}) copy-start(bf16[72]{0:T(256)(128)(2,1)} %param.48) | copy-start | bytes 436
  7.3 28.7 %copy-start.82 = (bf16[288]{0:T(512)(128)(2,1)S(1)}, bf16[288]{0:T(512)(128)(2,1)}, u32[]{:S(2)}) copy-start(bf16[288]{0:T(512)(128)(2,1)} %param.46) | copy-start | bytes 1732
  7.3 83.5 %copy-start.2 = (bf16[1,512,1152]{2,1,0:T(8,128)(2,1)S(1)}, bf16[1,512,1152]{2,1,0:T(8,128)(2,1)}, u32[]{:S(2)}) copy-start(bf16[1,512,1152]{2,1,0:T(8,128)(2,1)} %param.29) | copy-start | bytes 3538948
  7.3 84.2 %all-gather.9.cloned.1.call-start = ((), (), s32[]{:S(2)}) async-start(), calls=%async_computation.15 | async-start | bytes 8460288 | tf_op jit(solution)/shard_map/all_gather | solution.py:164
  8.0 284.8 %all-gather.13.cloned.1.call-start = ((), (), s32[]{:S(2)}) async-start(), calls=%async_computation.17 | async-start | bytes 5640192 | tf_op jit(solution)/shard_map/all_gather | solution.py:167
  8.8 305.0 %all-gather.11.cloned.1.call-start = ((), (), s32[]{:S(2)}) async-start(), calls=%async_computation.16 | async-start | bytes 2820096 | tf_op jit(solution)/shard_map/all_gather | solution.py:165
  9.5 310.2 %all-gather.15.cloned.1.call-start = ((), (), s32[]{:S(2)}) async-start(), calls=%async_computation.18 | async-start | bytes 2820096 | tf_op jit(solution)/shard_map/all_gather | solution.py:166
  10.1 323.3 %all-gather.17.cloned.1.call-start = ((), (), s32[]{:S(2)}) async-start(), calls=%async_computation.19 | async-start | bytes 2820096 | tf_op jit(solution)/shard_map/all_gather | solution.py:168
  10.7 351.7 %all-gather.19.cloned.1.call-start = ((), (), s32[]{:S(2)}) async-start(), calls=%async_computation.20 | async-start | bytes 11280384 | tf_op jit(solution)/shard_map/all_gather | solution.py:169
  121.2 25.1 %all-to-all-start = ((bf16[2,2,147456]{2,1,0:T(2,128)(2,1)}), bf16[2,2,147456]{2,1,0:T(2,128)(2,1)}, u32[]{:S(2)}, u32[]{:S(2)}) async-start(bf16[2,2,147456]{2,1,0:T(2,128)(2,1)} %reshape.686), calls=%async_computation | async-start | bytes 2359296 | tf_op jit(solution)/shard_map/all_to_all | solution.py:207
  146.3 22.2 %all-to-all-start.1 = ((bf16[2,2,147456]{2,1,0:T(2,128)(2,1)}), bf16[2,2,147456]{2,1,0:T(2,128)(2,1)}, u32[]{:S(2)}, u32[]{:S(2)}) async-start(bf16[2,2,147456]{2,1,0:T(2,128)(2,1)} %reshape.688), calls=%async_computation.1 | async-start | bytes 2359296 | tf_op jit(solution)/shard_map/all_to_all | solution.py:208
  168.5 37.1 %all-to-all-start.2 = ((bf16[2,2,147456]{2,1,0:T(2,128)(2,1)}), bf16[2,2,147456]{2,1,0:T(2,128)(2,1)}, u32[]{:S(2)}, u32[]{:S(2)}) async-start(bf16[2,2,147456]{2,1,0:T(2,128)(2,1)} %reshape.690), calls=%async_computation.2 | async-start | bytes 2359296 | tf_op jit(solution)/shard_map/all_to_all | solution.py:209
  173.2 278.4 %all-gather.21.cloned.1.call-start = ((), (), s32[]{:S(2)}) async-start(), calls=%async_computation.21 | async-start | bytes 11280384 | tf_op jit(solution)/shard_map/all_gather | solution.py:170
  289.1 14.7 all-to-all-start.3
  292.7 881.9 %reduce-scatter.23.cloned.1.call-start = ((), (), s32[]{:S(2)}) async-start(), calls=%async_computation.24 | async-start | bytes 5640192
  337.8 142.7 %copy-start.67 = (f32[512]{0:T(512)}, f32[512]{0:T(512)S(1)}, u32[]{:S(2)}) copy-start(f32[512]{0:T(512)S(1)} %broadcast_multiply_fusion) | copy-start | bytes 6148
  339.6 140.9 %copy-start.81 = (f32[512]{0:T(512)}, f32[512]{0:T(512)S(1)}, u32[]{:S(2)}) copy-start(f32[512]{0:T(512)S(1)} %fusion.93) | copy-start | bytes 6148
  362.4 89.2 %copy-start.29 = (bf16[1,512,1152]{2,1,0:T(8,128)(2,1)S(1)}, bf16[1,512,1152]{2,1,0:T(8,128)(2,1)}, u32[]{:S(2)}) copy-start(bf16[1,512,1152]{2,1,0:T(8,128)(2,1)} %param.49) | copy-start | bytes 3538948
  362.4 89.2 %copy-start.52 = (f32[1152]{0:T(1024)S(1)}, f32[1152]{0:T(1024)}, u32[]{:S(2)}) copy-start(f32[1152]{0:T(1024)} %get-tuple-element.497) | copy-start | bytes 13828
  362.4 89.2 %copy-start.57 = (f32[4608]{0:T(1024)S(1)}, f32[4608]{0:T(1024)}, u32[]{:S(2)}) copy-start(f32[4608]{0:T(1024)} %convert_element_type.323) | copy-start | bytes 55300
  517.8 207.6 %copy-start.42 = (bf16[1,60,1152]{2,1,0:T(8,128)(2,1)S(1)}, bf16[1,60,1152]{2,1,0:T(8,128)(2,1)}, u32[]{:S(2)}) copy-start(bf16[1,60,1152]{2,1,0:T(8,128)(2,1)} %param.30) | copy-start | bytes 414724
  737.9 438.8 %reduce-scatter.27.cloned.1.call-start = ((), (), s32[]{:S(2)}) async-start(), calls=%async_computation.26 | async-start | bytes 2820096
  751.1 425.6 %reduce-scatter.29.cloned.1.call-start = ((), (), s32[]{:S(2)}) async-start(), calls=%async_computation.27 | async-start | bytes 2820096
  777.7 17.8 %all-to-all-start.4 = ((bf16[2,2,147456]{2,1,0:T(2,128)(2,1)}), bf16[2,2,147456]{2,1,0:T(2,128)(2,1)S(1)}, u32[]{:S(2)}, u32[]{:S(2)}) async-start(bf16[2,2,147456]{2,1,0:T(2,128)(2,1)} %reshape.694), calls=%async_computation.4 | async-start | bytes 2359296 | tf_op jit(solution)/shard_map/all_to_all | solution.py:321
  781.3 395.4 %reduce-scatter.31.cloned.1.call-start = ((), (), s32[]{:S(2)}) async-start(), calls=%async_computation.28 | async-start | bytes 2820096
  1046.7 23.2 %all-to-all-start.7 = ((bf16[2,2,147456]{2,1,0:T(2,128)(2,1)}), bf16[2,2,147456]{2,1,0:T(2,128)(2,1)}, u32[]{:S(2)}, u32[]{:S(2)}) async-start(bf16[2,2,147456]{2,1,0:T(2,128)(2,1)} %reshape.696), calls=%async_computation.7 | async-start | bytes 2359296 | tf_op jit(solution)/shard_map/all_to_all | solution.py:333
  1069.8 23.4 %all-to-all-start.6 = ((bf16[2,2,147456]{2,1,0:T(2,128)(2,1)}), bf16[2,2,147456]{2,1,0:T(2,128)(2,1)}, u32[]{:S(2)}, u32[]{:S(2)}) async-start(bf16[2,2,147456]{2,1,0:T(2,128)(2,1)} %reshape.698), calls=%async_computation.6 | async-start | bytes 2359296 | tf_op jit(solution)/shard_map/all_to_all | solution.py:330
  1093.2 22.5 %all-to-all-start.5 = ((bf16[2,2,147456]{2,1,0:T(2,128)(2,1)}), bf16[2,2,147456]{2,1,0:T(2,128)(2,1)}, u32[]{:S(2)}, u32[]{:S(2)}) async-start(bf16[2,2,147456]{2,1,0:T(2,128)(2,1)} %reshape.700), calls=%async_computation.5 | async-start | bytes 2359296 | tf_op jit(solution)/shard_map/all_to_all | solution.py:327
  1097.7 138.6 %reduce-scatter.25.cloned.1.call-start = ((), (), s32[]{:S(2)}) async-start(), calls=%async_computation.25 | async-start | bytes 8460288
  1135.6 224.8 %reduce-scatter.19.cloned.1.call-start = ((), (), s32[]{:S(2)}) async-start(), calls=%async_computation.22 | async-start | bytes 11280384 | tf_op jit(solution)/shard_map/reduce_scatter | solution.py:374
  1148.0 336.4 %reduce-scatter.21.cloned.1.call-start = ((), (), s32[]{:S(2)}) async-start(), calls=%async_computation.23 | async-start | bytes 11280384 | tf_op jit(solution)/shard_map/reduce_scatter | solution.py:377
  1163.1 412.1 %all-reduce.29.cloned.1.call-start = ((), (), s32[]{:S(2)}) async-start(), calls=%async_computation.29 | async-start | bytes 5824512 | tf_op jit(solution)/shard_map/psum | solution.py:412
  (84 other events, 608.0 us)
Sparse Core Ops, SparseCore 0:
  10.3 73.7 all-gather.8
  86.2 55.3 all-gather.12
  143.8 41.7 all-gather.10
  187.6 42.0 all-gather.14
  231.6 42.0 all-gather.16
  275.8 86.5 all-gather.18
  364.7 86.8 all-gather.20
  738.1 77.3 reduce-scatter.22
  819.3 63.0 reduce-scatter.26
  886.6 62.7 reduce-scatter.28
  953.4 62.8 reduce-scatter.30
  1135.7 100.4 reduce-scatter.24
  1240.3 120.0 reduce-scatter.18
  1364.3 120.0 reduce-scatter.20
  1487.6 82.1 all-reduce.28
where the time goes:
time: 1620 us; the launch traced here: 1590 us
  waiting for transfers between devices  428 us (26%)
  blocking collectives  352 us (22%)
  matrix products  311 us (19%)
  local copies, waits for them, and re-layouts  287 us (18%)
  other arithmetic  157 us (10%)
  starting transfers between devices  35.7 us (2%)
  between operations  19.5 us (1%)
    unnamed x3, blocking collectives  312 us
    reduce_scatter x1, waiting for transfers between devices, on_device(): lax.psum_scatter(expand_wgrad.astype(jnp.bfloat16), 'fsdp', scatter_dimen...  124 us
    reduce_scatter x1, waiting for transfers between devices, on_device(): lax.psum_scatter(contract_wgrad.astype(jnp.bfloat16), 'fsdp', scatter_dim...  124 us
    unnamed x245, local copies, waits for them, and re-layouts  88.9 us
    all_gather x1, waiting for transfers between devices, on_device(): lax.all_gather(contract_weight, 'fsdp', axis=0, tiled=True)  76.5 us
    unnamed x9, other arithmetic  74.6 us
    unnamed x20, waiting for transfers between devices  64 us
    dot_general x7, matrix products, linear_back(): jnp.einsum('lse,de->lsd', grads, weight, preferred_element_type=jnp.float32)  55.3 us
  transfers between devices with their start and end apart: 23, of which 7 were waited for; matrix products, arithmetic and copies ran while one was open for 41% of the time, Pallas kernels for 0%

commit v1 on v0

v1 whole, which is shorter than its diff:
```python
from functools import partial

import jax
import jax.numpy as jnp
from jax import lax
from jax.experimental import pallas as pl
from jax.experimental.pallas import tpu as pltpu
from jax.sharding import PartitionSpec as P

HEADS = 16
HD = 72
SCALE = HD**-0.5
EPS = 1e-06
NEG = -1e30
F32 = jnp.float32
BF = jnp.bfloat16
NT = (((1,), (1,)), ((), ()))
TN = (((0,), (0,)), ((), ()))
NN = (((1,), (0,)), ((), ()))
VMEM = 56 << 20


def dot(a, b, dims=NN):
    return lax.dot_general(a, b, dims, preferred_element_type=F32)


def self_fwd_kernel(q_ref, k_ref, v_ref, o_ref, lse_ref, *, heads):
    for h in range(heads):
        sl = slice(HD * h, HD * h + HD)
        q, k, v = q_ref[0, :, sl], k_ref[0, :, sl], v_ref[0, :, sl]
        s = dot(k, q, NT) * SCALE
        m = jnp.max(s, axis=0, keepdims=True)
        p = jnp.exp(s - m)
        total = jnp.sum(p, axis=0, keepdims=True)
        o = dot(v, p.astype(BF), TN) * (1.0 / total)
        o_ref[0, :, sl] = o.T.astype(BF)
        lse_ref[0, h : h + 1, :] = m + jnp.log(total)


def self_bwd_kernel(q_ref, k_ref, v_ref, g_ref, lse_ref, dq_ref, dk_ref, dv_ref, *, heads):
    for h in range(heads):
        sl = slice(HD * h, HD * h + HD)
        q, k, v, g = q_ref[0, :, sl], k_ref[0, :, sl], v_ref[0, :, sl], g_ref[0, :, sl]
        p = jnp.exp(dot(k, q, NT) * SCALE - lse_ref[0, h : h + 1, :])
        dp = dot(v, g, NT)
        delta = jnp.sum(p * dp, axis=0, keepdims=True)
        ds = (p * (dp - delta)).astype(BF)
        dv_ref[0, :, sl] = dot(p.astype(BF), g).astype(BF)
        dk_ref[0, :, sl] = (dot(ds, q) * SCALE).astype(BF)
        dq_ref[0, :, sl] = (dot(k, ds, TN) * SCALE).T.astype(BF)


def cross_fwd_kernel(q_ref, k_ref, v_ref, bias_ref, o_ref, lse_ref):
    for h in range(HEADS):
        sl = slice(HD * h, HD * h + HD)
        q, k, v = q_ref[0, :, sl], k_ref[0, :, sl], v_ref[0, :, sl]
        s = dot(k, q, NT) * SCALE + bias_ref[0]
        m = jnp.max(s, axis=0, keepdims=True)
        p = jnp.exp(s - m)
        total = jnp.sum(p, axis=0, keepdims=True)
        o = dot(v, p.astype(BF), TN) * (1.0 / total)
        o_ref[0, :, sl] = o.T.astype(BF)
        lse_ref[0, h : h + 1, :] = m + jnp.log(total)


def cross_bwd_kernel(q_ref, k_ref, v_ref, g_ref, bias_ref, lse_ref, dq_ref, dk_ref, dv_ref):
    for h in range(HEADS):
        sl = slice(HD * h, HD * h + HD)
        q, k, v, g = q_ref[0, :, sl], k_ref[0, :, sl], v_ref[0, :, sl], g_ref[0, :, sl]
        p = jnp.exp(dot(k, q, NT) * SCALE + bias_ref[0] - lse_ref[0, h : h + 1, :])
        dp = dot(v, g, NT)
        delta = jnp.sum(p * dp, axis=0, keepdims=True)
        ds = (p * (dp - delta)).astype(BF)
        dv_ref[0, :, sl] = dot(p.astype(BF), g).astype(BF)
        dk_ref[0, :, sl] = (dot(ds, q) * SCALE).astype(BF)
        dq_ref[0, :, sl] = (dot(k, ds, TN) * SCALE).T.astype(BF)


def per_latent(kernel, ins, outs, flops):
    def spec(shape):
        return pl.BlockSpec((1,) + tuple(shape[1:]), lambda i: (i, 0, 0))

    nbytes = sum(a.size * a.dtype.itemsize for a in ins)
    return pl.pallas_call(
        kernel,
        grid=(ins[0].shape[0],),
        in_specs=[spec(a.shape) for a in ins],
        out_specs=[spec(s) for s, _ in outs],
        out_shape=[jax.ShapeDtypeStruct(s, d) for s, d in outs],
        compiler_params=pltpu.CompilerParams(vmem_limit_bytes=VMEM),
        cost_estimate=pl.CostEstimate(flops=flops, bytes_accessed=2 * nbytes, transcendentals=0),
    )(*ins)


def self_forward(q, k, v):
    n, t, w = q.shape
    heads = w // HD
    return per_latent(
        partial(self_fwd_kernel, heads=heads),
        (q, k, v),
        [(q.shape, BF), ((n, heads, t), F32)],
        4 * n * heads * t * t * 256,
    )


def self_backward(q, k, v, g, lse):
    n, t, w = q.shape
    heads = w // HD
    return per_latent(
        partial(self_bwd_kernel, heads=heads),
        (q, k, v, g, lse),
        [(q.shape, BF)] * 3,
        10 * n * heads * t * t * 256,
    )


def cross_forward(q, k, v, bias):
    n, t, _ = q.shape
    return per_latent(
        cross_fwd_kernel, (q, k, v, bias), [(q.shape, BF), ((n, HEADS, t), F32)], 4 * n * HEADS * t * 128 * 256
    )


def cross_backward(q, k, v, g, bias, lse):
    n, t, _ = q.shape
    return per_latent(
        cross_bwd_kernel,
        (q, k, v, g, bias, lse),
        [(q.shape, BF), (k.shape, BF), (k.shape, BF)],
        10 * n * HEADS * t * 128 * 256,
    )


def swap(x):
    return lax.ppermute(x, "sp", [(0, 1), (1, 0)])


def pick(x, index, axis):
    return lax.dynamic_index_in_dim(x, index, axis, keepdims=False)


def gather_tokens(x, nsp):
    if nsp == 2:
        return jnp.concatenate([x, swap(x)], axis=1)
    return lax.all_gather(x, "sp", axis=1, tiled=True)


def scatter_tokens(x, nsp):
    if nsp == 2:
        half = x.shape[1] // 2
        return x[:, :half].astype(F32) + swap(x[:, half:].astype(BF)).astype(F32)
    return lax.psum_scatter(x.astype(BF), "sp", scatter_dimension=1, tiled=True).astype(F32)


def in_order(own, other, index, axis=-1):
    return jnp.where(
        index == 0, jnp.concatenate([own, other], axis=axis), jnp.concatenate([other, own], axis=axis)
    )


def halves(x, index, axis=-1):
    low, high = jnp.split(x, 2, axis=axis)
    return jnp.where(index == 0, low, high), jnp.where(index == 0, high, low)


def heads_to_tokens(x, nsp, index):
    if nsp == 2:
        half = x.shape[1] // 2
        return in_order(x[:, :half], swap(x[:, half:]), index)
    return lax.all_to_all(x, "sp", split_axis=1, concat_axis=2, tiled=True)


def tokens_to_heads(x, nsp, index):
    if nsp == 2:
        own, other = halves(x, index)
        return jnp.concatenate([own, swap(other)], axis=1)
    return lax.all_to_all(x, "sp", split_axis=2, concat_axis=1, tiled=True)


def gather_axis(x, nsp, index, axis):
    if nsp == 2:
        return in_order(x, swap(x), index, axis)
    return lax.all_gather(x, "sp", axis=axis, tiled=True)


def scatter_axis(x, nsp, index, axis):
    if nsp == 2:
        own, other = halves(x, index, axis)
        return own.astype(F32) + swap(other.astype(BF)).astype(F32)
    return lax.psum_scatter(x.astype(BF), "sp", scatter_dimension=axis, tiled=True).astype(F32)


def sum_sp(x, nsp):
    if nsp == 2:
        return x.astype(F32) + swap(x).astype(F32)
    return lax.psum(x, "sp").astype(F32)


def scatter_rows(x, nf):
    f = lax.axis_index("fsdp")
    core, y, z, nz = f % 2, (f // 2) % 2, f // 4, nf // 4
    _, rows, w = x.shape
    kind = x.dtype
    x = x.reshape(nz, 2, 2, rows, w)
    got = lax.ppermute(pick(x, 1 - core, 2), "fsdp", [(i, i ^ 1) for i in range(nf)])
    x = (pick(x, core, 2).astype(F32) + got.astype(F32)).astype(kind)
    got = lax.ppermute(pick(x, 1 - y, 1), "fsdp", [(i, i ^ 2) for i in range(nf)])
    x = (pick(x, y, 1).astype(F32) + got.astype(F32)).astype(kind)
    total = pick(x, z, 0).astype(F32)
    for d in range(1, nz):
        part = pick(x, (z + d) % nz, 0)
        total = total + lax.ppermute(part, "fsdp", [(i, (i + 4 * d) % nf) for i in range(nf)]).astype(F32)
    return total


def gather_rows(x):
    return lax.all_gather(x, "fsdp", axis=0, tiled=True)


def normalise(stream):
    centre = stream - jnp.mean(stream, axis=-1, keepdims=True)
    inverse = lax.rsqrt(jnp.mean(centre * centre, axis=-1, keepdims=True) + EPS)
    return centre * inverse, inverse


def norm_back(w, unit, inverse, scale):
    u = w * (1.0 + scale)
    stream = (
        u - jnp.mean(u, axis=-1, keepdims=True) - unit * jnp.mean(u * unit, axis=-1, keepdims=True)
    ) * inverse
    return stream, jnp.sum(w, axis=1), jnp.sum(w * unit, axis=1)


def linear(x, w):
    return jnp.einsum("lsd,de->lse", x, w, preferred_element_type=F32)


def linear_back(x, w):
    return jnp.einsum("lse,de->lsd", x, w, preferred_element_type=F32)


def weight_grad(x, g):
    return jnp.einsum("lsd,lse->de", x, g, preferred_element_type=F32).astype(BF)


def column_sum(x):
    return jnp.sum(x, axis=(0, 1), dtype=F32)


def on_device(
    latent_tokens,
    caption_tokens,
    caption_len,
    time_embed,
    mod_table,
    self_input_weight,
    self_query_bias,
    self_value_bias,
    self_output_weight,
    self_output_bias,
    cross_query_weight,
    cross_query_bias,
    cross_keyval_weight,
    cross_value_bias,
    cross_output_weight,
    cross_output_bias,
    expand_weight,
    expand_bias,
    contract_weight,
    contract_bias,
    out_grad,
):
    nsp, nf = lax.axis_size("sp"), lax.axis_size("fsdp")
    sp = lax.axis_index("sp")
    latents, local_len, width = latent_tokens.shape
    rows = width // nf
    own = width // nsp
    hidden_rows = contract_weight.shape[0]
    hidden_own = hidden_rows // nsp
    ff = hidden_rows * nf
    ff_own = ff // nsp

    input_shard = pick(self_input_weight.reshape(rows, 3, nsp, own), sp, 2).reshape(rows, 3 * own)
    keyval_shard = pick(cross_keyval_weight.reshape(rows, 2, nsp, own), sp, 2).reshape(rows, 2 * own)
    expand_shard = pick(expand_weight.reshape(rows, nf, nsp, hidden_own), sp, 2).reshape(rows, ff_own)
    contract_shard = pick(contract_weight.reshape(nsp, hidden_own, width), sp, 0)
    small = jnp.concatenate(
        [
            jnp.stack(
                [
                    self_query_bias,
                    self_value_bias,
                    self_output_bias,
                    cross_query_bias,
                    cross_value_bias,
                    cross_output_bias,
                    contract_bias,
                ]
            ),
            mod_table,
            expand_bias.reshape(rows, ff // width).T,
        ],
        axis=0,
    )
    smalls = small.shape[0]
    small = jnp.pad(small.T, ((0, 0), (0, 128 - smalls)))

    first = gather_rows(jnp.concatenate([input_shard, small], axis=1))
    whole_input = first[:, : 3 * own]
    smalls_all = first[:, 3 * own :].astype(F32).T
    second = gather_rows(
        jnp.concatenate(
            [self_output_weight, cross_query_weight, keyval_shard, cross_output_weight], axis=1
        )
    )
    whole_output = second[:, :width]
    whole_xquery = second[:, width : 2 * width]
    whole_keyval = second[:, 2 * width : 2 * width + 2 * own]
    whole_xoutput = second[:, 2 * width + 2 * own :]
    whole_expand = gather_rows(expand_shard)
    whole_contract = gather_rows(contract_shard)

    bias_query = pick(smalls_all[0].reshape(nsp, own), sp, 0)
    bias_value = pick(smalls_all[1].reshape(nsp, own), sp, 0)
    bias_output = smalls_all[2]
    bias_xquery = smalls_all[3]
    bias_xvalue = pick(smalls_all[4].reshape(nsp, own), sp, 0)
    bias_xoutput = smalls_all[5]
    bias_contract = smalls_all[6]
    table = smalls_all[7:13]
    bias_expand = smalls_all[13:smalls].T.reshape(nf, nsp, hidden_own)
    bias_expand = pick(bias_expand, sp, 1).reshape(ff_own)

    modulation = table[None] + time_embed.reshape(latents, 6, width)
    shift_a, scale_a, gate_a, shift_b, scale_b, gate_b = [
        modulation[:, i][:, None, :] for i in range(6)
    ]

    stream_all = gather_tokens(latent_tokens, nsp)
    grad_all = gather_tokens(out_grad, nsp)
    caption_all = gather_axis(caption_tokens, nsp, sp, 1)
    unit_all, _ = normalise(stream_all.astype(F32))
    norm_a = (unit_all * (1.0 + scale_a) + shift_a).astype(BF)
    projected = linear(norm_a, whole_input)
    queries = (projected[..., :own] + bias_query).astype(BF)
    keys = projected[..., own : 2 * own].astype(BF)
    values = (projected[..., 2 * own :] + bias_value).astype(BF)
    mixed, lse = self_forward(queries, keys, values)
    mixed_tokens = heads_to_tokens(mixed, nsp, sp)

    stream = latent_tokens.astype(F32)
    attended = linear(mixed_tokens, whole_output) + bias_output
    after_attn = stream + gate_a * attended
    attn_low = after_attn.astype(BF)

    cross_queries = (linear(attn_low, whole_xquery) + bias_xquery).astype(BF)
    keyval = linear(caption_all, whole_keyval)
    cross_keys = gather_axis(keyval[..., :own].astype(BF), nsp, sp, 2)
    cross_values = gather_axis((keyval[..., own:] + bias_xvalue).astype(BF), nsp, sp, 2)
    captions = caption_all.shape[1]
    place = jnp.arange(captions)
    bias = jnp.where(place[None] < caption_len[:, None], 0.0, NEG).astype(F32)[..., None]
    cross_mixed, cross_lse = cross_forward(cross_queries, cross_keys, cross_values, bias)
    crossed = linear(cross_mixed, whole_xoutput) + bias_xoutput
    after_cross = after_attn + crossed

    unit_b, inverse_b = normalise(after_cross)
    norm_b = gather_tokens((unit_b * (1.0 + scale_b) + shift_b).astype(BF), nsp)
    fed_grad = (gate_b * grad_all.astype(F32)).astype(BF)
    hidden = linear(norm_b, whole_expand) + bias_expand
    activated, gelu_back = jax.vjp(partial(jax.nn.gelu, approximate=True), hidden)
    activated = activated.astype(BF)
    hidden_grad = gelu_back(linear_back(fed_grad, whole_contract))[0].astype(BF)
    norm_b_grad = scatter_tokens(linear_back(hidden_grad, whole_expand), nsp)

    contract_wgrad = weight_grad(activated, fed_grad)
    expand_wgrad = weight_grad(norm_b, hidden_grad)
    fed = scatter_tokens(linear(activated, whole_contract), nsp) + bias_contract
    block_out = (after_cross + gate_b * fed).astype(BF)
    cotangent = out_grad.astype(F32)
    gate_b_grad = jnp.sum(cotangent * fed, axis=1)
    contract_bgrad = column_sum(fed_grad[:, :local_len] if nsp == 2 else gate_b * cotangent)
    expand_bgrad = column_sum(hidden_grad)

    cross_stream_grad, shift_b_grad, scale_b_grad = norm_back(norm_b_grad, unit_b, inverse_b, scale_b)
    cross_stream_grad = cross_stream_grad + cotangent
    crossed_grad = cross_stream_grad.astype(BF)
    xoutput_wgrad = weight_grad(cross_mixed, crossed_grad)
    xoutput_bgrad = column_sum(crossed_grad)
    cross_mixed_grad = linear_back(crossed_grad, whole_xoutput).astype(BF)
    xquery_grad, xkey_part, xvalue_part = cross_backward(
        cross_queries, cross_keys, cross_values, cross_mixed_grad, bias, cross_lse
    )
    attn_stream_grad = cross_stream_grad + linear_back(xquery_grad, whole_xquery)
    gate_a_grad = jnp.sum(attn_stream_grad * attended, axis=1)
    attended_grad = (gate_a * attn_stream_grad).astype(BF)
    mixed_grad = tokens_to_heads(linear_back(attended_grad, whole_output).astype(BF), nsp, sp)

    keyval_grad = jnp.concatenate(
        [scatter_axis(xkey_part, nsp, sp, 2), scatter_axis(xvalue_part, nsp, sp, 2)], axis=-1
    ).astype(BF)
    caption_grad = scatter_axis(linear_back(keyval_grad, whole_keyval), nsp, sp, 1)
    keyval_wgrad = weight_grad(caption_all, keyval_grad)
    xvalue_bgrad = column_sum(keyval_grad[..., own:])
    xquery_wgrad = weight_grad(attn_low, xquery_grad)
    xquery_bgrad = column_sum(xquery_grad)
    output_wgrad = weight_grad(mixed_tokens, attended_grad)
    output_bgrad = column_sum(attended_grad)

    query_grad, key_grad, value_grad = self_backward(queries, keys, values, mixed_grad, lse)
    projected_grad = jnp.concatenate([query_grad, key_grad, value_grad], axis=-1)
    input_wgrad = weight_grad(norm_a, projected_grad)
    query_bgrad = column_sum(query_grad)
    value_bgrad = column_sum(value_grad)
    norm_a_grad = scatter_tokens(linear_back(projected_grad, whole_input), nsp)
    unit_a, inverse_a = normalise(stream)
    stream_part, shift_a_grad, scale_a_grad = norm_back(norm_a_grad, unit_a, inverse_a, scale_a)
    latent_grad = attn_stream_grad + stream_part

    def owned(x):
        return scatter_rows(x.reshape(nf, x.shape[0] // nf, x.shape[1]), nf).astype(BF)

    contract_own, expand_own = owned(contract_wgrad), owned(expand_wgrad)
    keyval_own, input_own = owned(keyval_wgrad), owned(input_wgrad)
    output_own, xquery_own, xoutput_own = owned(output_wgrad), owned(xquery_wgrad), owned(xoutput_wgrad)

    def gather_sp(x):
        if nsp == 2:
            got = swap(x)
            return jnp.where(sp == 0, jnp.stack([x, got]), jnp.stack([got, x])).astype(F32)
        return lax.all_gather(x, "sp").astype(F32)

    contract_out = gather_sp(contract_own).reshape(hidden_rows, width)
    expand_out = (
        gather_sp(expand_own.reshape(rows, nf, hidden_own)).transpose(1, 2, 0, 3).reshape(rows, ff)
    )
    keyval_out = (
        gather_sp(keyval_own.reshape(rows, 2, own)).transpose(1, 2, 0, 3).reshape(rows, 2 * width)
    )
    input_out = (
        gather_sp(input_own.reshape(rows, 3, own)).transpose(1, 2, 0, 3).reshape(rows, 3 * width)
    )
    output_out, xquery_out, xoutput_out = [
        sum_sp(x, nsp) for x in (output_own, xquery_own, xoutput_own)
    ]

    def spread(x):
        return jnp.where(jnp.arange(nsp)[:, None] == sp, x[None], 0.0).reshape(nsp * x.shape[0])

    embed_part = jnp.stack(
        [shift_a_grad, scale_a_grad, gate_a_grad, shift_b_grad, scale_b_grad, gate_b_grad], axis=1
    )
    expand_bias_part = jnp.where(
        jnp.arange(nsp)[None, :, None] == sp, expand_bgrad.reshape(nf, 1, hidden_own), 0.0
    )
    vectors = [
        spread(query_bgrad),
        spread(value_bgrad),
        output_bgrad,
        xquery_bgrad,
        spread(xvalue_bgrad),
        xoutput_bgrad,
        contract_bgrad,
        expand_bias_part.reshape(ff),
    ]
    sizes = [v.shape[0] // nf for v in vectors]
    table_part = jnp.sum(embed_part, axis=0).reshape(6, nf, rows).transpose(1, 0, 2).reshape(nf, 6 * rows)
    vectors = jnp.concatenate([v.reshape(nf, -1) for v in vectors] + [table_part], axis=1)
    owned_small = sum_sp(scatter_rows(vectors[:, None, :], nf)[0], nsp)
    pieces, at = [], 0
    for size in sizes:
        pieces.append(owned_small[at : at + size])
        at += size
    table_out = owned_small[at:].reshape(6, rows)
    time_grad = sum_sp(embed_part.reshape(latents, 6 * width), nsp)
    return (
        block_out,
        latent_grad,
        caption_grad,
        time_grad,
        table_out,
        input_out,
        pieces[0],
        pieces[1],
        output_out,
        pieces[2],
        xquery_out,
        pieces[3],
        keyval_out,
        pieces[4],
        xoutput_out,
        pieces[5],
        expand_out,
        pieces[7],
        contract_out,
        pieces[6],
    )


def solution(mesh):
    row, vec, tokens = P("fsdp", None), P("fsdp"), P("fsdp", "sp", None)
    in_specs = (
        (tokens, tokens, vec, row, P(None, "fsdp"), row, vec, vec)
        + (row, vec) * 2
        + (row, vec) * 4
        + (tokens,)
    )
    out_specs = (
        (tokens, tokens, tokens, row, P(None, "fsdp"), row, vec, vec) + (row, vec) * 2 + (row, vec) * 4
    )
    return jax.shard_map(
        on_device, mesh=mesh, in_specs=in_specs, out_specs=out_specs, check_vma=False
    )
```

time: 1620 us -> 811 us (0.50); the launches traced: 1590 us -> 801 us
  blocking collectives: 352 us -> 0 us
  matrix products: 311 us -> 137 us
  local copies, waits for them, and re-layouts: 287 us -> 115 us
  waiting for transfers between devices: 428 us -> 306 us
  other arithmetic: 157 us -> 71.3 us
  Pallas kernels: 0 us -> 72.1 us
  starting transfers between devices: 35.7 us -> 83.7 us
    unnamed x3 -> x0, blocking collectives: 312 us -> none
    reduce_scatter x2 -> x0, waiting for transfers between devices: 248 us -> none  [the longest x1 124 us: on_device(): lax.psum_scatter(expand_wgrad.astype(jnp.bfloat16), 'fsdp', scatter_dimen...]
    ppermute x0 -> x63, waiting for transfers between devices: none -> 221 us  [the longest x23 122 us: swap(): return lax.ppermute(x, 'sp', [(0, 1), (1, 0)])]
    dot_general x139 -> x21, matrix products: 311 us -> 137 us  [the longest x7 54.4 us: linear_back(): return jnp.einsum('lse,de->lsd', x, w, preferred_element_type=F32)]
    ppermute x0 -> x63, starting transfers between devices: none -> 82.9 us  [the longest x24 46.6 us: scatter_rows(): lax.ppermute(part, 'fsdp', [(i, (i + 4 * d) % nf) for i in range(nf)])]
    unnamed x245 -> x163, local copies, waits for them, and re-layouts: 88.9 us -> 6.71 us
    unnamed x9 -> x4, other arithmetic: 74.6 us -> 0.07 us
    pallas_call x0 -> x4, Pallas kernels: none -> 72.1 us  [per_latent(): pl.pallas_call(kernel, grid=(ins[0].shape[0],), in_specs=[spec(a.shape) f...]
  transfers between devices with their start and end apart: 23 -> 67, of which waited for: 7 -> 36; matrix products, arithmetic and copies ran while one was open for 41% -> 33% of each run, Pallas kernels for 0% -> 9%
where the time goes in v1:
time: 811 us; the launch traced here: 801 us
  waiting for transfers between devices  306 us (38%)
  matrix products  137 us (17%)
  local copies, waits for them, and re-layouts  115 us (14%)
  starting transfers between devices  83.7 us (10%)
  Pallas kernels  72.1 us (9%)
  other arithmetic  71.3 us (9%)
  between operations  16.3 us (2%)
    ppermute x23, waiting for transfers between devices, swap(): return lax.ppermute(x, 'sp', [(0, 1), (1, 0)])  122 us
    all_gather x4, waiting for transfers between devices, gather_rows(): return lax.all_gather(x, 'fsdp', axis=0, tiled=True)  84.4 us
    pallas_call x4, Pallas kernels, per_latent(): pl.pallas_call(kernel, grid=(ins[0].shape[0],), in_specs=[spec(a.shape) f...  72.1 us
    ppermute x24, waiting for transfers between devices, scatter_rows(): lax.ppermute(part, 'fsdp', [(i, (i + 4 * d) % nf) for i in range(nf)])  69.1 us
    dot_general x7, matrix products, linear_back(): return jnp.einsum('lse,de->lsd', x, w, preferred_element_type=F32)  54.4 us
    ppermute x24, starting transfers between devices, scatter_rows(): lax.ppermute(part, 'fsdp', [(i, (i + 4 * d) % nf) for i in range(nf)])  46.6 us
    dot_general x7, matrix products, linear(): return jnp.einsum('lsd,de->lse', x, w, preferred_element_type=F32)  44.4 us
    dot_general x7, matrix products, weight_grad(): jnp.einsum('lsd,lse->de', x, g, preferred_element_type=F32).astype(BF)  37.8 us
  transfers between devices with their start and end apart: 67, of which 36 were waited for; matrix products, arithmetic and copies ran while one was open for 33% of the time, Pallas kernels for 9%

profile of v1, /device:TPU:8, one launch (start us, length us, event | category | flops | bytes accessed | tf_op | source)
XLA Modules:
  0.0 800.9 jit_solution(1951747833387946009)
XLA Ops:
  38.2 24.3 %collective-permute-done = bf16[1,512,1152]{2,1,0:T(8,128)(2,1)S(1)} collective-permute-done((bf16[1,512,1152]{2,1,0:T(8,128)(2,1)S(1)}, bf16[1,512,1152]{2,1,0:T(8,128)(2,1)S(1)}, u32[]{:S(2)}, u32[]{:S(2)}) %collective-permute-start) | collective-permute-done | bytes 1179680 | tf_op jit(solution)/shard_map/ppermute | solution.py:135
  63.6 8.4 %all-gather.6.cloned.1.call-done = bf16[1152,1856]{1,0:T(8,128)(2,1)} async-done(((bf16[72,1856]{1,0:T(8,128)(2,1)}), bf16[1152,1856]{1,0:T(8,128)(2,1)}) %all-gather.6.cloned.1.call-update) | async-done | bytes 4276240 | tf_op jit(solution)/shard_map/all_gather | solution.py:217
  77.5 7.5 convolution_bitcast_fusion
  88.6 18.5 %shard_map.356 = (bf16[1,1024,576]{2,1,0:T(8,128)(2,1)}, f32[1,8,1024]{2,1,0:T(8,128)}) custom-call(bf16[1,1024,576]{2,1,0:T(8,128)(2,1)} %get-tuple-element.170.q_ref, bf16[1,1024,576]{2,1,0:T(8,128)(2,1)} %slice.320.k_ref, bf16[1,1024,576]{2,1,0:T(8,128)(2,1)} %get-tuple-element.169.v_ref), custom_call_target="tpu_custom_call" | custom-call | flops 8589934592 | bytes 7077888 | tf_op jit(solution)/shard_map/pallas_call | solution.py:84
  113.3 12.8 %collective-permute-done.1 = bf16[1,512,576]{1,2,0:T(8,128)(2,1)} collective-permute-done((bf16[1,512,576]{1,2,0:T(8,128)(2,1)}, bf16[1,512,576]{1,2,0:T(8,128)(2,1)}, u32[]{:S(2)}, u32[]{:S(2)}) %collective-permute-start.1) | collective-permute-done | bytes 589856 | tf_op jit(solution)/shard_map/ppermute | solution.py:135
  128.4 32.7 %all-gather.8.cloned.1.call-done = bf16[1152,4608]{1,0:T(8,128)(2,1)} async-done(((bf16[72,4608]{1,0:T(8,128)(2,1)}), bf16[1152,4608]{1,0:T(8,128)(2,1)}) %all-gather.8.cloned.1.call-update) | async-done | bytes 10616848 | tf_op jit(solution)/shard_map/all_gather | solution.py:217
  177.3 8.6 %shard_map.357 = (bf16[1,512,1152]{2,1,0:T(8,128)(2,1)}, f32[1,16,512]{2,1,0:T(8,128)}) custom-call(bf16[1,512,1152]{2,1,0:T(8,128)(2,1)} %fusion.36.q_ref, bf16[1,120,1152]{2,1,0:T(8,128)(2,1)} %maximum_select_fusion.5.k_ref, bf16[1,120,1152]{2,1,0:T(8,128)(2,1)} %maximum_select_fusion.6.v_ref, f32[1,120,1]{2,1,0:T(8,128)} %fusion.106.bias_ref), custom_call_target="tpu_custom_call" | custom-call | flops 1073741824 | bytes 3466176 | tf_op jit(solution)/shard_map/pallas_call | solution.py:84
  196.4 23.0 %all-gather.10.cloned.1.call-done = bf16[1152,2304]{1,0:T(8,128)(2,1)} async-done(((bf16[72,2304]{1,0:T(8,128)(2,1)}), bf16[1152,2304]{1,0:T(8,128)(2,1)}) %all-gather.10.cloned.1.call-update) | async-done | bytes 5308432 | tf_op jit(solution)/shard_map/all_gather | solution.py:217
  221.3 9.5 %fusion.63 = f32[1024,2304]{1,0:T(8,128)S(1)} fusion(bf16[1152,2304]{1,0:T(8,128)(2,1)} %all-gather.10.cloned.1.call-done, bf16[1,512,1152]{2,1,0:T(8,128)(2,1)} %collective-permute-done.5, bf16[1,512,1152]{2,1,0:T(8,128)(2,1)} %add_convert_fusion.2), kind=kOutput, calls=%fused_computation.132 | convolution fusion | flops 5440536576 | bytes 17104896 | tf_op jit(solution)/shard_map/lsd,de->lse/dot_general | solution.py:235
  230.8 14.4 %collective-permute-done.7 = bf16[1,512,1152]{2,1,0:T(8,128)(2,1)} collective-permute-done((bf16[1,512,1152]{2,1,0:T(8,128)(2,1)S(1)}, bf16[1,512,1152]{2,1,0:T(8,128)(2,1)}, u32[]{:S(2)}, u32[]{:S(2)}) %collective-permute-start.7) | collective-permute-done | bytes 1179680 | tf_op jit(solution)/shard_map/ppermute | solution.py:135
  245.3 11.4 %convolution_convert_fusion = bf16[2304,1152]{1,0:T(8,128)(2,1)} fusion(bf16[512,1152]{1,0:T(8,128)(2,1)} %bitcast.31, bf16[512,1152]{1,0:T(8,128)(2,1)S(1)} %bitcast.341, f32[1152]{0:T(1024)S(1)} %get-tuple-element.150, f32[1024,2304]{1,0:T(8,128)S(1)} %fusion.63, f32[2304]{0:T(1024)S(1)} %add.567), kind=kOutput, calls=%fused_computation.2 | convolution fusion | flops 5469143040 | bytes 17118720 | tf_op jit(solution)/shard_map/lsd,lse->de/dot_general | solution.py:243
  256.6 20.4 %all-gather.12.cloned.1.call-done = bf16[1,2304,1152]{2,1,0:T(8,128)(2,1)} async-done(((bf16[1,144,1152]{2,1,0:T(8,128)(2,1)}), bf16[1,2304,1152]{2,1,0:T(8,128)(2,1)}) %all-gather.12.cloned.1.call-update) | async-done | bytes 5308432 | tf_op jit(solution)/shard_map/all_gather | solution.py:217
  277.0 17.4 %convert_reduce_fusion = (f32[2304]{0:T(1024)S(1)}, bf16[1024,2304]{1,0:T(8,128)(2,1)}) fusion(f32[1024,2304]{1,0:T(8,128)} %copy-done.73, f32[2304]{0:T(1024)S(1)} %add.567, bf16[1,2304,1152]{2,1,0:T(8,128)(2,1)} %all-gather.12.cloned.1.call-done, bf16[512,1152]{1,0:T(8,128)(2,1)} %bitcast.31, bf16[512,1152]{1,0:T(8,128)(2,1)S(1)} %bitcast.342, ...), kind=kOutput, calls=%fused_computation.11 | convolution fusion | flops 5497157632 | bytes 21846528 | tf_op jit(solution)/shard_map/lse,de->lsd/dot_general | solution.py:239
  294.6 9.9 %convolution_bitcast_fusion.2 = f32[1,1024,1152]{2,1,0:T(8,128)S(1)} fusion(bf16[1024,2304]{1,0:T(8,128)(2,1)} %get-tuple-element.228, bf16[1152,2304]{1,0:T(8,128)(2,1)} %all-gather.10.cloned.1.call-done), kind=kOutput, calls=%fused_computation.35 | convolution fusion | flops 5435817984 | bytes 14745600 | tf_op jit(solution)/shard_map/lse,de->lsd/dot_general | solution.py:239
  304.7 11.6 %fusion.17 = f32[1,1024,1152]{2,1,0:T(8,128)S(1)} fusion(bf16[1,2304,1152]{2,1,0:T(8,128)(2,1)S(1)} %copy-done.70, f32[1024,2304]{1,0:T(8,128)} %copy-done.73, f32[2304]{0:T(1024)S(1)} %add.567), kind=kOutput, calls=%fused_computation.34 | convolution fusion | flops 5459410944 | bytes 19473408 | tf_op jit(solution)/shard_map/lsd,de->lse/dot_general | solution.py:235
  320.2 7.9 convolution_convert_fusion.1
  332.1 37.8 %collective-permute-done.8 = bf16[1,512,1152]{2,1,0:T(8,128)(2,1)S(1)} collective-permute-done((bf16[1,512,1152]{2,1,0:T(8,128)(2,1)S(1)}, bf16[1,512,1152]{2,1,0:T(8,128)(2,1)S(1)}, u32[]{:S(2)}, u32[]{:S(2)}) %collective-permute-start.8) | collective-permute-done | bytes 1179680 | tf_op jit(solution)/shard_map/ppermute | solution.py:135
  380.6 15.1 %shard_map.358 = (bf16[1,512,1152]{2,1,0:T(8,128)(2,1)}, bf16[1,120,1152]{2,1,0:T(8,128)(2,1)}, bf16[1,120,1152]{2,1,0:T(8,128)(2,1)}) custom-call(bf16[1,512,1152]{2,1,0:T(8,128)(2,1)} %fusion.36.q_ref, bf16[1,120,1152]{2,1,0:T(8,128)(2,1)} %maximum_select_fusion.5.k_ref, bf16[1,120,1152]{2,1,0:T(8,128)(2,1)} %maximum_select_fusion.6.v_ref, ...), custom_call_target="tpu_custom_call" | custom-call | flops 2684354560 | bytes 5891008 | tf_op jit(solution)/shard_map/pallas_call | solution.py:84
  449.5 5.8 collective-permute-done.13
  459.4 29.9 %shard_map.359 = (bf16[1,1024,576]{2,1,0:T(8,128)(2,1)}, bf16[1,1024,576]{2,1,0:T(8,128)(2,1)}, bf16[1,1024,576]{2,1,0:T(8,128)(2,1)}) custom-call(bf16[1,1024,576]{2,1,0:T(8,128)(2,1)} %get-tuple-element.170.q_ref, bf16[1,1024,576]{2,1,0:T(8,128)(2,1)} %slice.320.k_ref, bf16[1,1024,576]{2,1,0:T(8,128)(2,1)} %get-tuple-element.169.v_ref, ...), custom_call_target="tpu_custom_call" | custom-call | flops 21474836480 | bytes 9502720 | tf_op jit(solution)/shard_map/pallas_call | solution.py:84
  489.3 7.2 concatenate.201
  496.6 10.6 %convolution_bitcast_fusion.1 = f32[1,1024,1152]{2,1,0:T(8,128)} fusion(bf16[1,1024,1728]{2,1,0:T(8,128)(2,1)} %concatenate.201, bf16[1152,1856]{1,0:T(8,128)(2,1)} %all-gather.6.cloned.1.call-done), kind=kOutput, calls=%fused_computation.33 | convolution fusion | flops 4076863488 | bytes 12517376 | tf_op jit(solution)/shard_map/lse,de->lsd/dot_general | solution.py:239
  507.2 7.4 convolution_convert_fusion.2
  516.6 6.5 copy.159
  540.4 18.1 %collective-permute-done.10 = bf16[1,512,1152]{2,1,0:T(8,128)(2,1)S(1)} collective-permute-done((bf16[1,512,1152]{2,1,0:T(8,128)(2,1)S(1)}, bf16[1,512,1152]{2,1,0:T(8,128)(2,1)S(1)}, u32[]{:S(2)}, u32[]{:S(2)}) %collective-permute-start.10) | collective-permute-done | bytes 1179680 | tf_op jit(solution)/shard_map/ppermute | solution.py:135
  597.7 10.0 %collective-permute-done.28 = bf16[4,72,1152]{2,1,0:T(8,128)(2,1)} collective-permute-done((bf16[4,72,1152]{2,1,0:T(8,128)(2,1)}, bf16[4,72,1152]{2,1,0:T(8,128)(2,1)}, u32[]{:S(2)}, u32[]{:S(2)}) %collective-permute-start.28) | collective-permute-done | bytes 663584 | tf_op jit(solution)/shard_map/ppermute | solution.py:207
  610.6 11.2 %collective-permute-done.40 = bf16[4,72,1152]{2,1,0:T(8,128)(2,1)} collective-permute-done((bf16[4,72,1152]{2,1,0:T(8,128)(2,1)S(1)}, bf16[4,72,1152]{2,1,0:T(8,128)(2,1)}, u32[]{:S(2)}, u32[]{:S(2)}) %collective-permute-start.40) | collective-permute-done | bytes 663584 | tf_op jit(solution)/shard_map/ppermute | solution.py:207
  632.2 6.8 collective-permute-start.48
  709.1 17.2 %collective-permute-done.53 = bf16[72,2304]{1,0:T(8,128)(2,1)S(1)} collective-permute-done((bf16[72,2304]{1,0:T(8,128)(2,1)S(1)}, bf16[72,2304]{1,0:T(8,128)(2,1)S(1)}, u32[]{:S(2)}, u32[]{:S(2)}) %collective-permute-start.53) | collective-permute-done | bytes 331808 | tf_op jit(solution)/shard_map/ppermute | solution.py:212
  726.5 6.5 collective-permute-done.55
  733.0 9.1 %collective-permute-done.54 = bf16[72,2304]{1,0:T(8,128)(2,1)S(1)} collective-permute-done((bf16[72,2304]{1,0:T(8,128)(2,1)S(1)}, bf16[72,2304]{1,0:T(8,128)(2,1)S(1)}, u32[]{:S(2)}, u32[]{:S(2)}) %collective-permute-start.54) | collective-permute-done | bytes 331808 | tf_op jit(solution)/shard_map/ppermute | solution.py:212
  764.2 10.5 %collective-permute-done.23 = bf16[72,1728]{1,0:T(8,128)(2,1)S(1)} collective-permute-done((bf16[72,1728]{1,0:T(8,128)(2,1)S(1)}, bf16[72,1728]{1,0:T(8,128)(2,1)S(1)}, u32[]{:S(2)}, u32[]{:S(2)}) %collective-permute-start.23) | collective-permute-done | bytes 248864 | tf_op jit(solution)/shard_map/ppermute | solution.py:212
  (500 shorter events, 337.0 us)
Async XLA Ops:
  7.2 64.8 %all-gather.6.cloned.1.call-start = ((), (), s32[]{:S(2)}) async-start(), calls=%async_computation | async-start | bytes 4700160 | tf_op jit(solution)/shard_map/all_gather | solution.py:217
  19.0 142.1 %all-gather.8.cloned.1.call-start = ((), (), s32[]{:S(2)}) async-start(), calls=%async_computation.1 | async-start | bytes 11280384 | tf_op jit(solution)/shard_map/all_gather | solution.py:217
  21.8 197.6 %all-gather.10.cloned.1.call-start = ((), (), s32[]{:S(2)}) async-start(), calls=%async_computation.2 | async-start | bytes 5640192 | tf_op jit(solution)/shard_map/all_gather | solution.py:217
  34.4 242.6 %all-gather.12.cloned.1.call-start = ((), (), s32[]{:S(2)}) async-start(), calls=%async_computation.3 | async-start | bytes 5640192 | tf_op jit(solution)/shard_map/all_gather | solution.py:217
  34.7 27.8 %collective-permute-start = (bf16[1,512,1152]{2,1,0:T(8,128)(2,1)S(1)}, bf16[1,512,1152]{2,1,0:T(8,128)(2,1)S(1)}, u32[]{:S(2)}, u32[]{:S(2)}) collective-permute-start(bf16[1,512,1152]{2,1,0:T(8,128)(2,1)S(1)} %copy-done.2), channel_id=1, source_target_pairs={{0,1},{1,0},{2,3},{3,2},{4,5},{5,4},{6,7},{7,6},{8,9},{9,8},{10,11... | collective-permute-start | bytes 3538952 | tf_op jit(solution)/shard_map/ppermute | solution.py:135
  192.1 29.2 %collective-permute-start.5 = (bf16[1,512,1152]{2,1,0:T(8,128)(2,1)}, bf16[1,512,1152]{2,1,0:T(8,128)(2,1)}, u32[]{:S(2)}, u32[]{:S(2)}) collective-permute-start(bf16[1,512,1152]{2,1,0:T(8,128)(2,1)} %add_convert_fusion.2), channel_id=1, source_target_pairs={{0,1},{1,0},{2,3},{3,2},{4,5},{5,4},{6,7},{7,6},{8,9},{9,8},{10,11... | collective-permute-start | bytes 3538952 | tf_op jit(solution)/shard_map/ppermute | solution.py:135
  193.6 51.6 %collective-permute-start.7 = (bf16[1,512,1152]{2,1,0:T(8,128)(2,1)S(1)}, bf16[1,512,1152]{2,1,0:T(8,128)(2,1)}, u32[]{:S(2)}, u32[]{:S(2)}) collective-permute-start(bf16[1,512,1152]{2,1,0:T(8,128)(2,1)S(1)} %copy-done.38), channel_id=1, source_target_pairs={{0,1},{1,0},{2,3},{3,2},{4,5},{5,4},{6,7},{7,6},{8,9},{9,8},{10,11... | collective-permute-start | bytes 3538952 | tf_op jit(solution)/shard_map/ppermute | solution.py:135
  316.4 54.7 %collective-permute-start.6 = (bf16[1,512,1152]{2,1,0:T(8,128)(2,1)S(1)}, bf16[1,512,1152]{2,1,0:T(8,128)(2,1)S(1)}, u32[]{:S(2)}, u32[]{:S(2)}) collective-permute-start(bf16[1,512,1152]{2,1,0:T(8,128)(2,1)S(1)} %slice.323), channel_id=1, source_target_pairs={{0,1},{1,0},{2,3},{3,2},{4,5},{5,4},{6,7},{7,6},{8,9},{9,8},{10,11... | collective-permute-start | bytes 3538952 | tf_op jit(solution)/shard_map/ppermute | solution.py:135
  317.9 52.0 %collective-permute-start.8 = (bf16[1,512,1152]{2,1,0:T(8,128)(2,1)S(1)}, bf16[1,512,1152]{2,1,0:T(8,128)(2,1)S(1)}, u32[]{:S(2)}, u32[]{:S(2)}) collective-permute-start(bf16[1,512,1152]{2,1,0:T(8,128)(2,1)S(1)} %slice.322), channel_id=1, source_target_pairs={{0,1},{1,0},{2,3},{3,2},{4,5},{5,4},{6,7},{7,6},{8,9},{9,8},{10,11... | collective-permute-start | bytes 3538952 | tf_op jit(solution)/shard_map/ppermute | solution.py:135
  320.2 247.2 %collective-permute-start.57 = (bf16[4,2,144,1152]{3,2,1,0:T(8,128)(2,1)}, bf16[4,2,144,1152]{3,2,1,0:T(8,128)(2,1)}, u32[]{:S(2)}, u32[]{:S(2)}) collective-permute-start(bf16[4,2,144,1152]{3,2,1,0:T(8,128)(2,1)} %dynamic-slice_bitcast_fusion), channel_id=1, source_target_pairs={{0,2},{2,0},{4,6},{6,4},{8,10},{10,8},{12,14},{14,12},{16,18},{18,... | collective-permute-start | bytes 7962632 | tf_op jit(solution)/shard_map/ppermute | solution.py:205
  331.6 231.9 %collective-permute-start.51 = (bf16[4,2,72,2304]{3,2,1,0:T(8,128)(2,1)}, bf16[4,2,72,2304]{3,2,1,0:T(8,128)(2,1)}, u32[]{:S(2)}, u32[]{:S(2)}) collective-permute-start(bf16[4,2,72,2304]{3,2,1,0:T(8,128)(2,1)} %dynamic-slice_bitcast_fusion.1), channel_id=1, source_target_pairs={{0,2},{2,0},{4,6},{6,4},{8,10},{10,8},{12,14},{14,12},{16,18},{18,... | collective-permute-start | bytes 7962632 | tf_op jit(solution)/shard_map/ppermute | solution.py:205
  407.2 29.3 %collective-permute-start.12 = (bf16[1,120,576]{2,1,0:T(8,128)(2,1)}, bf16[1,120,576]{2,1,0:T(8,128)(2,1)S(1)}, u32[]{:S(2)}, u32[]{:S(2)}) collective-permute-start(bf16[1,120,576]{2,1,0:T(8,128)(2,1)} %broadcast_select_fusion.3), channel_id=1, source_target_pairs={{0,1},{1,0},{2,3},{3,2},{4,5},{5,4},{6,7},{7,6},{8,9},{9,8},{10,11... | collective-permute-start | bytes 414728 | tf_op jit(solution)/shard_map/ppermute | solution.py:135
  408.6 31.0 %collective-permute-start.11 = (bf16[1,120,576]{2,1,0:T(8,128)(2,1)}, bf16[1,120,576]{2,1,0:T(8,128)(2,1)}, u32[]{:S(2)}, u32[]{:S(2)}) collective-permute-start(bf16[1,120,576]{2,1,0:T(8,128)(2,1)} %broadcast_select_fusion.4), channel_id=1, source_target_pairs={{0,1},{1,0},{2,3},{3,2},{4,5},{5,4},{6,7},{7,6},{8,9},{9,8},{10,11... | collective-permute-start | bytes 414728 | tf_op jit(solution)/shard_map/ppermute | solution.py:135
  412.4 115.8 %collective-permute-start.33 = (bf16[4,2,72,1152]{3,2,0,1:T(8,128)(2,1)}, bf16[4,2,72,1152]{3,2,0,1:T(8,128)(2,1)}, u32[]{:S(2)}, u32[]{:S(2)}) collective-permute-start(bf16[4,2,72,1152]{3,2,0,1:T(8,128)(2,1)} %bitcast.315), channel_id=1, source_target_pairs={{0,2},{2,0},{4,6},{6,4},{8,10},{10,8},{12,14},{14,12},{16,18},{18,... | collective-permute-start | bytes 3981320 | tf_op jit(solution)/shard_map/ppermute | solution.py:205
  437.1 19.2 %collective-permute-start.9 = (bf16[1,512,576]{1,2,0:T(8,128)(2,1)}, bf16[1,512,576]{1,2,0:T(8,128)(2,1)}, u32[]{:S(2)}, u32[]{:S(2)}) collective-permute-start(bf16[1,512,576]{1,2,0:T(8,128)(2,1)} %copy.157), channel_id=1, source_target_pairs={{0,1},{1,0},{2,3},{3,2},{4,5},{5,4},{6,7},{7,6},{8,9},{9,8},{10,11... | collective-permute-start | bytes 1769480 | tf_op jit(solution)/shard_map/ppermute | solution.py:135
  455.3 74.8 %collective-permute-start.45 = (bf16[4,2,72,1152]{3,2,0,1:T(8,128)(2,1)}, bf16[4,2,72,1152]{3,2,0,1:T(8,128)(2,1)}, u32[]{:S(2)}, u32[]{:S(2)}) collective-permute-start(bf16[4,2,72,1152]{3,2,0,1:T(8,128)(2,1)} %bitcast.313), channel_id=1, source_target_pairs={{0,2},{2,0},{4,6},{6,4},{8,10},{10,8},{12,14},{14,12},{16,18},{18,... | collective-permute-start | bytes 3981320 | tf_op jit(solution)/shard_map/ppermute | solution.py:205
  456.4 78.1 %collective-permute-start.27 = (bf16[4,2,72,1152]{3,2,0,1:T(8,128)(2,1)}, bf16[4,2,72,1152]{3,2,0,1:T(8,128)(2,1)}, u32[]{:S(2)}, u32[]{:S(2)}) collective-permute-start(bf16[4,2,72,1152]{3,2,0,1:T(8,128)(2,1)} %bitcast.316), channel_id=1, source_target_pairs={{0,2},{2,0},{4,6},{6,4},{8,10},{10,8},{12,14},{14,12},{16,18},{18,... | collective-permute-start | bytes 3981320 | tf_op jit(solution)/shard_map/ppermute | solution.py:205
  530.1 28.4 %collective-permute-start.10 = (bf16[1,512,1152]{2,1,0:T(8,128)(2,1)S(1)}, bf16[1,512,1152]{2,1,0:T(8,128)(2,1)S(1)}, u32[]{:S(2)}, u32[]{:S(2)}) collective-permute-start(bf16[1,512,1152]{2,1,0:T(8,128)(2,1)S(1)} %slice.321), channel_id=1, source_target_pairs={{0,1},{1,0},{2,3},{3,2},{4,5},{5,4},{6,7},{7,6},{8,9},{9,8},{10,11... | collective-permute-start | bytes 3538952 | tf_op jit(solution)/shard_map/ppermute | solution.py:135
  534.5 156.0 %collective-permute-start.21 = (bf16[4,2,72,1728]{3,2,1,0:T(8,128)(2,1)}, bf16[4,2,72,1728]{3,2,1,0:T(8,128)(2,1)}, u32[]{:S(2)}, u32[]{:S(2)}) collective-permute-start(bf16[4,2,72,1728]{3,2,1,0:T(8,128)(2,1)} %dynamic-slice_bitcast_fusion.2), channel_id=1, source_target_pairs={{0,2},{2,0},{4,6},{6,4},{8,10},{10,8},{12,14},{14,12},{16,18},{18,... | collective-permute-start | bytes 5971976 | tf_op jit(solution)/shard_map/ppermute | solution.py:205
  538.4 46.8 %collective-permute-start.34 = (bf16[4,72,1152]{2,1,0:T(8,128)(2,1)}, bf16[4,72,1152]{2,1,0:T(8,128)(2,1)}, u32[]{:S(2)}, u32[]{:S(2)}) collective-permute-start(bf16[4,72,1152]{2,1,0:T(8,128)(2,1)} %dynamic-slice_bitcast_fusion.8), channel_id=1, source_target_pairs={{0,4},{2,6},{4,0},{6,2},{8,12},{10,14},{12,8},{14,10},{16,20},{18,... | collective-permute-start | bytes 1990664 | tf_op jit(solution)/shard_map/ppermute | solution.py:207
  580.5 27.2 %collective-permute-start.28 = (bf16[4,72,1152]{2,1,0:T(8,128)(2,1)}, bf16[4,72,1152]{2,1,0:T(8,128)(2,1)}, u32[]{:S(2)}, u32[]{:S(2)}) collective-permute-start(bf16[4,72,1152]{2,1,0:T(8,128)(2,1)} %dynamic-slice_bitcast_fusion.9), channel_id=1, source_target_pairs={{0,4},{2,6},{4,0},{6,2},{8,12},{10,14},{12,8},{14,10},{16,20},{18,... | collective-permute-start | bytes 1990664 | tf_op jit(solution)/shard_map/ppermute | solution.py:207
  582.2 39.7 %collective-permute-start.40 = (bf16[4,72,1152]{2,1,0:T(8,128)(2,1)S(1)}, bf16[4,72,1152]{2,1,0:T(8,128)(2,1)}, u32[]{:S(2)}, u32[]{:S(2)}) collective-permute-start(bf16[4,72,1152]{2,1,0:T(8,128)(2,1)S(1)} %dynamic-slice_bitcast_fusion.7), channel_id=1, source_target_pairs={{0,4},{2,6},{4,0},{6,2},{8,12},{10,14},{12,8},{14,10},{16,20},{18,... | collective-permute-start | bytes 1990664 | tf_op jit(solution)/shard_map/ppermute | solution.py:207
  585.1 120.8 %collective-permute-start.58 = (bf16[4,144,1152]{2,1,0:T(8,128)(2,1)}, bf16[4,144,1152]{2,1,0:T(8,128)(2,1)}, u32[]{:S(2)}, u32[]{:S(2)}) collective-permute-start(bf16[4,144,1152]{2,1,0:T(8,128)(2,1)} %dynamic-slice_bitcast_fusion.3), channel_id=1, source_target_pairs={{0,4},{2,6},{4,0},{6,2},{8,12},{10,14},{12,8},{14,10},{16,20},{18,... | collective-permute-start | bytes 3981320 | tf_op jit(solution)/shard_map/ppermute | solution.py:207
  593.4 31.9 %collective-permute-start.35 = (bf16[72,1152]{1,0:T(8,128)(2,1)S(1)}, bf16[72,1152]{1,0:T(8,128)(2,1)S(1)}, u32[]{:S(2)}, u32[]{:S(2)}) collective-permute-start(bf16[72,1152]{1,0:T(8,128)(2,1)S(1)} %get-tuple-element.205), channel_id=1, source_target_pairs={{0,8},{2,10},{4,12},{6,14},{8,16},{10,18},{12,20},{14,22},{16,24},... | collective-permute-start | bytes 497672 | tf_op jit(solution)/shard_map/ppermute | solution.py:212
  668.3 30.1 %collective-permute-start.52 = (bf16[4,72,2304]{2,1,0:T(8,128)(2,1)}, bf16[4,72,2304]{2,1,0:T(8,128)(2,1)}, u32[]{:S(2)}, u32[]{:S(2)}) collective-permute-start(bf16[4,72,2304]{2,1,0:T(8,128)(2,1)} %dynamic-slice_bitcast_fusion.4), channel_id=1, source_target_pairs={{0,4},{2,6},{4,0},{6,2},{8,12},{10,14},{12,8},{14,10},{16,20},{18,... | collective-permute-start | bytes 3981320 | tf_op jit(solution)/shard_map/ppermute | solution.py:207
  694.5 60.9 %collective-permute-start.22 = (bf16[4,72,1728]{2,1,0:T(8,128)(2,1)}, bf16[4,72,1728]{2,1,0:T(8,128)(2,1)}, u32[]{:S(2)}, u32[]{:S(2)}) collective-permute-start(bf16[4,72,1728]{2,1,0:T(8,128)(2,1)} %dynamic-slice_bitcast_fusion.5), channel_id=1, source_target_pairs={{0,4},{2,6},{4,0},{6,2},{8,12},{10,14},{12,8},{14,10},{16,20},{18,... | collective-permute-start | bytes 2985992 | tf_op jit(solution)/shard_map/ppermute | solution.py:207
  700.1 26.2 %collective-permute-start.53 = (bf16[72,2304]{1,0:T(8,128)(2,1)S(1)}, bf16[72,2304]{1,0:T(8,128)(2,1)S(1)}, u32[]{:S(2)}, u32[]{:S(2)}) collective-permute-start(bf16[72,2304]{1,0:T(8,128)(2,1)S(1)} %get-tuple-element.187), channel_id=1, source_target_pairs={{0,8},{2,10},{4,12},{6,14},{8,16},{10,18},{12,20},{14,22},{16,24},... | collective-permute-start | bytes 995336 | tf_op jit(solution)/shard_map/ppermute | solution.py:212
  704.4 28.6 %collective-permute-start.55 = (bf16[72,2304]{1,0:T(8,128)(2,1)S(1)}, bf16[72,2304]{1,0:T(8,128)(2,1)S(1)}, u32[]{:S(2)}, u32[]{:S(2)}) collective-permute-start(bf16[72,2304]{1,0:T(8,128)(2,1)S(1)} %get-tuple-element.188), channel_id=1, source_target_pairs={{0,24},{2,26},{4,28},{6,30},{8,0},{10,2},{12,4},{14,6},{16,8},{18,... | collective-permute-start | bytes 995336 | tf_op jit(solution)/shard_map/ppermute | solution.py:212
  704.4 37.7 %collective-permute-start.54 = (bf16[72,2304]{1,0:T(8,128)(2,1)S(1)}, bf16[72,2304]{1,0:T(8,128)(2,1)S(1)}, u32[]{:S(2)}, u32[]{:S(2)}) collective-permute-start(bf16[72,2304]{1,0:T(8,128)(2,1)S(1)} %get-tuple-element.189), channel_id=1, source_target_pairs={{0,16},{2,18},{4,20},{6,22},{8,24},{10,26},{12,28},{14,30},{16,0},... | collective-permute-start | bytes 995336 | tf_op jit(solution)/shard_map/ppermute | solution.py:212
  708.6 39.7 %collective-permute-start.59 = (bf16[144,1152]{1,0:T(8,128)(2,1)}, bf16[144,1152]{1,0:T(8,128)(2,1)}, u32[]{:S(2)}, u32[]{:S(2)}) collective-permute-start(bf16[144,1152]{1,0:T(8,128)(2,1)} %get-tuple-element.184), channel_id=1, source_target_pairs={{0,8},{2,10},{4,12},{6,14},{8,16},{10,18},{12,20},{14,22},{16,24},... | collective-permute-start | bytes 995336 | tf_op jit(solution)/shard_map/ppermute | solution.py:212
  726.4 24.2 %collective-permute-start.61 = (bf16[144,1152]{1,0:T(8,128)(2,1)}, bf16[144,1152]{1,0:T(8,128)(2,1)}, u32[]{:S(2)}, u32[]{:S(2)}) collective-permute-start(bf16[144,1152]{1,0:T(8,128)(2,1)} %get-tuple-element.185), channel_id=1, source_target_pairs={{0,24},{2,26},{4,28},{6,30},{8,0},{10,2},{12,4},{14,6},{16,8},{18,... | collective-permute-start | bytes 995336 | tf_op jit(solution)/shard_map/ppermute | solution.py:212
  754.7 26.4 %collective-permute-start.56 = (bf16[72,16,144]{2,1,0:T(8,128)(2,1)}, bf16[72,16,144]{2,1,0:T(8,128)(2,1)}, u32[]{:S(2)}, u32[]{:S(2)}) collective-permute-start(bf16[72,16,144]{2,1,0:T(8,128)(2,1)} %reshape.990), channel_id=1, source_target_pairs={{0,1},{1,0},{2,3},{3,2},{4,5},{5,4},{6,7},{7,6},{8,9},{9,8},{10,11... | collective-permute-start | bytes 995336 | tf_op jit(solution)/shard_map/ppermute | solution.py:135
  (115 other events, 1412.7 us)
Sparse Core Ops, SparseCore 0:
  19.1 52.8 all-gather.5
  74.9 86.1 all-gather.7
  163.8 55.5 all-gather.9
  222.0 54.9 all-gather.11

commit v2 on v1

v2 whole, which is shorter than its diff:
```python
from functools import partial

import jax
import jax.numpy as jnp
from jax import lax
from jax.experimental import pallas as pl
from jax.experimental.pallas import tpu as pltpu
from jax.sharding import PartitionSpec as P

HEADS = 16
HD = 72
GROUPS = 2
SCALE = HD**-0.5
COST = 1 << 20
EPS = 1e-06
NEG = -1e30
F32 = jnp.float32
BF = jnp.bfloat16
NT = (((1,), (1,)), ((), ()))
TN = (((0,), (0,)), ((), ()))
NN = (((1,), (0,)), ((), ()))
VMEM = 56 << 20


def dot(a, b, dims=NN):
    return lax.dot_general(a, b, dims, preferred_element_type=F32)


def whole(shape, n=1):
    return pl.BlockSpec((1,) + tuple(shape[1:]), lambda i, *_: (i,) + (0,) * (len(shape) - 1))


def constant(shape, at=None):
    at = at or (0,) * len(shape)
    return pl.BlockSpec(tuple(shape), lambda *_: at, pipeline_mode=pl.Buffered(1))


def anywhere(n):
    return [pl.BlockSpec(memory_space=pl.ANY)] * n


def smem():
    return pl.BlockSpec(memory_space=pltpu.SMEM)


def call(kernel, ins, in_specs, outs, out_specs, grid=(), scratch=(), waits=(), vmem=VMEM, aliases=None):
    n_in, n_wait = len(ins), len(waits)

    def body(*refs):
        kernel(*refs[:n_in], *refs[n_in + n_wait :])

    return pl.pallas_call(
        body,
        name=(kernel.func if isinstance(kernel, partial) else kernel).__name__,
        grid=grid,
        in_specs=list(in_specs) + anywhere(n_wait),
        out_specs=out_specs,
        out_shape=[jax.ShapeDtypeStruct(s, d) for s, d in outs],
        scratch_shapes=list(scratch),
        input_output_aliases=aliases or {},
        compiler_params=pltpu.CompilerParams(vmem_limit_bytes=vmem),
        cost_estimate=pl.CostEstimate(flops=0, bytes_accessed=COST, transcendentals=0),
    )(*ins, *waits)


def unit_of(v):
    centre = v - jnp.mean(v, axis=-1, keepdims=True)
    inverse = lax.rsqrt(jnp.mean(centre * centre, axis=-1, keepdims=True) + EPS)
    return centre * inverse, inverse


def qkv_kernel(x_ref, mod_ref, bias_ref, w_ref, norm_ref, qkv_ref):
    unit, _ = unit_of(x_ref[0].astype(F32))
    norm = (unit * (1.0 + mod_ref[0, 1:2]) + mod_ref[0, 0:1]).astype(BF)
    norm_ref[0] = norm
    qkv_ref[0] = (dot(norm, w_ref[:, : bias_ref.shape[1]]) + bias_ref[...]).astype(BF)


def qkv_forward(x, mods, bias, first, width3, waits=()):
    n, t, d = x.shape
    tb = min(256, t)
    rows = lambda w: pl.BlockSpec((1, tb, w), lambda i, j: (i, j, 0))
    return call(
        qkv_kernel,
        (x, mods, bias, first),
        [rows(d), whole(mods.shape), constant(bias.shape), constant(first.shape)],
        [((n, t, d), BF), ((n, t, width3), BF)],
        [rows(d), rows(width3)],
        grid=(n, t // tb),
        waits=waits,
    )


def self_fwd_kernel(qkv_ref, *refs, heads):
    o_ref, lse_ref = refs[-2:]
    for h in range(heads):
        q, k, v = [qkv_ref[0, :, (p * heads + h) * HD : (p * heads + h + 1) * HD] for p in range(3)]
        s = dot(k, q, NT) * SCALE
        m = jnp.max(s, axis=0, keepdims=True)
        p = jnp.exp(s - m)
        total = jnp.sum(p, axis=0, keepdims=True)
        o = dot(v, p.astype(BF), TN) * (1.0 / total)
        o_ref[0, :, h * HD : h * HD + HD] = o.T.astype(BF)
        lse_ref[0, h : h + 1, :] = m + jnp.log(total)


def self_forward(qkv, waits=()):
    n, t, w = qkv.shape
    heads = w // HD // 3
    outs = [((n, t, w // 3), BF), ((n, heads, t), F32)]
    return call(
        partial(self_fwd_kernel, heads=heads),
        (qkv,),
        [whole(qkv.shape)],
        outs,
        [whole(s) for s, _ in outs],
        grid=(n,),
        waits=waits,
        vmem=40 << 20,
    )


def middle_fwd_kernel(
    mixed_ref, x_ref, mod_ref, vec_ref, so_ref, xq_ref, xo_ref, k_ref, v_ref, mask_ref,
    attended_ref, low_ref, q_ref, lse_ref, cmix_ref, stream_ref, norm_ref,
):
    attended = dot(mixed_ref[0], so_ref[...]) + vec_ref[2:3]
    attended_ref[0] = attended.astype(BF)
    stream = x_ref[0].astype(F32) + mod_ref[0, 2:3] * attended
    low = stream.astype(BF)
    low_ref[0] = low
    q_ref[0] = (dot(low, xq_ref[...]) + vec_ref[3:4]).astype(BF)
    for h in range(HEADS):
        sl = slice(HD * h, HD * h + HD)
        q, k, v = q_ref[0, :, sl], k_ref[0, :, sl], v_ref[0, :, sl]
        s = dot(k, q, NT) * SCALE + mask_ref[0]
        m = jnp.max(s, axis=0, keepdims=True)
        p = jnp.exp(s - m)
        total = jnp.sum(p, axis=0, keepdims=True)
        o = dot(v, p.astype(BF), TN) * (1.0 / total)
        cmix_ref[0, :, sl] = o.T.astype(BF)
        lse_ref[0, h : h + 1, :] = m + jnp.log(total)
    stream = stream + dot(cmix_ref[0], xo_ref[...]) + vec_ref[5:6]
    stream_ref[0] = stream
    unit, _ = unit_of(stream)
    norm_ref[0] = (unit * (1.0 + mod_ref[0, 4:5]) + mod_ref[0, 3:4]).astype(BF)


def middle_forward(mixed, x, mods, vecs, second, k, v, mask, waits=()):
    n, t, d = x.shape
    tb = min(256, t)
    rows = lambda w: pl.BlockSpec((1, tb, w), lambda i, j: (i, j, 0))
    weight = lambda c: constant((d, d), (0, c))
    outs = [
        ((n, t, d), BF),
        ((n, t, d), BF),
        ((n, t, d), BF),
        ((n, HEADS, t), F32),
        ((n, t, d), BF),
        ((n, t, d), F32),
        ((n, t, d), BF),
    ]
    out_specs = [rows(d)] * 3 + [pl.BlockSpec((1, HEADS, tb), lambda i, j: (i, 0, j))] + [rows(d)] * 3
    return call(
        middle_fwd_kernel,
        (mixed, x, mods, vecs, second, second, second, k, v, mask),
        [rows(d), rows(d), whole(mods.shape), constant(vecs.shape), weight(0), weight(1), weight(2)]
        + [whole(k.shape), whole(v.shape), whole(mask.shape)],
        outs,
        out_specs,
        grid=(n, t // tb),
        waits=waits,
    )


ROOT = (2.0 / 3.141592653589793) ** 0.5


def ff_kernel(x_ref, g_ref, mod_ref, e_ref, *refs, parts):
    cs, (bias_ref, act_ref, hg_ref, fg_ref, out_ref, sum_ref, gsum_ref) = refs[:parts], refs[parts:]
    ff = bias_ref.shape[1]
    pw = ff // parts
    x = x_ref[0]
    fg = (mod_ref[0, 5:6] * g_ref[0].astype(F32)).astype(BF)
    fg_ref[0] = fg

    @pl.when(pl.program_id(1) == 0)
    def _():
        sum_ref[...] = jnp.zeros_like(sum_ref)
        gsum_ref[...] = jnp.zeros_like(gsum_ref)

    gsum_ref[0] += jnp.sum(fg.astype(F32), axis=0, keepdims=True)
    back = 0.0
    for j in range(parts):
        cols = slice(j * pw, (j + 1) * pw)
        h = dot(x, e_ref[:, cols]) + bias_ref[:, cols]
        u = dot(fg, cs[j][...], NT)
        square = h * h
        th = jnp.tanh(h * (ROOT + (ROOT * 0.044715) * square))
        half = 0.5 + 0.5 * th
        act_ref[0, :, cols] = (h * half).astype(BF)
        slope = half + h * (1.0 - th * th) * (0.5 * ROOT + (1.5 * ROOT * 0.044715) * square)
        hg = (u * slope).astype(BF)
        hg_ref[0, :, cols] = hg
        sum_ref[0, :, cols] += jnp.sum(hg.astype(F32), axis=0, keepdims=True)
        back = back + dot(hg, e_ref[:, cols], NT)
    out_ref[0] = back.astype(BF)


def feed_forward(x, g, mods, expand, contracts, bias, waits=()):
    n, t, d = x.shape
    ff, parts = bias.shape[0], len(contracts)
    tb = min(256, t)
    rows = lambda w: pl.BlockSpec((1, tb, w), lambda i, j: (i, j, 0))
    return call(
        partial(ff_kernel, parts=parts),
        (x, g, mods, expand, *[c for c, _ in contracts], bias.reshape(1, ff)),
        [rows(d), rows(d), whole(mods.shape), constant((d, ff))]
        + [constant((ff // parts, d), (0, b)) for _, b in contracts]
        + [constant((1, ff))],
        [((n, t, ff), BF)] * 2 + [((n, t, d), BF)] * 2 + [((n, 1, ff), F32), ((n, 1, d), F32)],
        [rows(ff), rows(ff), rows(d), rows(d), whole((n, 1, ff)), whole((n, 1, d))],
        grid=(n, t // tb),
        waits=waits,
        vmem=44 << 20,
    )


def fed_kernel(*refs, chunks, parts, steps):
    acts, cs, outs = refs[:chunks], refs[chunks : chunks + parts], refs[chunks + parts :]
    pw = cs[0].shape[0]
    for c in range(chunks):
        fed = sum(dot(acts[c][0, :, j * pw : (j + 1) * pw], cs[j][...]) for j in range(parts))
        outs[c][0] = fed.astype(BF)


def fed_forward(acts, contracts, d, waits=()):
    n, t, ff = acts[0].shape
    parts = len(contracts)
    tb = min(256, t)
    rows = lambda w: pl.BlockSpec((1, tb, w), lambda i, j: (i, j, 0))
    return call(
        partial(fed_kernel, chunks=len(acts), parts=parts, steps=t // tb),
        (*acts, *[c for c, _ in contracts]),
        [rows(ff)] * len(acts) + [constant((ff // parts, d), (0, b)) for _, b in contracts],
        [((n, t, d), BF)] * len(acts),
        [rows(d)] * len(acts),
        grid=(n, t // tb),
        waits=waits,
        vmem=32 << 20,
    )


def columns_kernel(*refs, chunks):
    lefts, rights, out_ref = refs[:chunks], refs[chunks : 2 * chunks], refs[-1]
    out_ref[...] = sum(dot(a[...], b[...], TN) for a, b in zip(lefts, rights)).astype(BF)


def columns_wgrad(lefts, rights, across, width, first, into=None, waits=()):
    flat = lambda x: x.reshape(-1, x.shape[-1])
    lefts, rights = [flat(x) for x in lefts], [flat(x) for x in rights]
    d = (rights if across else lefts)[0].shape[1]
    m, wide = lefts[0].shape[1], rights[0].shape[1]
    steps = (m if across else wide) // d
    if across:
        specs = [pl.BlockSpec((x.shape[0], d), lambda s: (0, s)) for x in lefts] + [constant(x.shape) for x in rights]
    else:
        specs = [constant(x.shape) for x in lefts] + [pl.BlockSpec((x.shape[0], d), lambda s: (0, s)) for x in rights]
    ins = [*lefts, *rights]
    aliases = {}
    if into is not None:
        waits = (into, *waits)
        aliases = {len(ins): 0}
    return call(
        partial(columns_kernel, chunks=len(lefts)),
        ins,
        specs,
        [((d, width), BF)],
        [pl.BlockSpec((d, d), lambda s: (0, first + s))],
        grid=(steps,),
        waits=waits,
        vmem=44 << 20,
        aliases=aliases,
    )[0]


def finish_kernel(fed_ref, got_ref, stream_ref, g_ref, mod_ref, vec_ref, out_ref, sum_ref):
    fed = fed_ref[0].astype(F32) + got_ref[0].astype(F32) + vec_ref[6:7]
    out_ref[0] = (stream_ref[0] + mod_ref[0, 5:6] * fed).astype(BF)
    sum_ref[0] = jnp.sum(g_ref[0].astype(F32) * fed, axis=0, keepdims=True)


def finish_forward(fed, got, stream, g, mods, vecs, waits=()):
    n, t, d = stream.shape
    return call(
        finish_kernel,
        (fed, got, stream, g, mods, vecs),
        [whole(stream.shape)] * 4 + [whole(mods.shape), constant(vecs.shape)],
        [((n, t, d), BF), ((n, 1, d), F32)],
        [whole(stream.shape), whole((n, 1, d))],
        grid=(n,),
        waits=waits,
    )


def norm_back(w, unit, inverse, scale):
    u = w * (1.0 + scale)
    stream = (
        u - jnp.mean(u, axis=-1, keepdims=True) - unit * jnp.mean(u * unit, axis=-1, keepdims=True)
    ) * inverse
    return stream, jnp.sum(w, axis=0, keepdims=True), jnp.sum(w * unit, axis=0, keepdims=True)


def middle_bwd_kernel(
    pos_ref, nb_ref, got_ref, stream_ref, g_ref, mod_ref, xo_ref, xq_ref, so_ref, k_ref, v_ref, mask_ref,
    q_ref, lse_ref, attended_ref,
    cg_ref, xg_ref, ag_ref, grad_ref, dk_ref, dv_ref, sum_ref, *refs,
):
    tg_refs, cm_ref = refs[:-1], refs[-1]
    step = pl.program_id(1)
    unit, inverse = unit_of(stream_ref[0])
    w = nb_ref[0].astype(F32) + got_ref[0].astype(F32)
    back, shift, scale = norm_back(w, unit, inverse, mod_ref[0, 4:5])
    grad = back + g_ref[0].astype(F32)
    crossed = grad.astype(BF)
    cg_ref[0] = crossed
    cm_ref[...] = dot(crossed, xo_ref[...], NT).astype(BF)

    @pl.when(step == 0)
    def _():
        dk_ref[...] = jnp.zeros_like(dk_ref)
        dv_ref[...] = jnp.zeros_like(dv_ref)
        sum_ref[...] = jnp.zeros_like(sum_ref)

    for h in range(HEADS):
        sl = slice(HD * h, HD * h + HD)
        q, k, v, g = q_ref[0, :, sl], k_ref[0, :, sl], v_ref[0, :, sl], cm_ref[:, sl]
        p = jnp.exp(dot(k, q, NT) * SCALE + mask_ref[0] - lse_ref[0, h : h + 1, :])
        dp = dot(v, g, NT)
        ds = (p * (dp - jnp.sum(p * dp, axis=0, keepdims=True))).astype(BF)
        dv_ref[0, :, sl] += dot(p.astype(BF), g)
        dk_ref[0, :, sl] += dot(ds, q) * SCALE
        xg_ref[0, :, sl] = (dot(k, ds, TN) * SCALE).T.astype(BF)
    grad = grad + dot(xg_ref[0], xq_ref[...], NT)
    grad_ref[0] = grad
    attended_grad = (mod_ref[0, 2:3] * grad).astype(BF)
    ag_ref[0] = attended_grad
    tokens_grad = dot(attended_grad, so_ref[...], NT).astype(BF)
    if len(tg_refs) == 2:
        half = tokens_grad.shape[1] // 2
        low, high = tokens_grad[:, :half], tokens_grad[:, half:]
        tg_refs[0][0] = jnp.where(pos_ref[0] == 0, low, high)
        tg_refs[1][0] = jnp.where(pos_ref[0] == 0, high, low)
    else:
        tg_refs[0][0] = tokens_grad
    sums = [
        shift,
        scale,
        jnp.sum(grad * attended_ref[0].astype(F32), axis=0, keepdims=True),
        jnp.sum(crossed.astype(F32), axis=0, keepdims=True),
        jnp.sum(xg_ref[0].astype(F32), axis=0, keepdims=True),
        jnp.sum(attended_grad.astype(F32), axis=0, keepdims=True),
    ]
    for i, total in enumerate(sums):
        sum_ref[0, i : i + 1] += total


def middle_backward(pos, nb, got, stream, g, mods, second, k, v, mask, q, lse, attended, nsp, waits=()):
    n, t, d = stream.shape
    tb = min(256, t)
    rows = lambda w: pl.BlockSpec((1, tb, w), lambda i, j: (i, j, 0))
    weight = lambda c: constant((d, d), (0, c))
    stats = pl.BlockSpec((1, HEADS, tb), lambda i, j: (i, 0, j))
    pieces = 2 if nsp == 2 else 1
    outs = [((n, t, d), BF)] * 3 + [((n, t, d), F32), (k.shape, F32), (v.shape, F32), ((n, 8, d), F32)]
    return call(
        middle_bwd_kernel,
        (pos, nb, got, stream, g, mods, second, second, second, k, v, mask, q, lse, attended),
        [smem()]
        + [rows(d)] * 4
        + [whole(mods.shape), weight(2), weight(1), weight(0), whole(k.shape), whole(v.shape), whole(mask.shape)]
        + [rows(d), stats, rows(d)],
        outs + [((n, t, d // pieces), BF)] * pieces,
        [rows(d)] * 4 + [whole(k.shape), whole(v.shape), whole((n, 8, d))] + [rows(d // pieces)] * pieces,
        grid=(n, t // tb),
        scratch=[pltpu.VMEM((tb, d), BF)],
        waits=waits,
        vmem=44 << 20,
    )


def self_bwd_kernel(qkv_ref, *refs, chunks, heads):
    gs, (lse_ref, grad_ref) = refs[:chunks], refs[chunks:]
    for h in range(heads):
        spans = [slice((p * heads + h) * HD, (p * heads + h + 1) * HD) for p in range(3)]
        q, k, v = [qkv_ref[0, :, sl] for sl in spans]
        g = jnp.concatenate([r[0, :, spans[0]] for r in gs], axis=0) if chunks > 1 else gs[0][0, :, spans[0]]
        p = jnp.exp(dot(k, q, NT) * SCALE - lse_ref[0, h : h + 1, :])
        dp = dot(v, g, NT)
        delta = jnp.sum(p * dp, axis=0, keepdims=True)
        ds = (p * (dp - delta)).astype(BF)
        grad_ref[0, :, spans[2]] = dot(p.astype(BF), g).astype(BF)
        grad_ref[0, :, spans[1]] = (dot(ds, q) * SCALE).astype(BF)
        grad_ref[0, :, spans[0]] = (dot(k, ds, TN) * SCALE).T.astype(BF)


def self_backward(qkv, gs, lse, waits=()):
    n, t, w = qkv.shape
    heads = w // HD // 3
    return call(
        partial(self_bwd_kernel, chunks=len(gs), heads=heads),
        (qkv, *gs, lse),
        [whole(qkv.shape)] + [whole(g.shape) for g in gs] + [whole(lse.shape)],
        [((n, t, w), BF)],
        [whole((n, t, w))],
        grid=(n,),
        waits=waits,
        vmem=40 << 20,
    )[0]


def input_bwd_kernel(*refs, chunks):
    gs, xs, w_ref = refs[:chunks], refs[chunks : 2 * chunks], refs[2 * chunks]
    outs, sum_ref = refs[2 * chunks + 1 : -1], refs[-1]

    @pl.when(pl.program_id(1) == 0)
    def _():
        sum_ref[...] = jnp.zeros_like(sum_ref)

    for c in range(chunks):
        value = dot(gs[c][0], w_ref[:, : gs[c].shape[2]], NT)
        outs[c][0] = value.astype(BF)
        unit, _ = unit_of(xs[c][0].astype(F32))
        sum_ref[0, 0:1] += jnp.sum(value, axis=0, keepdims=True)
        sum_ref[0, 1:2] += jnp.sum(value * unit, axis=0, keepdims=True)


def input_backward(grad, xs, first, waits=()):
    n, t, w = grad.shape
    d = first.shape[0]
    chunks = len(xs)
    each = t // chunks
    tb = min(256, each)
    blocks = each // tb
    rows = pl.BlockSpec((1, tb, d), lambda i, j: (i, j, 0))
    return call(
        partial(input_bwd_kernel, chunks=chunks),
        (*[grad] * chunks, *xs, first),
        [pl.BlockSpec((1, tb, w), lambda i, j, c=c: (i, c * blocks + j, 0)) for c in range(chunks)]
        + [rows] * chunks
        + [constant(first.shape)],
        [((n, each, d), BF)] * chunks + [((n, 8, d), F32)],
        [rows] * chunks + [whole((n, 8, d))],
        grid=(n, blocks),
        waits=waits,
        vmem=36 << 20,
    )


def last_kernel(w_ref, got_ref, x_ref, mod_ref, grad_ref, out_ref):
    unit, inverse = unit_of(x_ref[0].astype(F32))
    w = w_ref[0].astype(F32) + got_ref[0].astype(F32)
    u = w * (1.0 + mod_ref[0, 1:2])
    back = u - jnp.mean(u, axis=-1, keepdims=True) - unit * jnp.mean(u * unit, axis=-1, keepdims=True)
    out_ref[0] = grad_ref[0] + back * inverse


def last_backward(w, got, x, mods, grad, waits=()):
    n, t, d = x.shape
    tb = min(256, t)
    rows = pl.BlockSpec((1, tb, d), lambda i, j: (i, j, 0))
    return call(
        last_kernel,
        (w, got, x, mods, grad),
        [rows, rows, rows, whole(mods.shape), rows],
        [((n, t, d), F32)],
        [rows],
        grid=(n, t // tb),
        waits=waits,
        vmem=16 << 20,
    )[0]


def wgrad_kernel(pos_ref, *refs, pairs, extra, r):
    at = 0
    lefts, rights = [], []
    for a, b in pairs:
        lefts.append(refs[at : at + a])
        rights.append(refs[at + a : at + a + b])
        at += a + b
    extras = refs[at : at + extra]
    own_ref, other_ref = refs[at + extra :]
    first = pos_ref[1] == 0
    chips = own_ref.shape[0]

    def put(value, col):
        w = value.shape[1]
        for c in range(chips):
            low, high = value[2 * c * r : 2 * c * r + r], value[2 * c * r + r : 2 * c * r + 2 * r]
            own_ref[c, :, col : col + w] = jnp.where(first, low, high).astype(BF)
            other_ref[c, :, col : col + w] = jnp.where(first, high, low).astype(BF)

    col = 0
    for left, right in zip(lefts, rights):
        width = right[0].shape[1]
        for a in range(0, width, 1152):
            b = min(a + 1152, width)
            put(sum(dot(x[...], y[:, a:b], TN) for x, y in zip(left, right)), col + a)
        col += width
    if extra:
        pad = own_ref.shape[2] - 128 - col
        if pad:
            own_ref[:, :, col : col + pad] = jnp.zeros((chips, r, pad), BF)
            other_ref[:, :, col : col + pad] = jnp.zeros((chips, r, pad), BF)
        put(extras[0][...].astype(F32), own_ref.shape[2] - 128)


def wgrad(pos, pairs, nf, extra=None, waits=()):
    flat = lambda x: x.reshape(-1, x.shape[-1])
    pairs = [([flat(x) for x in a], [flat(x) for x in b]) for a, b in pairs]
    m = pairs[0][0][0].shape[1]
    r = m // nf
    cols = sum(b[0].shape[1] for _, b in pairs)
    if extra is not None:
        cols = -(-cols // 128) * 128 + 128
    ins = [x for a, b in pairs for x in a + b] + ([] if extra is None else [extra])
    shape = (nf // 2, r, cols)
    return call(
        partial(wgrad_kernel, pairs=[(len(a), len(b)) for a, b in pairs], extra=int(extra is not None), r=r),
        (pos, *ins),
        [smem()] + [pl.BlockSpec(memory_space=pltpu.VMEM)] * len(ins),
        [(shape, BF)] * 2,
        [pl.BlockSpec(memory_space=pltpu.VMEM)] * 2,
        waits=waits,
        vmem=40 << 20,
    )


def core_sum_kernel(pos_ref, own_ref, got_ref, y_ref, other_ref):
    first = pos_ref[2] == 0
    low = own_ref[0].astype(F32) + got_ref[0].astype(F32)
    high = own_ref[1].astype(F32) + got_ref[1].astype(F32)
    y_ref[0] = jnp.where(first, low, high).astype(BF)
    other_ref[0] = jnp.where(first, high, low).astype(BF)


def y_sum_kernel(pos_ref, own_ref, got_ref, *outs):
    nz = len(outs)
    for d in range(nz):
        at = lax.rem(pos_ref[3] + d, nz)
        outs[d][...] = (own_ref[at].astype(F32) + got_ref[at].astype(F32)).astype(BF)


def z_sum_kernel(*refs):
    refs[-1][...] = sum(x[...].astype(F32) for x in refs[:-1]).astype(BF)


def in_vmem(kernel, ins, outs, waits=()):
    spec = pl.BlockSpec(memory_space=pltpu.VMEM)
    specs = [smem() if x.dtype == jnp.int32 else spec for x in ins]
    return call(kernel, ins, specs, [(s, BF) for s in outs], [spec] * len(outs), waits=waits, vmem=16 << 20)


def shift_z(x, nf, d):
    return lax.ppermute(x, "fsdp", [(i, (i + 4 * d) % nf) for i in range(nf)])


def cross_y(x, nf):
    return lax.ppermute(x, "fsdp", [(i, i ^ 2) for i in range(nf)])


def cross_core(x, nf):
    return lax.ppermute(x, "fsdp", [(i, i ^ 1) for i in range(nf)])


def sum_core(pos, own, other, nf, waits=()):
    _, r, w = own.shape
    two, one = pl.BlockSpec((2, r, w), lambda i: (i, 0, 0)), pl.BlockSpec((1, r, w), lambda i: (i, 0, 0))
    return call(
        core_sum_kernel,
        (pos, own, cross_core(other, nf)),
        [smem(), two, two],
        [((nf // 4, r, w), BF)] * 2,
        [one, one],
        grid=(nf // 4,),
        waits=waits,
        vmem=16 << 20,
    )


def sum_y(pos, mine, other, nf, waits=()):
    nz, r, w = mine.shape
    return in_vmem(y_sum_kernel, (pos, mine, cross_y(other, nf)), [(r, w)] * nz, waits)


def sum_z(chunks, nf, waits=()):
    got = [shift_z(chunks[d], nf, d) for d in range(1, len(chunks))]
    return in_vmem(z_sum_kernel, (chunks[0], *got), [chunks[0].shape], waits)[0]


def swap(x):
    return lax.ppermute(x, "sp", [(0, 1), (1, 0)])


def pick(x, index, axis):
    return lax.dynamic_index_in_dim(x, index, axis, keepdims=False)


def in_order(own, other, index, axis=-1):
    return jnp.where(
        index == 0, jnp.concatenate([own, other], axis=axis), jnp.concatenate([other, own], axis=axis)
    )


def halves(x, index, axis=-1):
    low, high = jnp.split(x, 2, axis=axis)
    return jnp.where(index == 0, low, high), jnp.where(index == 0, high, low)


def gather_tokens(x, nsp):
    if nsp == 2:
        return [x, swap(x)]
    return [lax.all_gather(x, "sp", axis=1, tiled=True)]


def scatter_tokens(parts, nsp):
    if nsp == 2:
        return parts[0], swap(parts[1])
    total = lax.psum_scatter(parts[0], "sp", scatter_dimension=1, tiled=True)
    return total, jnp.zeros_like(total)


def heads_to_tokens(x, nsp, index, others):
    if nsp == 2:
        half = x.shape[1] // 2
        return in_order(x[:, :half], after(swap(x[:, half:]), *others), index)
    return lax.all_to_all(x, "sp", split_axis=1, concat_axis=2, tiled=True)


def tokens_to_heads(parts, nsp):
    if nsp == 2:
        return [parts[0], swap(parts[1])]
    return [lax.all_to_all(parts[0], "sp", split_axis=2, concat_axis=1, tiled=True)]


def gather_axis(x, nsp, index, axis):
    if nsp == 2:
        return in_order(x, swap(x), index, axis)
    return lax.all_gather(x, "sp", axis=axis, tiled=True)


def scatter_axis(x, nsp, index, axis):
    if nsp == 2:
        own, other = halves(x, index, axis)
        return own.astype(F32) + swap(other.astype(BF)).astype(F32)
    return lax.psum_scatter(x.astype(BF), "sp", scatter_dimension=axis, tiled=True).astype(F32)


def sum_sp(x, nsp):
    if nsp == 2:
        return x.astype(F32) + swap(x).astype(F32)
    return lax.psum(x, "sp").astype(F32)


def gather_sp(x, nsp, index):
    if nsp == 2:
        got = swap(x)
        return [jnp.where(index == 0, x, got).astype(F32), jnp.where(index == 0, got, x).astype(F32)]
    return list(lax.all_gather(x, "sp").astype(F32))


def merge_sp(x, sums, gathers, nsp, index):
    (a, b), (c, d) = sums[0], gathers[0]
    if nsp == 2:
        got = swap(x)
        total = x[:, a:b].astype(F32) + got[:, a:b].astype(F32)
        x, got = x[:, c:d].astype(F32), got[:, c:d].astype(F32)
        return total, [jnp.where(index == 0, x, got), jnp.where(index == 0, got, x)]
    return lax.psum(x[:, a:b].astype(F32), "sp"), list(lax.all_gather(x[:, c:d], "sp").astype(F32))


def copy_kernel(at_ref, *refs, n, dim):
    ins, out, sems = refs[:n], refs[n], refs[n + 1]
    copies = []
    for i in range(n):
        index = (slice(None),) * dim + (at_ref[i],)
        copies.append(pltpu.make_async_copy(ins[i], out.at[index], sems.at[i]))
    for c in copies:
        c.start()
    for c in copies:
        c.wait()


def place_all(parts, at, dim, waits=()):
    n = len(parts)
    shape = parts[0].shape[:dim] + (n,) + parts[0].shape[dim:]
    return call(
        partial(copy_kernel, n=n, dim=dim),
        (at, *parts),
        [smem()] + anywhere(n),
        [(shape, parts[0].dtype)],
        [pl.BlockSpec(memory_space=pltpu.VMEM)],
        scratch=[pltpu.SemaphoreType.DMA((n,))],
        waits=waits,
        vmem=24 << 20,
    )[0]


def after(x, *others):
    return lax.optimization_barrier((x, *others))[0]


def column_sum(x):
    return jnp.sum(x, axis=(0, 1), dtype=F32)


def linear(x, w):
    return jnp.einsum("lsd,de->lse", x, w, preferred_element_type=F32)


def linear_back(x, w):
    return jnp.einsum("lse,de->lsd", x, w, preferred_element_type=F32)


def on_device(
    latent_tokens,
    caption_tokens,
    caption_len,
    time_embed,
    mod_table,
    self_input_weight,
    self_query_bias,
    self_value_bias,
    self_output_weight,
    self_output_bias,
    cross_query_weight,
    cross_query_bias,
    cross_keyval_weight,
    cross_value_bias,
    cross_output_weight,
    cross_output_bias,
    expand_weight,
    expand_bias,
    contract_weight,
    contract_bias,
    out_grad,
):
    nsp, nf = lax.axis_size("sp"), lax.axis_size("fsdp")
    sp, fsdp = lax.axis_index("sp"), lax.axis_index("fsdp")
    core, y, z, nz = fsdp % 2, (fsdp // 2) % 2, fsdp // 4, nf // 4
    pos = jnp.stack([sp, core, y, z]).astype(jnp.int32)
    latents, local_len, width = latent_tokens.shape
    rows = width // nf
    own = width // nsp
    hidden_rows = contract_weight.shape[0]
    hidden_own = hidden_rows // nsp
    parts = max(1, hidden_own // rows)
    block = hidden_own // parts
    part_width = nf * block

    def columns(w, pieces, groups=1):
        size = w.shape[1] // pieces // nsp // groups
        out = []
        for i in range(nsp):
            starts = [
                p * size * nsp * groups + (i * groups + g) * size for g in range(groups) for p in range(pieces)
            ]
            out.append(jnp.concatenate([w[:, a : a + size] for a in starts], axis=1))
        if nsp == 2:
            return jnp.where(sp == 0, out[0], out[1])
        return pick(jnp.stack(out), sp, 0)

    small = jnp.concatenate(
        [
            jnp.stack(
                [
                    self_query_bias,
                    self_value_bias,
                    self_output_bias,
                    cross_query_bias,
                    cross_value_bias,
                    cross_output_bias,
                    contract_bias,
                ]
            ),
            mod_table,
            expand_bias.reshape(-1, rows),
        ],
        axis=0,
    )
    smalls = small.shape[0]
    small = jnp.pad(small.T, ((0, 0), (0, 128 - smalls)))

    stream_swap = gather_tokens(latent_tokens, nsp)

    grads = gather_tokens(out_grad, nsp)
    caption_all = gather_axis(caption_tokens, nsp, sp, 1)
    stream_all = jnp.concatenate(stream_swap, axis=1)
    first = jnp.concatenate([columns(self_input_weight, 3), small], axis=1)
    second = jnp.concatenate(
        [self_output_weight, cross_query_weight, cross_output_weight, columns(cross_keyval_weight, 2)], axis=1
    )
    last = pick(expand_weight.reshape(rows, nf, nsp, parts, block), sp, 2)
    last = last.transpose(0, 2, 1, 3).reshape(rows, parts * part_width)
    contract_shard = pick(contract_weight.reshape(nsp, parts, block, width), sp, 0)
    if block == rows:
        last = jnp.concatenate([last] + [contract_shard[j] for j in range(parts)], axis=1)

    second = lax.all_gather(second, "fsdp", axis=0, tiled=True)
    ring = [first] + [shift_z(first, nf, d) for d in range(1, nz)]
    across = [cross_y(x, nf) for x in ring]
    at = jnp.stack([((z - d) % nz) * 2 + y for d in range(nz)] + [((z - d) % nz) * 2 + 1 - y for d in range(nz)])
    mine = place_all(ring + across, at.astype(jnp.int32), 0, (stream_all, last, caption_all))
    first = place_all([mine, cross_core(mine, nf)], jnp.stack([core, 1 - core]).astype(jnp.int32), 1)
    first = first.reshape(width, -1)
    whole_expand = lax.all_gather(after(last, mine), "fsdp", axis=0, tiled=True)
    if block == rows:
        whole_contracts = [(whole_expand, parts * part_width // width + j) for j in range(parts)]
    else:
        contract_shard = lax.all_gather(after(contract_shard[0], mine), "fsdp", axis=0, tiled=True)
        whole_contracts = [(contract_shard, 0)]

    smalls_all = first[:, 3 * own :].astype(F32).T

    def own_part(v):
        return pick(v.reshape(nsp, own), sp, 0)

    bias_query, bias_value = own_part(smalls_all[0]), own_part(smalls_all[1])
    bias_qkv = jnp.concatenate([bias_query, jnp.zeros_like(bias_query), bias_value]).reshape(1, 3 * own)
    vecs = smalls_all[:8]
    bias_xvalue = own_part(smalls_all[4])
    bias_expand = smalls_all[13:smalls].reshape(-1, nf, rows).transpose(1, 0, 2).reshape(nf, nsp, parts, block)
    bias_expand = pick(bias_expand, sp, 1).transpose(1, 0, 2).reshape(parts * part_width)
    mods = smalls_all[7:13][None] + time_embed.reshape(latents, 6, width)
    mods = jnp.pad(mods, ((0, 0), (0, 2), (0, 0)))

    norm_a, qkv = qkv_forward(stream_all, mods, bias_qkv, first, 3 * own)

    mixed, lse = self_forward(qkv, tuple(grads[1:]))
    second = after(second, mixed)
    whole_keyval = second[:, 3 * width :]

    keyval = linear(caption_all, whole_keyval)
    cross_keys = gather_axis(keyval[..., :own].astype(BF), nsp, sp, 2)
    cross_values = gather_axis((keyval[..., own:] + bias_xvalue).astype(BF), nsp, sp, 2)
    mixed_tokens = heads_to_tokens(mixed, nsp, sp, (cross_keys, cross_values))
    place = jnp.arange(caption_all.shape[1])
    mask = jnp.where(place[None] < caption_len[:, None], 0.0, NEG).astype(F32)[..., None]
    attended, attn_low, cross_queries, cross_lse, cross_mixed, after_cross, norm_b = middle_forward(
        mixed_tokens, latent_tokens, mods, vecs, second, cross_keys, cross_values, mask
    )

    norm_bs = gather_tokens(norm_b, nsp)
    ff_out = [None] * len(norm_bs)
    waits = ()
    for c in reversed(range(len(norm_bs))):
        ff_out[c] = feed_forward(norm_bs[c], grads[c], mods, whole_expand, whole_contracts, bias_expand, waits)
        waits = (ff_out[c][3],)
    acts, hidden_grads, fed_grads, norm_b_grads, hidden_sums, fed_sums = zip(*ff_out)
    norm_b_terms = scatter_tokens(norm_b_grads, nsp)
    expand_bgrad = sum(jnp.sum(x, axis=(0, 1)) for x in hidden_sums)
    if nsp == 2:
        contract_bgrad = jnp.sum(fed_sums[0], axis=(0, 1))
    else:
        contract_bgrad = column_sum(mods[:, 5:6] * out_grad.astype(F32))
    if block == rows:
        ff_own = columns_wgrad(acts, fed_grads, True, 2 * parts * width, 0)
        ff_own = columns_wgrad(norm_bs, hidden_grads, False, 2 * parts * width, parts, ff_own, (norm_b_terms[1],))
        ff_done = ff_own
        ff_own = lax.psum_scatter(ff_own, "fsdp", scatter_dimension=0, tiled=True)
        ff_sp = gather_sp(ff_own, nsp, sp)
        contract_sp, expand_sp = [g[:, : parts * width] for g in ff_sp], [g[:, parts * width :] for g in ff_sp]
    else:
        contract_own = jnp.einsum("lsd,lse->de", acts[0], fed_grads[0], preferred_element_type=F32).astype(BF)
        expand_own = jnp.einsum("lsd,lse->de", norm_bs[0], hidden_grads[0], preferred_element_type=F32).astype(BF)
        ff_done = expand_own
        contract_sp = gather_sp(lax.psum_scatter(contract_own, "fsdp", scatter_dimension=0, tiled=True), nsp, sp)
        expand_sp = gather_sp(lax.psum_scatter(expand_own, "fsdp", scatter_dimension=0, tiled=True), nsp, sp)

    crossed_grad, xquery_grad, attended_grad, attn_stream_grad, dk, dv, sums, *tokens_grads = middle_backward(
        pos, *norm_b_terms, after_cross, out_grad, mods, second, cross_keys, cross_values, mask,
        cross_queries, cross_lse, attended, nsp, waits=(ff_done,),
    )
    shift_b_grad, scale_b_grad, gate_a_grad = sums[:, 0], sums[:, 1], sums[:, 2]
    mixed_grads = tokens_to_heads(tokens_grads, nsp)
    cross_halves = wgrad(pos, [([attn_low], [xquery_grad]), ([cross_mixed], [crossed_grad])], nf)
    feds = fed_forward(acts, whole_contracts, width, (cross_halves[0],))
    cross_core_sum = sum_core(pos, *cross_halves, nf, waits=(feds[0],))

    keyval_grad = jnp.concatenate([scatter_axis(dk, nsp, sp, 2), scatter_axis(dv, nsp, sp, 2)], axis=-1).astype(BF)
    middle_halves = wgrad(
        pos, [([mixed_tokens], [attended_grad]), ([caption_all], [keyval_grad])], nf, waits=(cross_core_sum[0], mixed_grads[-1])
    )
    middle_core = sum_core(pos, *middle_halves, nf)
    caption_grad = scatter_axis(linear_back(keyval_grad, whole_keyval), nsp, sp, 1)
    xvalue_bgrad = column_sum(keyval_grad[..., own:])

    projected_grad = self_backward(qkv, mixed_grads, lse, (cross_core_sum[0], middle_core[0]))
    cross_y_sum = sum_y(pos, *cross_core_sum, nf, waits=(projected_grad,))
    input_out = input_backward(projected_grad, stream_swap, first, (cross_y_sum[0],))
    norm_a_terms = scatter_tokens(list(input_out[:-1]), nsp)
    shift_a_grad, scale_a_grad = input_out[-1][:, 0], input_out[-1][:, 1]
    fed_terms = scatter_tokens(feds, nsp)
    block_out, gate_b_grad = finish_forward(
        *fed_terms, after_cross, out_grad, mods, vecs, waits=(projected_grad,)
    )
    gate_b_grad = gate_b_grad[:, 0]

    def spread(x):
        return jnp.where(jnp.arange(nsp)[:, None] == sp, x[None], 0.0).reshape(nsp * x.shape[0])

    qkv_bgrad = column_sum(projected_grad)
    expand_bias_part = jnp.where(
        jnp.arange(nsp)[None, :, None, None] == sp,
        expand_bgrad.reshape(parts, nf, block).transpose(1, 0, 2)[:, None],
        0.0,
    ).reshape(nf, -1, rows)
    vectors = jnp.stack(
        [
            spread(qkv_bgrad[:own]),
            spread(qkv_bgrad[2 * own :]),
            jnp.sum(sums[:, 5], axis=0),
            jnp.sum(sums[:, 4], axis=0),
            spread(xvalue_bgrad),
            jnp.sum(sums[:, 3], axis=0),
            contract_bgrad,
            jnp.sum(shift_a_grad, axis=0),
            jnp.sum(scale_a_grad, axis=0),
            jnp.sum(gate_a_grad, axis=0),
            jnp.sum(shift_b_grad, axis=0),
            jnp.sum(scale_b_grad, axis=0),
            jnp.sum(gate_b_grad, axis=0),
        ]
    )
    vectors = jnp.concatenate([vectors, expand_bias_part.transpose(1, 0, 2).reshape(-1, width)])
    count = vectors.shape[0]
    vectors = jnp.pad(vectors.T, ((0, 0), (0, 128 - count))).astype(BF)
    middle_y = sum_y(pos, *middle_core, nf, waits=(block_out,))
    input_halves = wgrad(pos, [([norm_a], [projected_grad])], nf, extra=vectors, waits=(middle_y[0],))
    contract_out = jnp.concatenate(
        [g[:, j * width : (j + 1) * width] for g in contract_sp for j in range(contract_sp[0].shape[1] // width)], axis=0
    )
    expand_out = jnp.stack(
        [g.reshape(rows, parts, nf, block).transpose(0, 2, 1, 3) for g in expand_sp], axis=2
    ).reshape(rows, -1)
    input_core = sum_core(pos, *input_halves, nf)
    cross_own = sum_z(cross_y_sum, nf, waits=(input_core[0],))
    latent_grad = last_backward(*norm_a_terms, latent_tokens, mods, attn_stream_grad, (cross_own,))
    middle_own = sum_z(middle_y, nf, waits=(latent_grad, contract_out, expand_out))
    input_y = sum_y(pos, *input_core, nf, waits=(middle_own,))

    cross_sum = sum_sp(cross_own, nsp)
    xquery_out, xoutput_out = cross_sum[:, :width], cross_sum[:, width:]
    output_out, keyvals = merge_sp(middle_own, [(0, width)], [(width, width + 2 * own)], nsp, sp)
    keyval_out = jnp.concatenate([g[:, p * own : (p + 1) * own] for p in range(2) for g in keyvals], axis=1)
    input_own = sum_z(input_y, nf, waits=(xquery_out, xoutput_out, output_out, keyval_out))
    owned, inputs = merge_sp(
        input_own, [(input_own.shape[1] - 128, input_own.shape[1])], [(0, 3 * own)], nsp, sp
    )
    input_out = jnp.concatenate([g[:, p * own : (p + 1) * own] for p in range(3) for g in inputs], axis=1)
    owned = owned[:, :count].T
    expand_bout = owned[13:count].reshape(hidden_rows)

    embed_part = jnp.stack(
        [shift_a_grad, scale_a_grad, gate_a_grad, shift_b_grad, scale_b_grad, gate_b_grad], axis=1
    )
    time_grad = sum_sp(embed_part.reshape(latents, 6 * width), nsp)
    table_out = owned[7:13]
    return (
        block_out,
        latent_grad,
        caption_grad,
        time_grad,
        table_out,
        input_out,
        owned[0],
        owned[1],
        output_out,
        owned[2],
        xquery_out,
        owned[3],
        keyval_out,
        owned[4],
        xoutput_out,
        owned[5],
        expand_out,
        expand_bout,
        contract_out,
        owned[6],
    )


def solution(mesh):
    row, vec, tokens = P("fsdp", None), P("fsdp"), P("fsdp", "sp", None)
    in_specs = (
        (tokens, tokens, vec, row, P(None, "fsdp"), row, vec, vec)
        + (row, vec) * 2
        + (row, vec) * 4
        + (tokens,)
    )
    out_specs = (
        (tokens, tokens, tokens, row, P(None, "fsdp"), row, vec, vec) + (row, vec) * 2 + (row, vec) * 4
    )
    return jax.shard_map(
        on_device, mesh=mesh, in_specs=in_specs, out_specs=out_specs, check_vma=False
    )
```

time: 811 us -> 558 us (0.69)
  waiting for transfers between devices: 306 us -> 168 us
  matrix products: 137 us -> 5.09 us
  Pallas kernels: 72.1 us -> 199 us
  other arithmetic: 71.3 us -> 28.2 us
  starting transfers between devices: 83.7 us -> 45.3 us
  local copies, waits for them, and re-layouts: 115 us -> 86.9 us
    pallas_call x4 -> x27, Pallas kernels: 72.1 us -> 199 us  [call(): pl.pallas_call(body, name=(kernel.func if isinstance(kernel, partial) els...]
    ppermute x23 -> x19, waiting for transfers between devices: 122 us -> 39 us  [swap(): return lax.ppermute(x, 'sp', [(0, 1), (1, 0)])]
    dot_general x7 -> x1, matrix products: 54.4 us -> 2.77 us  [linear_back(): return jnp.einsum('lse,de->lsd', x, w, preferred_element_type=F32)]
    all_gather x4 -> x2, waiting for transfers between devices: 84.4 us -> 36.9 us  [the longest x1 36.9 us: on_device(): whole_expand = lax.all_gather(after(last, mine), 'fsdp', axis=0, tiled=True)]
    dot_general x7 -> x1, matrix products: 44.4 us -> 2.32 us  [linear(): return jnp.einsum('lsd,de->lse', x, w, preferred_element_type=F32)]
    dot_general x7 -> x0, matrix products: 37.8 us -> none  [weight_grad(): jnp.einsum('lsd,lse->de', x, g, preferred_element_type=F32).astype(BF)]
    unnamed x163 -> x221, local copies, waits for them, and re-layouts: 6.71 us -> 43.5 us
    convert_element_type x24 -> x1, other arithmetic: 34 us -> 0.18 us  [gather_sp(): jnp.where(index == 0, x, got).astype(F32)]
  transfers between devices with their start and end apart: 67 -> 45, of which waited for: 36 -> 21; matrix products, arithmetic and copies ran while one was open for 33% -> 13% of each run, Pallas kernels for 9% -> 32%
where the time goes in v2:
time: 558 us; the launch traced here: 549 us
  Pallas kernels  199 us (36%)
  waiting for transfers between devices  168 us (30%)
  local copies, waits for them, and re-layouts  86.9 us (16%)
  starting transfers between devices  45.3 us (8%)
  other arithmetic  28.2 us (5%)
  between operations  16.1 us (3%)
    pallas_call x27, Pallas kernels, call(): pl.pallas_call(body, name=(kernel.func if isinstance(kernel, partial) els...  199 us
    ppermute x12, waiting for transfers between devices, shift_z(): return lax.ppermute(x, 'fsdp', [(i, (i + 4 * d) % nf) for i in range(nf)])  68.9 us
    unnamed x221, local copies, waits for them, and re-layouts  43.5 us
    ppermute x19, waiting for transfers between devices, swap(): return lax.ppermute(x, 'sp', [(0, 1), (1, 0)])  39 us
    all_gather x1, waiting for transfers between devices, on_device(): whole_expand = lax.all_gather(after(last, mine), 'fsdp', axis=0, tiled=True)  36.9 us
    ppermute x19, starting transfers between devices, swap(): return lax.ppermute(x, 'sp', [(0, 1), (1, 0)])  21.3 us
    ppermute x7, waiting for transfers between devices, cross_y(): return lax.ppermute(x, 'fsdp', [(i, i ^ 2) for i in range(nf)])  19.7 us
    ppermute x12, starting transfers between devices, shift_z(): return lax.ppermute(x, 'fsdp', [(i, (i + 4 * d) % nf) for i in range(nf)])  17.4 us
  transfers between devices with their start and end apart: 45, of which 21 were waited for; matrix products, arithmetic and copies ran while one was open for 13% of the time, Pallas kernels for 32%

profile of v2, /device:TPU:8, one launch (start us, length us, event | category | flops | bytes accessed | tf_op | source)
XLA Modules:
  0.0 549.0 jit_solution(17499368669570251213)
XLA Ops:
  28.7 15.4 %collective-permute-done.2.refs_3_ = bf16[72,1856]{1,0:T(8,128)(2,1)} collective-permute-done((bf16[72,1856]{1,0:T(8,128)(2,1)}, bf16[72,1856]{1,0:T(8,128)(2,1)}, u32[]{:S(2)}, u32[]{:S(2)}) %collective-permute-start.2) | collective-permute-done | bytes 267296 | tf_op jit(solution)/shard_map/ppermute | solution.py:565
  45.9 13.8 %collective-permute-done.1.refs_2_ = bf16[72,1856]{1,0:T(8,128)(2,1)} collective-permute-done((bf16[72,1856]{1,0:T(8,128)(2,1)}, bf16[72,1856]{1,0:T(8,128)(2,1)}, u32[]{:S(2)}, u32[]{:S(2)}) %collective-permute-start.1) | collective-permute-done | bytes 267296 | tf_op jit(solution)/shard_map/ppermute | solution.py:565
  62.7 3.7 collective-permute-done.5.refs_6_
  85.4 10.3 %qkv_kernel.1 = (bf16[1,1024,1152]{2,1,0:T(8,128)(2,1)}, bf16[1,1024,1728]{2,1,0:T(8,128)(2,1)}) custom-call(bf16[1,1024,1152]{2,1,0:T(8,128)(2,1)} %copy-done.9, f32[1,8,1152]{2,1,0:T(8,128)} %pad.14.refs_1_.refs_2_.refs_5_.refs_4_.refs_3_, f32[1,1728]{1,0:T(1,128)} %reshape.541.refs_2_, bf16[1152,1856]{1,0:T(8,128)(2,1)} %bitcast.120), custom_call_target="tpu_custom_call" | custom-call | bytes 1048576 | tf_op jit(solution)/shard_map/qkv_kernel/pallas_call | solution.py:52
  100.4 15.0 %self_fwd_kernel.1 = (bf16[1,1024,576]{2,1,0:T(8,128)(2,1)S(1)}, f32[1,8,1024]{2,1,0:T(8,128)S(1)}) custom-call(bf16[1,1024,1728]{2,1,0:T(8,128)(2,1)S(1)} %copy-done.10, bf16[1,512,1152]{2,1,0:T(8,128)(2,1)S(1)} %collective-permute-done.10.refs_1_), custom_call_target="tpu_custom_call" | custom-call | bytes 1048576 | tf_op jit(solution)/shard_map/self_fwd_kernel/pallas_call | solution.py:52
  123.9 13.6 %collective-permute-done.12 = bf16[1,120,576]{2,1,0:T(8,128)(2,1)S(1)} collective-permute-done((bf16[1,120,576]{2,1,0:T(8,128)(2,1)S(1)}, bf16[1,120,576]{2,1,0:T(8,128)(2,1)S(1)}, u32[]{:S(2)}, u32[]{:S(2)}) %collective-permute-start.12) | collective-permute-done | bytes 138272 | tf_op jit(solution)/shard_map/ppermute | solution.py:602
  145.0 17.0 %middle_fwd_kernel.1 = (bf16[1,512,1152]{2,1,0:T(8,128)(2,1)}, bf16[1,512,1152]{2,1,0:T(8,128)(2,1)}, bf16[1,512,1152]{2,1,0:T(8,128)(2,1)}, f32[1,16,512]{2,1,0...) custom-call(bf16[1,512,1152]{2,1,0:T(8,128)(2,1)} %maximum_select_fusion.refs_0_, ...), custom_call_target="tpu_custom_call" | custom-call | bytes 1048576 | tf_op jit(solution)/shard_map/middle_fwd_kernel/pallas_call | solution.py:52
  168.7 36.9 %all-gather.5.cloned.1.call-done.refs_3_.refs_4_.refs_5_.refs_2_ = bf16[1152,4608]{1,0:T(8,128)(2,1)} async-done(((bf16[72,4608]{1,0:T(8,128)(2,1)}), bf16[1152,4608]{1,0:T(8,128)(2,1)}) %all-gather.5.cloned.1.call-update) | async-done | bytes 10616848 | tf_op jit(solution)/shard_map/all_gather | solution.py:816
  206.4 16.1 %ff_kernel.2 = (bf16[1,512,2304]{2,1,0:T(8,128)(2,1)S(1)}, bf16[1,512,2304]{2,1,0:T(8,128)(2,1)S(1)}, bf16[1,512,1152]{2,1,0:T(8,128)(2,1)S(1)}, bf16[1,512,1152...) custom-call(bf16[1,512,1152]{2,1,0:T(8,128)(2,1)S(1)} %collective-permute-done.14.refs_0_, ...), custom_call_target="tpu_custom_call" | custom-call | bytes 1048576 | tf_op jit(solution)/shard_map/ff_kernel/pallas_call | solution.py:52
  224.0 15.3 %ff_kernel.3 = (bf16[1,512,2304]{2,1,0:T(8,128)(2,1)S(1)}, bf16[1,512,2304]{2,1,0:T(8,128)(2,1)}, bf16[1,512,1152]{2,1,0:T(8,128)(2,1)S(1)}, bf16[1,512,1152]{2,...) custom-call(bf16[1,512,1152]{2,1,0:T(8,128)(2,1)S(1)} %copy-done.30, ...), custom_call_target="tpu_custom_call" | custom-call | bytes 1048576 | tf_op jit(solution)/shard_map/ff_kernel/pallas_call | solution.py:52
  240.3 8.6 %columns_kernel.2.refs_4_ = bf16[1152,4608]{1,0:T(8,128)(2,1)} custom-call(bf16[512,2304]{1,0:T(8,128)(2,1)S(1)} %bitcast.123, bf16[512,2304]{1,0:T(8,128)(2,1)S(1)} %bitcast.122, bf16[512,1152]{1,0:T(8,128)(2,1)S(1)} %bitcast.130, bf16[512,1152]{1,0:T(8,128)(2,1)S(1)} %bitcast.129), custom_call_target="tpu_custom_call" | custom-call | bytes 1048576 | tf_op jit(solution)/shard_map/columns_kernel/pallas_call | solution.py:52
  250.6 8.6 %columns_kernel.3.refs_15_ = bf16[1152,4608]{1,0:T(8,128)(2,1)} custom-call(bf16[512,1152]{1,0:T(8,128)(2,1)S(1)} %bitcast.125, bf16[512,1152]{1,0:T(8,128)(2,1)S(1)} %bitcast.124, bf16[512,2304]{1,0:T(8,128)(2,1)S(1)} %bitcast.127, bf16[512,2304]{1,0:T(8,128)(2,1)S(1)} %bitcast.126, ...), custom_call_target="tpu_custom_call", output_to_operand_aliasing={{}: (4, {})} | custom-call | bytes 1048576 | tf_op jit(solution)/shard_map/columns_kernel/pallas_call | solution.py:52
  263.1 22.3 %middle_bwd_kernel.1 = (bf16[1,512,1152]{2,1,0:T(8,128)(2,1)S(1)}, bf16[1,512,1152]{2,1,0:T(8,128)(2,1)S(1)}, bf16[1,512,1152]{2,1,0:T(8,128)(2,1)S(1)}, f32[1,5...) custom-call(s32[4]{0:T(128)S(1)} %pad_add_fusion.1.refs_0_, ...), custom_call_target="tpu_custom_call" | custom-call | bytes 1048576 | tf_op jit(solution)/shard_map/middle_bwd_kernel/pallas_call | solution.py:52
  285.5 5.3 wgrad_kernel.3
  300.0 4.1 copy-done
  307.5 7.8 %fed_kernel.1 = (bf16[1,512,1152]{2,1,0:T(8,128)(2,1)S(1)}, bf16[1,512,1152]{2,1,0:T(8,128)(2,1)S(1)}) custom-call(bf16[1,512,2304]{2,1,0:T(8,128)(2,1)S(1)} %copy-done.18, bf16[1,512,2304]{2,1,0:T(8,128)(2,1)S(1)} %copy-done.16, bf16[1152,4608]{1,0:T(8,128)(2,1)S(1)} %copy-done, bf16[1152,4608]{1,0:T(8,128)(2,1)S(1)} %copy-done, ...), custom_call_target="tpu_custom_call" | custom-call | bytes 1048576 | tf_op jit(solution)/shard_map/fed_kernel/pallas_call | solution.py:52
  325.7 4.5 wgrad_kernel.4
  333.2 3.8 collective-permute-done.21.refs_2_
  338.9 4.3 core_sum_kernel.4
  343.4 25.9 %self_bwd_kernel.1.refs_6_.refs_3_.refs_0_.refs_1_ = bf16[1,1024,1728]{2,1,0:T(8,128)(2,1)S(1)} custom-call(bf16[1,1024,1728]{2,1,0:T(8,128)(2,1)S(1)} %copy-done.11, bf16[1,512,576]{2,1,0:T(8,128)(2,1)S(1)} %copy-done.63, bf16[1,512,576]{2,1,0:T(8,128)(2,1)S(1)} %copy.98.refs_6_.refs_2_, f32[1,8,1024]{2,1,0:T(8,128)S(1)} %copy-done.67, ...), custom_call_target="tpu_custom_call" | custom-call | bytes 1048576 | tf_op jit(solution)/shard_map/self_bwd_kernel/pallas_call | solution.py:52
  371.4 4.7 collective-permute-done.22.refs_2_
  384.5 6.7 %input_bwd_kernel.1 = (bf16[1,512,1152]{2,1,0:T(8,128)(2,1)S(1)}, bf16[1,512,1152]{2,1,0:T(8,128)(2,1)S(1)}, f32[1,8,1152]{2,1,0:T(8,128)S(1)}) custom-call(bf16[1,1024,1728]{2,1,0:T(8,128)(2,1)S(1)} %copy-done.3, bf16[1,1024,1728]{2,1,0:T(8,128)(2,1)S(1)} %copy-done.3, bf16[1,512,1152]{2,1,0:T(8,128)(2,1)S(1)} %copy-done.8, ...), custom_call_target="tpu_custom_call" | custom-call | bytes 1048576 | tf_op jit(solution)/shard_map/input_bwd_kernel/pallas_call | solution.py:52
  393.3 4.6 finish_kernel.1
  399.2 7.7 %collective-permute-done.27.refs_2_ = bf16[4,72,2304]{2,1,0:T(8,128)(2,1)} collective-permute-done((bf16[4,72,2304]{2,1,0:T(8,128)(2,1)}, bf16[4,72,2304]{2,1,0:T(8,128)(2,1)}, u32[]{:S(2)}, u32[]{:S(2)}) %collective-permute-start.27) | collective-permute-done | bytes 1327136 | tf_op jit(solution)/shard_map/ppermute | solution.py:569
  412.4 5.7 %wgrad_kernel.5 = (bf16[8,72,1920]{2,1,0:T(8,128)(2,1)S(1)}, bf16[8,72,1920]{2,1,0:T(8,128)(2,1)S(1)}) custom-call(s32[4]{0:T(128)S(1)} %pad_add_fusion.1.refs_0_, bf16[1024,1152]{1,0:T(8,128)(2,1)S(1)} %bitcast.128, bf16[1024,1728]{1,0:T(8,128)(2,1)S(1)} %bitcast.118, bf16[1152,128]{1,0:T(8,128)(2,1)S(1)} %pad.15.refs_3_, ...), custom_call_target="tpu_custom_call" | custom-call | bytes 1048576 | tf_op jit(solution)/shard_map/wgrad_kernel/pallas_call | solution.py:52
  429.9 14.7 %collective-permute-done.24.refs_1_ = bf16[72,2304]{1,0:T(8,128)(2,1)S(1)} collective-permute-done((bf16[72,2304]{1,0:T(8,128)(2,1)S(1)}, bf16[72,2304]{1,0:T(8,128)(2,1)S(1)}, u32[]{:S(2)}, u32[]{:S(2)}) %collective-permute-start.24) | collective-permute-done | bytes 331808 | tf_op jit(solution)/shard_map/ppermute | solution.py:565
  444.5 6.3 %collective-permute-done.25.refs_2_ = bf16[72,2304]{1,0:T(8,128)(2,1)S(1)} collective-permute-done((bf16[72,2304]{1,0:T(8,128)(2,1)S(1)}, bf16[72,2304]{1,0:T(8,128)(2,1)S(1)}, u32[]{:S(2)}, u32[]{:S(2)}) %collective-permute-start.25) | collective-permute-done | bytes 331808 | tf_op jit(solution)/shard_map/ppermute | solution.py:565
  465.2 14.2 %collective-permute-done.35 = bf16[72,4608]{1,0:T(8,128)(2,1)S(1)} collective-permute-done((bf16[72,4608]{1,0:T(8,128)(2,1)}, bf16[72,4608]{1,0:T(8,128)(2,1)S(1)}, u32[]{:S(2)}, u32[]{:S(2)}) %collective-permute-start.35) | collective-permute-done | bytes 663584 | tf_op jit(solution)/shard_map/ppermute | solution.py:602
  490.3 4.4 reshape.563.refs_6_
  500.2 3.6 collective-permute-done.31.refs_2_
  512.5 11.7 %collective-permute-done.36.refs_1_ = bf16[72,1920]{1,0:T(8,128)(2,1)S(1)} collective-permute-done((bf16[72,1920]{1,0:T(8,128)(2,1)}, bf16[72,1920]{1,0:T(8,128)(2,1)S(1)}, u32[]{:S(2)}, u32[]{:S(2)}) %collective-permute-start.36) | collective-permute-done | bytes 276512 | tf_op jit(solution)/shard_map/ppermute | solution.py:565
  533.6 4.4 collective-permute-done.41
  (431 shorter events, 192.0 us)
Async XLA Ops:
  7.2 112.0 %all-gather.3.cloned.1.call-start = ((), (), s32[]{:S(2)}) async-start(), calls=%async_computation.1 | async-start | bytes 11280384 | tf_op jit(solution)/shard_map/all_gather | solution.py:809
  9.7 195.8 %all-gather.5.cloned.1.call-start = ((), (), s32[]{:S(2)}) async-start(), calls=%async_computation.2 | async-start | bytes 11280384 | tf_op jit(solution)/shard_map/all_gather | solution.py:816
  11.6 32.6 %collective-permute-start.2 = (bf16[72,1856]{1,0:T(8,128)(2,1)}, bf16[72,1856]{1,0:T(8,128)(2,1)}, u32[]{:S(2)}, u32[]{:S(2)}) collective-permute-start(bf16[72,1856]{1,0:T(8,128)(2,1)} %fusion.4.refs_1_), channel_id=1, source_target_pairs={{0,16},{2,18},{4,20},{6,22},{8,24},{10,26},{12,28},{14,30},{16,0},... | collective-permute-start | bytes 801800 | tf_op jit(solution)/shard_map/ppermute | solution.py:565
  14.6 45.1 %collective-permute-start.1 = (bf16[72,1856]{1,0:T(8,128)(2,1)}, bf16[72,1856]{1,0:T(8,128)(2,1)}, u32[]{:S(2)}, u32[]{:S(2)}) collective-permute-start(bf16[72,1856]{1,0:T(8,128)(2,1)} %fusion.4.refs_1_), channel_id=1, source_target_pairs={{0,8},{2,10},{4,12},{6,14},{8,16},{10,18},{12,20},{14,22},{16,24},... | collective-permute-start | bytes 801800 | tf_op jit(solution)/shard_map/ppermute | solution.py:565
  18.6 42.6 %collective-permute-start = (bf16[1,512,1152]{2,1,0:T(8,128)(2,1)S(1)}, bf16[1,512,1152]{2,1,0:T(8,128)(2,1)}, u32[]{:S(2)}, u32[]{:S(2)}) collective-permute-start(bf16[1,512,1152]{2,1,0:T(8,128)(2,1)S(1)} %copy-done.7), channel_id=1, source_target_pairs={{0,1},{1,0},{2,3},{3,2},{4,5},{5,4},{6,7},{7,6},{8,9},{9,8},{10,11... | collective-permute-start | bytes 3538952 | tf_op jit(solution)/shard_map/ppermute | solution.py:602
  25.3 37.4 %collective-permute-start.4 = (bf16[72,1856]{1,0:T(8,128)(2,1)}, bf16[72,1856]{1,0:T(8,128)(2,1)S(1)}, u32[]{:S(2)}, u32[]{:S(2)}) collective-permute-start(bf16[72,1856]{1,0:T(8,128)(2,1)} %fusion.4.refs_1_), channel_id=1, source_target_pairs={{0,4},{2,6},{4,0},{6,2},{8,12},{10,14},{12,8},{14,10},{16,20},{18,... | collective-permute-start | bytes 801800 | tf_op jit(solution)/shard_map/ppermute | solution.py:569
  28.2 34.5 %collective-permute-start.7 = (bf16[72,1856]{1,0:T(8,128)(2,1)}, bf16[72,1856]{1,0:T(8,128)(2,1)S(1)}, u32[]{:S(2)}, u32[]{:S(2)}) collective-permute-start(bf16[72,1856]{1,0:T(8,128)(2,1)} %collective-permute-done.3.refs_4_), channel_id=1, source_target_pairs={{0,4},{2,6},{4,0},{6,2},{8,12},{10,14},{12,8},{14,10},{16,20},{18,... | collective-permute-start | bytes 801800 | tf_op jit(solution)/shard_map/ppermute | solution.py:569
  44.1 18.6 %collective-permute-start.6 = (bf16[72,1856]{1,0:T(8,128)(2,1)}, bf16[72,1856]{1,0:T(8,128)(2,1)S(1)}, u32[]{:S(2)}, u32[]{:S(2)}) collective-permute-start(bf16[72,1856]{1,0:T(8,128)(2,1)} %collective-permute-done.2.refs_3_), channel_id=1, source_target_pairs={{0,4},{2,6},{4,0},{6,2},{8,12},{10,14},{12,8},{14,10},{16,20},{18,... | collective-permute-start | bytes 801800 | tf_op jit(solution)/shard_map/ppermute | solution.py:569
  69.9 393.9 %reduce-scatter.2.cloned.1.call-start = ((), (), s32[]{:S(2)}) async-start(), calls=%async_computation.3 | async-start | bytes 11280384 | tf_op jit(solution)/shard_map/reduce_scatter | solution.py:870
  70.0 28.4 %collective-permute-start.10 = (bf16[1,512,1152]{2,1,0:T(8,128)(2,1)S(1)}, bf16[1,512,1152]{2,1,0:T(8,128)(2,1)S(1)}, u32[]{:S(2)}, u32[]{:S(2)}) collective-permute-start(bf16[1,512,1152]{2,1,0:T(8,128)(2,1)S(1)} %copy-done.14), channel_id=1, source_target_pairs={{0,1},{1,0},{2,3},{3,2},{4,5},{5,4},{6,7},{7,6},{8,9},{9,8},{10,11... | collective-permute-start | bytes 3538952 | tf_op jit(solution)/shard_map/ppermute | solution.py:602
  117.8 22.6 %collective-permute-start.11 = (bf16[1,512,576]{1,2,0:T(8,128)(2,1)}, bf16[1,512,576]{1,2,0:T(8,128)(2,1)}, u32[]{:S(2)}, u32[]{:S(2)}) collective-permute-start(bf16[1,512,576]{1,2,0:T(8,128)(2,1)} %copy.92), channel_id=1, source_target_pairs={{0,1},{1,0},{2,3},{3,2},{4,5},{5,4},{6,7},{7,6},{8,9},{9,8},{10,11... | collective-permute-start | bytes 1769480 | tf_op jit(solution)/shard_map/ppermute | solution.py:602
  162.1 43.5 %collective-permute-start.14 = (bf16[1,512,1152]{2,1,0:T(8,128)(2,1)}, bf16[1,512,1152]{2,1,0:T(8,128)(2,1)S(1)}, u32[]{:S(2)}, u32[]{:S(2)}) collective-permute-start(bf16[1,512,1152]{2,1,0:T(8,128)(2,1)} %get-tuple-element.89.refs_0_), channel_id=1, source_target_pairs={{0,1},{1,0},{2,3},{3,2},{4,5},{5,4},{6,7},{7,6},{8,9},{9,8},{10,11... | collective-permute-start | bytes 3538952 | tf_op jit(solution)/shard_map/ppermute | solution.py:602
  222.5 28.1 %collective-permute-start.15 = (bf16[1,512,1152]{2,1,0:T(8,128)(2,1)S(1)}, bf16[1,512,1152]{2,1,0:T(8,128)(2,1)S(1)}, u32[]{:S(2)}, u32[]{:S(2)}) collective-permute-start(bf16[1,512,1152]{2,1,0:T(8,128)(2,1)S(1)} %get-tuple-element.91.refs_7_), channel_id=1, source_target_pairs={{0,1},{1,0},{2,3},{3,2},{4,5},{5,4},{6,7},{7,6},{8,9},{9,8},{10,11... | collective-permute-start | bytes 3538952 | tf_op jit(solution)/shard_map/ppermute | solution.py:602
  290.9 27.6 %collective-permute-start.18 = (bf16[8,72,2304]{2,1,0:T(8,128)(2,1)}, bf16[8,72,2304]{2,1,0:T(8,128)(2,1)}, u32[]{:S(2)}, u32[]{:S(2)}) collective-permute-start(bf16[8,72,2304]{2,1,0:T(8,128)(2,1)} %get-tuple-element.113), channel_id=1, source_target_pairs={{0,2},{2,0},{4,6},{6,4},{8,10},{10,8},{12,14},{14,12},{16,18},{18,... | collective-permute-start | bytes 7962632 | tf_op jit(solution)/shard_map/ppermute | solution.py:573
  293.6 21.7 %collective-permute-start.20 = (bf16[1,120,576]{2,1,0:T(8,128)(2,1)}, bf16[1,120,576]{2,1,0:T(8,128)(2,1)}, u32[]{:S(2)}, u32[]{:S(2)}) collective-permute-start(bf16[1,120,576]{2,1,0:T(8,128)(2,1)} %select_convert_fusion.2), channel_id=1, source_target_pairs={{0,1},{1,0},{2,3},{3,2},{4,5},{5,4},{6,7},{7,6},{8,9},{9,8},{10,11... | collective-permute-start | bytes 414728 | tf_op jit(solution)/shard_map/ppermute | solution.py:602
  295.9 20.7 %collective-permute-start.19 = (bf16[1,120,576]{2,1,0:T(8,128)(2,1)}, bf16[1,120,576]{2,1,0:T(8,128)(2,1)S(1)}, u32[]{:S(2)}, u32[]{:S(2)}) collective-permute-start(bf16[1,120,576]{2,1,0:T(8,128)(2,1)} %select_convert_fusion.3), channel_id=1, source_target_pairs={{0,1},{1,0},{2,3},{3,2},{4,5},{5,4},{6,7},{7,6},{8,9},{9,8},{10,11... | collective-permute-start | bytes 414728 | tf_op jit(solution)/shard_map/ppermute | solution.py:602
  298.6 18.4 %collective-permute-start.17 = (bf16[1,512,576]{1,2,0:T(8,128)(2,1)}, bf16[1,512,576]{1,2,0:T(8,128)(2,1)}, u32[]{:S(2)}, u32[]{:S(2)}) collective-permute-start(bf16[1,512,576]{1,2,0:T(8,128)(2,1)} %copy.95), channel_id=1, source_target_pairs={{0,1},{1,0},{2,3},{3,2},{4,5},{5,4},{6,7},{7,6},{8,9},{9,8},{10,11... | collective-permute-start | bytes 1769480 | tf_op jit(solution)/shard_map/ppermute | solution.py:602
  332.2 43.9 %collective-permute-start.22 = (bf16[4,72,2304]{2,1,0:T(8,128)(2,1)}, bf16[4,72,2304]{2,1,0:T(8,128)(2,1)}, u32[]{:S(2)}, u32[]{:S(2)}) collective-permute-start(bf16[4,72,2304]{2,1,0:T(8,128)(2,1)} %copy-done.75), channel_id=1, source_target_pairs={{0,4},{2,6},{4,0},{6,2},{8,12},{10,14},{12,8},{14,10},{16,20},{18,... | collective-permute-start | bytes 3981320 | tf_op jit(solution)/shard_map/ppermute | solution.py:569
  332.4 60.8 %collective-permute-start.16 = (bf16[1,512,1152]{2,1,0:T(8,128)(2,1)}, bf16[1,512,1152]{2,1,0:T(8,128)(2,1)}, u32[]{:S(2)}, u32[]{:S(2)}) collective-permute-start(bf16[1,512,1152]{2,1,0:T(8,128)(2,1)} %copy-done.76), channel_id=1, source_target_pairs={{0,1},{1,0},{2,3},{3,2},{4,5},{5,4},{6,7},{7,6},{8,9},{9,8},{10,11... | collective-permute-start | bytes 3538952 | tf_op jit(solution)/shard_map/ppermute | solution.py:602
  343.2 63.6 %collective-permute-start.27 = (bf16[4,72,2304]{2,1,0:T(8,128)(2,1)}, bf16[4,72,2304]{2,1,0:T(8,128)(2,1)}, u32[]{:S(2)}, u32[]{:S(2)}) collective-permute-start(bf16[4,72,2304]{2,1,0:T(8,128)(2,1)} %get-tuple-element.137), channel_id=1, source_target_pairs={{0,4},{2,6},{4,0},{6,2},{8,12},{10,14},{12,8},{14,10},{16,20},{18,... | collective-permute-start | bytes 3981320 | tf_op jit(solution)/shard_map/ppermute | solution.py:569
  418.3 39.2 %collective-permute-start.23 = (bf16[1,512,1152]{2,1,0:T(8,128)(2,1)S(1)}, bf16[1,512,1152]{2,1,0:T(8,128)(2,1)S(1)}, u32[]{:S(2)}, u32[]{:S(2)}) collective-permute-start(bf16[1,512,1152]{2,1,0:T(8,128)(2,1)S(1)} %copy-done.78), channel_id=1, source_target_pairs={{0,1},{1,0},{2,3},{3,2},{4,5},{5,4},{6,7},{7,6},{8,9},{9,8},{10,11... | collective-permute-start | bytes 3538952 | tf_op jit(solution)/shard_map/ppermute | solution.py:602
  419.8 24.7 %collective-permute-start.24 = (bf16[72,2304]{1,0:T(8,128)(2,1)S(1)}, bf16[72,2304]{1,0:T(8,128)(2,1)S(1)}, u32[]{:S(2)}, u32[]{:S(2)}) collective-permute-start(bf16[72,2304]{1,0:T(8,128)(2,1)S(1)} %copy-done.84), channel_id=1, source_target_pairs={{0,8},{2,10},{4,12},{6,14},{8,16},{10,18},{12,20},{14,22},{16,24},... | collective-permute-start | bytes 995336 | tf_op jit(solution)/shard_map/ppermute | solution.py:565
  422.1 28.7 %collective-permute-start.25 = (bf16[72,2304]{1,0:T(8,128)(2,1)S(1)}, bf16[72,2304]{1,0:T(8,128)(2,1)S(1)}, u32[]{:S(2)}, u32[]{:S(2)}) collective-permute-start(bf16[72,2304]{1,0:T(8,128)(2,1)S(1)} %copy-done.82), channel_id=1, source_target_pairs={{0,16},{2,18},{4,20},{6,22},{8,24},{10,26},{12,28},{14,30},{16,0},... | collective-permute-start | bytes 995336 | tf_op jit(solution)/shard_map/ppermute | solution.py:565
  424.4 28.4 %collective-permute-start.26 = (bf16[72,2304]{1,0:T(8,128)(2,1)S(1)}, bf16[72,2304]{1,0:T(8,128)(2,1)S(1)}, u32[]{:S(2)}, u32[]{:S(2)}) collective-permute-start(bf16[72,2304]{1,0:T(8,128)(2,1)S(1)} %copy-done.80), channel_id=1, source_target_pairs={{0,24},{2,26},{4,28},{6,30},{8,0},{10,2},{12,4},{14,6},{16,8},{18,... | collective-permute-start | bytes 995336 | tf_op jit(solution)/shard_map/ppermute | solution.py:565
  454.3 75.7 %collective-permute-start.29 = (bf16[1,60,1152]{2,1,0:T(8,128)(2,1)}, bf16[1,60,1152]{2,1,0:T(8,128)(2,1)}, u32[]{:S(2)}, u32[]{:S(2)}) collective-permute-start(bf16[1,60,1152]{2,1,0:T(8,128)(2,1)} %select_convert_fusion.4), channel_id=1, source_target_pairs={{0,1},{1,0},{2,3},{3,2},{4,5},{5,4},{6,7},{7,6},{8,9},{9,8},{10,11... | collective-permute-start | bytes 414728 | tf_op jit(solution)/shard_map/ppermute | solution.py:602
  455.9 40.8 %collective-permute-start.32 = (bf16[72,2304]{1,0:T(8,128)(2,1)}, bf16[72,2304]{1,0:T(8,128)(2,1)S(1)}, u32[]{:S(2)}, u32[]{:S(2)}) collective-permute-start(bf16[72,2304]{1,0:T(8,128)(2,1)} %get-tuple-element.143), channel_id=1, source_target_pairs={{0,8},{2,10},{4,12},{6,14},{8,16},{10,18},{12,20},{14,22},{16,24},... | collective-permute-start | bytes 995336 | tf_op jit(solution)/shard_map/ppermute | solution.py:565
  455.9 41.4 %collective-permute-start.33 = (bf16[72,2304]{1,0:T(8,128)(2,1)}, bf16[72,2304]{1,0:T(8,128)(2,1)}, u32[]{:S(2)}, u32[]{:S(2)}) collective-permute-start(bf16[72,2304]{1,0:T(8,128)(2,1)} %get-tuple-element.144), channel_id=1, source_target_pairs={{0,16},{2,18},{4,20},{6,22},{8,24},{10,26},{12,28},{14,30},{16,0},... | collective-permute-start | bytes 995336 | tf_op jit(solution)/shard_map/ppermute | solution.py:565
  457.4 39.9 %collective-permute-start.34 = (bf16[72,2304]{1,0:T(8,128)(2,1)}, bf16[72,2304]{1,0:T(8,128)(2,1)}, u32[]{:S(2)}, u32[]{:S(2)}) collective-permute-start(bf16[72,2304]{1,0:T(8,128)(2,1)} %get-tuple-element.145), channel_id=1, source_target_pairs={{0,24},{2,26},{4,28},{6,30},{8,0},{10,2},{12,4},{14,6},{16,8},{18,... | collective-permute-start | bytes 995336 | tf_op jit(solution)/shard_map/ppermute | solution.py:565
  479.5 24.3 %collective-permute-start.31 = (bf16[4,72,1920]{2,1,0:T(8,128)(2,1)}, bf16[4,72,1920]{2,1,0:T(8,128)(2,1)}, u32[]{:S(2)}, u32[]{:S(2)}) collective-permute-start(bf16[4,72,1920]{2,1,0:T(8,128)(2,1)} %get-tuple-element.142), channel_id=1, source_target_pairs={{0,4},{2,6},{4,0},{6,2},{8,12},{10,14},{12,8},{14,10},{16,20},{18,... | collective-permute-start | bytes 3317768 | tf_op jit(solution)/shard_map/ppermute | solution.py:569
  496.7 35.6 %collective-permute-start.30 = (f32[1,6912]{1,0:T(1,128)S(1)}, f32[1,6912]{1,0:T(1,128)}, u32[]{:S(2)}, u32[]{:S(2)}) collective-permute-start(f32[1,6912]{1,0:T(1,128)S(1)} %bitcast.143), channel_id=1, source_target_pairs={{0,1},{1,0},{2,3},{3,2},{4,5},{5,4},{6,7},{7,6},{8,9},{9,8},{10,11... | collective-permute-start | bytes 82952 | tf_op jit(solution)/shard_map/ppermute | solution.py:602
  505.9 21.2 %collective-permute-start.37 = (bf16[72,1920]{1,0:T(8,128)(2,1)S(1)}, bf16[72,1920]{1,0:T(8,128)(2,1)S(1)}, u32[]{:S(2)}, u32[]{:S(2)}) collective-permute-start(bf16[72,1920]{1,0:T(8,128)(2,1)S(1)} %get-tuple-element.148), channel_id=1, source_target_pairs={{0,16},{2,18},{4,20},{6,22},{8,24},{10,26},{12,28},{14,30},{16,0},... | collective-permute-start | bytes 829448 | tf_op jit(solution)/shard_map/ppermute | solution.py:565
  507.5 21.7 %collective-permute-start.38 = (bf16[72,1920]{1,0:T(8,128)(2,1)S(1)}, bf16[72,1920]{1,0:T(8,128)(2,1)S(1)}, u32[]{:S(2)}, u32[]{:S(2)}) collective-permute-start(bf16[72,1920]{1,0:T(8,128)(2,1)S(1)} %get-tuple-element.149), channel_id=1, source_target_pairs={{0,24},{2,26},{4,28},{6,30},{8,0},{10,2},{12,4},{14,6},{16,8},{18,... | collective-permute-start | bytes 829448 | tf_op jit(solution)/shard_map/ppermute | solution.py:565
  (121 other events, 928.2 us)
Sparse Core Ops, SparseCore 0:
  10.9 104.6 all-gather.2
  118.5 87.0 all-gather.4
  259.4 134.6 reduce-scatter.1

commit v3 on v2

--- a/solution.py
+++ b/solution.py
@@ -43,10 +43,16 @@
     return pl.BlockSpec(memory_space=pltpu.SMEM)
 
 
-def call(kernel, ins, in_specs, outs, out_specs, grid=(), scratch=(), waits=(), vmem=VMEM, aliases=None):
+def call(kernel, ins, in_specs, outs, out_specs, grid=(), scratch=(), waits=(), vmem=VMEM, aliases=None, token=False):
     n_in, n_wait = len(ins), len(waits)
+    if token:
+        outs, out_specs = [*outs, ((8, 128), F32)], [*out_specs, pl.BlockSpec((8, 128), lambda *_: (0, 0))]
 
     def body(*refs):
+        if token:
+            at = n_in + n_wait + len(outs) - 1
+            refs[at][...] = jnp.zeros((8, 128), F32)
+            refs = refs[:at] + refs[at + 1 :]
         kernel(*refs[:n_in], *refs[n_in + n_wait :])
 
     return pl.pallas_call(
@@ -226,29 +232,44 @@
     )
 
 
-def fed_kernel(*refs, chunks, parts, steps):
-    acts, cs, outs = refs[:chunks], refs[chunks : chunks + parts], refs[chunks + parts :]
+def fed_kernel(*refs, chunks, parts, share):
+    acts, gs, cs = refs[:chunks], refs[chunks : 2 * chunks], refs[2 * chunks : 2 * chunks + parts]
+    vec_ref, outs, sum_ref = refs[2 * chunks + parts], refs[2 * chunks + parts + 1 : -1], refs[-1]
     pw = cs[0].shape[0]
+    total = 0.0
     for c in range(chunks):
         fed = sum(dot(acts[c][0, :, j * pw : (j + 1) * pw], cs[j][...]) for j in range(parts))
         outs[c][0] = fed.astype(BF)
-
-
-def fed_forward(acts, contracts, d, waits=()):
+        if c == 0:
+            fed = fed + share * vec_ref[6:7]
+        total = total + jnp.sum(gs[c][0].astype(F32) * fed, axis=0, keepdims=True)
+
+    @pl.when(pl.program_id(1) == 0)
+    def _():
+        sum_ref[...] = jnp.zeros_like(sum_ref)
+
+    sum_ref[0] += total
+
+
+def fed_forward(acts, gs, contracts, vecs, d, share, waits=()):
     n, t, ff = acts[0].shape
     parts = len(contracts)
     tb = min(256, t)
     rows = lambda w: pl.BlockSpec((1, tb, w), lambda i, j: (i, j, 0))
-    return call(
-        partial(fed_kernel, chunks=len(acts), parts=parts, steps=t // tb),
-        (*acts, *[c for c, _ in contracts]),
-        [rows(ff)] * len(acts) + [constant((ff // parts, d), (0, b)) for _, b in contracts],
-        [((n, t, d), BF)] * len(acts),
-        [rows(d)] * len(acts),
+    *feds, sums = call(
+        partial(fed_kernel, chunks=len(acts), parts=parts, share=share),
+        (*acts, *gs, *[c for c, _ in contracts], vecs),
+        [rows(ff)] * len(acts)
+        + [rows(d)] * len(acts)
+        + [constant((ff // parts, d), (0, b)) for _, b in contracts]
+        + [constant(vecs.shape)],
+        [((n, t, d), BF)] * len(acts) + [((n, 1, d), F32)],
+        [rows(d)] * len(acts) + [whole((n, 1, d))],
         grid=(n, t // tb),
         waits=waits,
-        vmem=32 << 20,
-    )
+        vmem=28 << 20,
+    )
+    return feds, sums[:, 0]
 
 
 def columns_kernel(*refs, chunks):
@@ -284,22 +305,25 @@
     )[0]
 
 
-def finish_kernel(fed_ref, got_ref, stream_ref, g_ref, mod_ref, vec_ref, out_ref, sum_ref):
+def finish_kernel(fed_ref, got_ref, stream_ref, mod_ref, vec_ref, out_ref):
     fed = fed_ref[0].astype(F32) + got_ref[0].astype(F32) + vec_ref[6:7]
     out_ref[0] = (stream_ref[0] + mod_ref[0, 5:6] * fed).astype(BF)
-    sum_ref[0] = jnp.sum(g_ref[0].astype(F32) * fed, axis=0, keepdims=True)
-
-
-def finish_forward(fed, got, stream, g, mods, vecs, waits=()):
+
+
+def finish_forward(fed, got, stream, mods, vecs, waits=()):
     n, t, d = stream.shape
+    tb = min(256, t)
+    rows = pl.BlockSpec((1, tb, d), lambda i, j: (i, j, 0))
     return call(
         finish_kernel,
-        (fed, got, stream, g, mods, vecs),
-        [whole(stream.shape)] * 4 + [whole(mods.shape), constant(vecs.shape)],
-        [((n, t, d), BF), ((n, 1, d), F32)],
-        [whole(stream.shape), whole((n, 1, d))],
-        grid=(n,),
-        waits=waits,
+        (fed, got, stream, mods, vecs),
+        [rows] * 3 + [whole(mods.shape), constant(vecs.shape)],
+        [((n, t, d), BF)],
+        [rows],
+        grid=(n, t // tb),
+        waits=waits,
+        vmem=16 << 20,
+        token=True,
     )
 
 
@@ -314,9 +338,11 @@
 def middle_bwd_kernel(
     pos_ref, nb_ref, got_ref, stream_ref, g_ref, mod_ref, xo_ref, xq_ref, so_ref, k_ref, v_ref, mask_ref,
     q_ref, lse_ref, attended_ref,
-    cg_ref, xg_ref, ag_ref, grad_ref, dk_ref, dv_ref, sum_ref, *refs,
+    cg_ref, xg_ref, ag_ref, grad_ref, sum_ref, *refs, steps,
 ):
-    tg_refs, cm_ref = refs[:-1], refs[-1]
+    dk_ref, dv_ref, cm_ref = refs[-3:]
+    refs = refs[:-3]
+    tg_refs, kv_refs = refs[: len(refs) // 2], refs[len(refs) // 2 :]
     step = pl.program_id(1)
     unit, inverse = unit_of(stream_ref[0])
     w = nb_ref[0].astype(F32) + got_ref[0].astype(F32)
@@ -338,8 +364,8 @@
         p = jnp.exp(dot(k, q, NT) * SCALE + mask_ref[0] - lse_ref[0, h : h + 1, :])
         dp = dot(v, g, NT)
         ds = (p * (dp - jnp.sum(p * dp, axis=0, keepdims=True))).astype(BF)
-        dv_ref[0, :, sl] += dot(p.astype(BF), g)
-        dk_ref[0, :, sl] += dot(ds, q) * SCALE
+        dv_ref[:, sl] += dot(p.astype(BF), g)
+        dk_ref[:, sl] += dot(ds, q) * SCALE
         xg_ref[0, :, sl] = (dot(k, ds, TN) * SCALE).T.astype(BF)
     grad = grad + dot(xg_ref[0], xq_ref[...], NT)
     grad_ref[0] = grad
@@ -349,8 +375,13 @@
     if len(tg_refs) == 2:
         half = tokens_grad.shape[1] // 2
         low, high = tokens_grad[:, :half], tokens_grad[:, half:]
-        tg_refs[0][0] = jnp.where(pos_ref[0] == 0, low, high)
-        tg_refs[1][0] = jnp.where(pos_ref[0] == 0, high, low)
+        for i in range(2):
+
+            @pl.when(step == i)
+            def _(i=i):
+                tg_refs[0][0, :, i * half : (i + 1) * half] = jnp.where(pos_ref[0] == 0, low, high)
+                tg_refs[1][0, :, i * half : (i + 1) * half] = jnp.where(pos_ref[0] == 0, high, low)
+
     else:
         tg_refs[0][0] = tokens_grad
     sums = [
@@ -364,6 +395,18 @@
     for i, total in enumerate(sums):
         sum_ref[0, i : i + 1] += total
 
+    @pl.when(step == steps - 1)
+    def _():
+        d = dk_ref.shape[1]
+        for at, ref in ((0, dk_ref), (1, dv_ref)):
+            if len(kv_refs) == 2:
+                low, high = ref[:, : d // 2], ref[:, d // 2 :]
+                cols = slice(at * (d // 2), (at + 1) * (d // 2))
+                kv_refs[0][0, :, cols] = jnp.where(pos_ref[0] == 0, low, high).astype(BF)
+                kv_refs[1][0, :, cols] = jnp.where(pos_ref[0] == 0, high, low).astype(BF)
+            else:
+                kv_refs[0][0, :, at * d : (at + 1) * d] = ref[...].astype(BF)
+
 
 def middle_backward(pos, nb, got, stream, g, mods, second, k, v, mask, q, lse, attended, nsp, waits=()):
     n, t, d = stream.shape
@@ -372,18 +415,21 @@
     weight = lambda c: constant((d, d), (0, c))
     stats = pl.BlockSpec((1, HEADS, tb), lambda i, j: (i, 0, j))
     pieces = 2 if nsp == 2 else 1
-    outs = [((n, t, d), BF)] * 3 + [((n, t, d), F32), (k.shape, F32), (v.shape, F32), ((n, 8, d), F32)]
-    return call(
-        middle_bwd_kernel,
+    kv_shape = (n, k.shape[1], 2 * d // pieces)
+    tb = t // 2 if pieces == 2 else tb
+    tokens = [whole((n, tb, d))] * 2 if pieces == 2 else [rows(d)]
+    outs = [((n, t, d), BF)] * 3 + [((n, t, d), F32), ((n, 8, d), F32)]
+    return call(
+        partial(middle_bwd_kernel, steps=t // tb),
         (pos, nb, got, stream, g, mods, second, second, second, k, v, mask, q, lse, attended),
         [smem()]
         + [rows(d)] * 4
         + [whole(mods.shape), weight(2), weight(1), weight(0), whole(k.shape), whole(v.shape), whole(mask.shape)]
         + [rows(d), stats, rows(d)],
-        outs + [((n, t, d // pieces), BF)] * pieces,
-        [rows(d)] * 4 + [whole(k.shape), whole(v.shape), whole((n, 8, d))] + [rows(d // pieces)] * pieces,
+        outs + [((n, t // pieces, d), BF)] * pieces + [(kv_shape, BF)] * pieces,
+        [rows(d)] * 4 + [whole((n, 8, d))] + tokens + [whole(kv_shape)] * pieces,
         grid=(n, t // tb),
-        scratch=[pltpu.VMEM((tb, d), BF)],
+        scratch=[pltpu.VMEM(k.shape[1:], F32), pltpu.VMEM(k.shape[1:], F32), pltpu.VMEM((tb, d), BF)],
         waits=waits,
         vmem=44 << 20,
     )
@@ -394,7 +440,10 @@
     for h in range(heads):
         spans = [slice((p * heads + h) * HD, (p * heads + h + 1) * HD) for p in range(3)]
         q, k, v = [qkv_ref[0, :, sl] for sl in spans]
-        g = jnp.concatenate([r[0, :, spans[0]] for r in gs], axis=0) if chunks > 1 else gs[0][0, :, spans[0]]
+        g = gs[0][0, :, spans[0]]
+        if chunks > 1:
+            cols = [slice(i * heads * HD + h * HD, i * heads * HD + h * HD + HD) for i in range(2)]
+            g = jnp.concatenate([r[0, :, c] for r in gs for c in cols], axis=0)
         p = jnp.exp(dot(k, q, NT) * SCALE - lse_ref[0, h : h + 1, :])
         dp = dot(v, g, NT)
         delta = jnp.sum(p * dp, axis=0, keepdims=True)
@@ -415,19 +464,21 @@
         [whole((n, t, w))],
         grid=(n,),
         waits=waits,
-        vmem=40 << 20,
+        vmem=60 << 20,
     )[0]
 
 
 def input_bwd_kernel(*refs, chunks):
     gs, xs, w_ref = refs[:chunks], refs[chunks : 2 * chunks], refs[2 * chunks]
-    outs, sum_ref = refs[2 * chunks + 1 : -1], refs[-1]
+    outs, (sum_ref, gsum_ref) = refs[2 * chunks + 1 : -2], refs[-2:]
 
     @pl.when(pl.program_id(1) == 0)
     def _():
         sum_ref[...] = jnp.zeros_like(sum_ref)
+        gsum_ref[...] = jnp.zeros_like(gsum_ref)
 
     for c in range(chunks):
+        gsum_ref[0] += jnp.sum(gs[c][0].astype(F32), axis=0, keepdims=True)
         value = dot(gs[c][0], w_ref[:, : gs[c].shape[2]], NT)
         outs[c][0] = value.astype(BF)
         unit, _ = unit_of(xs[c][0].astype(F32))
@@ -449,11 +500,11 @@
         [pl.BlockSpec((1, tb, w), lambda i, j, c=c: (i, c * blocks + j, 0)) for c in range(chunks)]
         + [rows] * chunks
         + [constant(first.shape)],
-        [((n, each, d), BF)] * chunks + [((n, 8, d), F32)],
-        [rows] * chunks + [whole((n, 8, d))],
+        [((n, each, d), BF)] * chunks + [((n, 8, d), F32), ((n, 1, w), F32)],
+        [rows] * chunks + [whole((n, 8, d)), whole((n, 1, w))],
         grid=(n, blocks),
         waits=waits,
-        vmem=36 << 20,
+        vmem=60 << 20,
     )
 
 
@@ -478,70 +529,170 @@
         grid=(n, t // tb),
         waits=waits,
         vmem=16 << 20,
-    )[0]
-
-
-def wgrad_kernel(pos_ref, *refs, pairs, extra, r):
-    at = 0
-    lefts, rights = [], []
+        token=True,
+    )
+
+
+def wgrad_kernel(pos_ref, *refs, pairs, cuts, r):
+    at, terms = 0, []
     for a, b in pairs:
-        lefts.append(refs[at : at + a])
-        rights.append(refs[at + a : at + a + b])
+        terms.append((refs[at : at + a], refs[at + a : at + a + b]))
         at += a + b
-    extras = refs[at : at + extra]
-    own_ref, other_ref = refs[at + extra :]
+    outs = refs[at:]
+    owns, others = outs[: len(cuts)], outs[len(cuts) :]
     first = pos_ref[1] == 0
-    chips = own_ref.shape[0]
-
-    def put(value, col):
-        w = value.shape[1]
-        for c in range(chips):
+    for (pair, a, b), own_ref, other_ref in zip(cuts, owns, others):
+        left, right = terms[pair]
+        value = sum(dot(x[...], y[:, a:b], TN) for x, y in zip(left, right))
+        for c in range(own_ref.shape[0]):
             low, high = value[2 * c * r : 2 * c * r + r], value[2 * c * r + r : 2 * c * r + 2 * r]
-            own_ref[c, :, col : col + w] = jnp.where(first, low, high).astype(BF)
-            other_ref[c, :, col : col + w] = jnp.where(first, high, low).astype(BF)
-
-    col = 0
-    for left, right in zip(lefts, rights):
-        width = right[0].shape[1]
-        for a in range(0, width, 1152):
-            b = min(a + 1152, width)
-            put(sum(dot(x[...], y[:, a:b], TN) for x, y in zip(left, right)), col + a)
-        col += width
-    if extra:
-        pad = own_ref.shape[2] - 128 - col
-        if pad:
-            own_ref[:, :, col : col + pad] = jnp.zeros((chips, r, pad), BF)
-            other_ref[:, :, col : col + pad] = jnp.zeros((chips, r, pad), BF)
-        put(extras[0][...].astype(F32), own_ref.shape[2] - 128)
-
-
-def wgrad(pos, pairs, nf, extra=None, waits=()):
+            own_ref[c] = jnp.where(first, low, high).astype(BF)
+            other_ref[c] = jnp.where(first, high, low).astype(BF)
+
+
+def wgrad(pos, pairs, nf, waits=()):
     flat = lambda x: x.reshape(-1, x.shape[-1])
     pairs = [([flat(x) for x in a], [flat(x) for x in b]) for a, b in pairs]
     m = pairs[0][0][0].shape[1]
     r = m // nf
-    cols = sum(b[0].shape[1] for _, b in pairs)
-    if extra is not None:
-        cols = -(-cols // 128) * 128 + 128
-    ins = [x for a, b in pairs for x in a + b] + ([] if extra is None else [extra])
-    shape = (nf // 2, r, cols)
-    return call(
-        partial(wgrad_kernel, pairs=[(len(a), len(b)) for a, b in pairs], extra=int(extra is not None), r=r),
+    cuts = []
+    for i, (_, right) in enumerate(pairs):
+        width = right[0].shape[1]
+        cuts += [(i, a, min(a + 1152, width)) for a in range(0, width, 1152)]
+    ins = [x for a, b in pairs for x in a + b]
+    shapes = [((nf // 2, r, b - a), BF) for _, a, b in cuts]
+    vmem = pl.BlockSpec(memory_space=pltpu.VMEM)
+    outs = call(
+        partial(wgrad_kernel, pairs=[(len(a), len(b)) for a, b in pairs], cuts=cuts, r=r),
         (pos, *ins),
-        [smem()] + [pl.BlockSpec(memory_space=pltpu.VMEM)] * len(ins),
-        [(shape, BF)] * 2,
-        [pl.BlockSpec(memory_space=pltpu.VMEM)] * 2,
+        [smem()] + [vmem] * len(ins),
+        shapes * 2,
+        [vmem] * (2 * len(cuts)),
         waits=waits,
         vmem=40 << 20,
     )
-
-
-def core_sum_kernel(pos_ref, own_ref, got_ref, y_ref, other_ref):
+    return list(outs[: len(cuts)]), list(outs[len(cuts) :])
+
+
+def vectors_kernel(pos_ref, sums_ref, a_ref, gate_ref, qkv_ref, xv_ref, fed_ref, *refs, parts, r):
+    hiddens, (own_ref, other_ref, all_ref) = refs[:-3], refs[-3:]
+    sp = pos_ref[0]
+    all_ref[...] = jnp.zeros_like(all_ref)
+    sums, a_sums = jnp.sum(sums_ref[...], axis=0), jnp.sum(a_ref[...], axis=0)
+    qkv = jnp.sum(qkv_ref[...], axis=0)
+    own = qkv.shape[1] // 3
+
+    def spread(row, value):
+        for i in range(2):
+            all_ref[row : row + 1, i * own : (i + 1) * own] = jnp.where(sp == i, value, 0.0)
+
+    spread(0, qkv[:, :own])
+    spread(1, qkv[:, 2 * own :])
+    spread(4, xv_ref[...])
+    fed = jnp.sum(fed_ref[...], axis=0)
+    gate = jnp.sum(gate_ref[...], axis=0)
+    rows = {2: sums[5:6], 3: sums[4:5], 5: sums[3:4], 6: fed, 7: a_sums[0:1], 8: a_sums[1:2]}
+    rows |= {9: sums[2:3], 10: sums[0:1], 11: sums[1:2], 12: gate}
+    for row, value in rows.items():
+        all_ref[row : row + 1] = value
+    hidden = sum(jnp.sum(h[...], axis=0) for h in hiddens)
+    pw = hidden.shape[1] // parts
+    for i in range(2):
+        for j in range(parts):
+            row = 13 + i * parts + j
+            all_ref[row : row + 1] = jnp.where(sp == i, hidden[:, j * pw : (j + 1) * pw], 0.0)
+    columns = all_ref[...].T
+    first = pos_ref[1] == 0
+    for c in range(own_ref.shape[0]):
+        low, high = columns[2 * c * r : 2 * c * r + r], columns[2 * c * r + r : 2 * c * r + 2 * r]
+        own_ref[c] = jnp.where(first, low, high).astype(BF)
+        other_ref[c] = jnp.where(first, high, low).astype(BF)
+
+
+def vector_halves(pos, sums, a_sums, gate, qkv, xv, fed, hiddens, parts, nf, waits=()):
+    d = sums.shape[2]
+    ins = (pos, sums, a_sums, gate, qkv, xv, fed, *hiddens)
+    vmem = pl.BlockSpec(memory_space=pltpu.VMEM)
+    return call(
+        partial(vectors_kernel, parts=parts, r=d // nf),
+        ins,
+        [smem()] + [vmem] * (len(ins) - 1),
+        [((nf // 2, d // nf, 128), BF)] * 2,
+        [vmem] * 2,
+        scratch=[pltpu.VMEM((128, d), F32)],
+        waits=waits,
+        vmem=16 << 20,
+    )
+
+
+def last_out_kernel(pos_ref, x_ref, got_ref, kv_ref, in_ref, vec_ref):
+    first = pos_ref[0] == 0
+    own = kv_ref.shape[1] // 4
+    for p in range(5):
+        x, got = x_ref[:, p * own : (p + 1) * own].astype(F32), got_ref[:, p * own : (p + 1) * own].astype(F32)
+        ref, at = (kv_ref, p) if p < 2 else (in_ref, p - 2)
+        ref[:, 2 * at * own : (2 * at + 1) * own] = jnp.where(first, x, got)
+        ref[:, (2 * at + 1) * own : (2 * at + 2) * own] = jnp.where(first, got, x)
+    vec_ref[...] = x_ref[:, 5 * own :].astype(F32) + got_ref[:, 5 * own :].astype(F32)
+
+
+def last_outputs(pos, x, own):
+    vmem = pl.BlockSpec(memory_space=pltpu.VMEM)
+    r = x.shape[0]
+    return call(
+        last_out_kernel,
+        (pos, x, swap(x)),
+        [smem()] + [vmem] * 2,
+        [((r, 4 * own), F32), ((r, 6 * own), F32), ((r, 128), F32)],
+        [vmem] * 3,
+        vmem=16 << 20,
+    )
+
+
+def ff_out_kernel(pos_ref, x_ref, got_ref, c_ref, e_ref, *, parts, nf):
+    first = pos_ref[0] == 0
+    r, d = x_ref.shape[0], c_ref.shape[1]
+    for i in range(2):
+        for j in range(parts):
+            cols = slice(j * d, (j + 1) * d)
+            value = jnp.where(first == (i == 0), x_ref[:, cols], got_ref[:, cols])
+            c_ref[(i * parts + j) * r : (i * parts + j + 1) * r] = value.astype(F32)
+    for j in range(parts):
+        cols = slice((parts + j) * d, (parts + j + 1) * d)
+        x, got = x_ref[:, cols].astype(F32), got_ref[:, cols].astype(F32)
+        low, high = jnp.where(first, x, got), jnp.where(first, got, x)
+        for f in range(nf):
+            at = f * 2 * parts * r + j * r
+            e_ref[:, at : at + r] = low[:, f * r : (f + 1) * r]
+            e_ref[:, at + parts * r : at + parts * r + r] = high[:, f * r : (f + 1) * r]
+
+
+def ff_outputs(pos, x, parts, d, nf, waits=()):
+    vmem = pl.BlockSpec(memory_space=pltpu.VMEM)
+    r = x.shape[0]
+    return call(
+        partial(ff_out_kernel, parts=parts, nf=nf),
+        (pos, x, swap(x)),
+        [smem()] + [vmem] * 2,
+        [((2 * parts * r, d), F32), ((r, 2 * parts * d), F32)],
+        [vmem] * 2,
+        waits=waits,
+        vmem=16 << 20,
+        token=True,
+    )
+
+
+def core_sum_kernel(pos_ref, *refs, pieces):
+    owns, gots, (y_ref, other_ref) = refs[:pieces], refs[pieces : 2 * pieces], refs[2 * pieces :]
     first = pos_ref[2] == 0
-    low = own_ref[0].astype(F32) + got_ref[0].astype(F32)
-    high = own_ref[1].astype(F32) + got_ref[1].astype(F32)
-    y_ref[0] = jnp.where(first, low, high).astype(BF)
-    other_ref[0] = jnp.where(first, high, low).astype(BF)
+    at = 0
+    for own, got in zip(owns, gots):
+        cols = slice(at, at + own.shape[2])
+        low = own[0].astype(F32) + got[0].astype(F32)
+        high = own[1].astype(F32) + got[1].astype(F32)
+        y_ref[0, :, cols] = jnp.where(first, low, high).astype(BF)
+        other_ref[0, :, cols] = jnp.where(first, high, low).astype(BF)
+        at += own.shape[2]
 
 
 def y_sum_kernel(pos_ref, own_ref, got_ref, *outs):
@@ -573,13 +724,14 @@
     return lax.ppermute(x, "fsdp", [(i, i ^ 1) for i in range(nf)])
 
 
-def sum_core(pos, own, other, nf, waits=()):
-    _, r, w = own.shape
-    two, one = pl.BlockSpec((2, r, w), lambda i: (i, 0, 0)), pl.BlockSpec((1, r, w), lambda i: (i, 0, 0))
-    return call(
-        core_sum_kernel,
-        (pos, own, cross_core(other, nf)),
-        [smem(), two, two],
+def sum_core(pos, owns, others, nf, waits=()):
+    r, w = owns[0].shape[1], sum(x.shape[2] for x in owns)
+    two = [pl.BlockSpec((2,) + x.shape[1:], lambda i: (i, 0, 0)) for x in owns]
+    one = pl.BlockSpec((1, r, w), lambda i: (i, 0, 0))
+    return call(
+        partial(core_sum_kernel, pieces=len(owns)),
+        (pos, *owns, *[cross_core(x, nf) for x in others]),
+        [smem(), *two, *two],
         [((nf // 4, r, w), BF)] * 2,
         [one, one],
         grid=(nf // 4,),
@@ -843,7 +995,7 @@
     keyval = linear(caption_all, whole_keyval)
     cross_keys = gather_axis(keyval[..., :own].astype(BF), nsp, sp, 2)
     cross_values = gather_axis((keyval[..., own:] + bias_xvalue).astype(BF), nsp, sp, 2)
-    mixed_tokens = heads_to_tokens(mixed, nsp, sp, (cross_keys, cross_values))
+    mixed_tokens = after(heads_to_tokens(mixed, nsp, sp, (cross_keys, cross_values)), mixed)
     place = jnp.arange(caption_all.shape[1])
     mask = jnp.where(place[None] < caption_len[:, None], 0.0, NEG).astype(F32)[..., None]
     attended, attn_low, cross_queries, cross_lse, cross_mixed, after_cross, norm_b = middle_forward(
@@ -877,94 +1029,120 @@
         contract_sp = gather_sp(lax.psum_scatter(contract_own, "fsdp", scatter_dimension=0, tiled=True), nsp, sp)
         expand_sp = gather_sp(lax.psum_scatter(expand_own, "fsdp", scatter_dimension=0, tiled=True), nsp, sp)
 
-    crossed_grad, xquery_grad, attended_grad, attn_stream_grad, dk, dv, sums, *tokens_grads = middle_backward(
+    crossed_grad, xquery_grad, attended_grad, attn_stream_grad, sums, *rest = middle_backward(
         pos, *norm_b_terms, after_cross, out_grad, mods, second, cross_keys, cross_values, mask,
         cross_queries, cross_lse, attended, nsp, waits=(ff_done,),
     )
     shift_b_grad, scale_b_grad, gate_a_grad = sums[:, 0], sums[:, 1], sums[:, 2]
+    tokens_grads, keyval_parts = rest[: len(rest) // 2], rest[len(rest) // 2 :]
     mixed_grads = tokens_to_heads(tokens_grads, nsp)
-    cross_halves = wgrad(pos, [([attn_low], [xquery_grad]), ([cross_mixed], [crossed_grad])], nf)
-    feds = fed_forward(acts, whole_contracts, width, (cross_halves[0],))
-    cross_core_sum = sum_core(pos, *cross_halves, nf, waits=(feds[0],))
-
-    keyval_grad = jnp.concatenate([scatter_axis(dk, nsp, sp, 2), scatter_axis(dv, nsp, sp, 2)], axis=-1).astype(BF)
-    middle_halves = wgrad(
-        pos, [([mixed_tokens], [attended_grad]), ([caption_all], [keyval_grad])], nf, waits=(cross_core_sum[0], mixed_grads[-1])
-    )
-    middle_core = sum_core(pos, *middle_halves, nf)
+    feds, gate_b_grad = fed_forward(
+        acts, grads, whole_contracts, vecs, width, 1.0 if nsp == 2 else 1.0 / nsp, (attended_grad,)
+    )
+    fed_terms = scatter_tokens(feds, nsp)
+    if nsp == 2:
+        keyval_grad = (keyval_parts[0].astype(F32) + swap(keyval_parts[1]).astype(F32)).astype(BF)
+    else:
+        dk, dv = jnp.split(keyval_parts[0], 2, axis=-1)
+        keyval_grad = jnp.concatenate([scatter_axis(dk, nsp, sp, 2), scatter_axis(dv, nsp, sp, 2)], axis=-1)
+        keyval_grad = keyval_grad.astype(BF)
+    outer_halves = wgrad(
+        pos,
+        [([attn_low], [xquery_grad]), ([cross_mixed], [crossed_grad]), ([mixed_tokens], [attended_grad])],
+        nf,
+        (feds[0], mixed_grads[-1], keyval_grad),
+    )
+    outer_core = sum_core(pos, *outer_halves, nf)
     caption_grad = scatter_axis(linear_back(keyval_grad, whole_keyval), nsp, sp, 1)
     xvalue_bgrad = column_sum(keyval_grad[..., own:])
 
-    projected_grad = self_backward(qkv, mixed_grads, lse, (cross_core_sum[0], middle_core[0]))
-    cross_y_sum = sum_y(pos, *cross_core_sum, nf, waits=(projected_grad,))
-    input_out = input_backward(projected_grad, stream_swap, first, (cross_y_sum[0],))
-    norm_a_terms = scatter_tokens(list(input_out[:-1]), nsp)
-    shift_a_grad, scale_a_grad = input_out[-1][:, 0], input_out[-1][:, 1]
-    fed_terms = scatter_tokens(feds, nsp)
-    block_out, gate_b_grad = finish_forward(
-        *fed_terms, after_cross, out_grad, mods, vecs, waits=(projected_grad,)
-    )
-    gate_b_grad = gate_b_grad[:, 0]
-
-    def spread(x):
-        return jnp.where(jnp.arange(nsp)[:, None] == sp, x[None], 0.0).reshape(nsp * x.shape[0])
-
-    qkv_bgrad = column_sum(projected_grad)
-    expand_bias_part = jnp.where(
-        jnp.arange(nsp)[None, :, None, None] == sp,
-        expand_bgrad.reshape(parts, nf, block).transpose(1, 0, 2)[:, None],
-        0.0,
-    ).reshape(nf, -1, rows)
-    vectors = jnp.stack(
-        [
-            spread(qkv_bgrad[:own]),
-            spread(qkv_bgrad[2 * own :]),
-            jnp.sum(sums[:, 5], axis=0),
-            jnp.sum(sums[:, 4], axis=0),
-            spread(xvalue_bgrad),
-            jnp.sum(sums[:, 3], axis=0),
-            contract_bgrad,
-            jnp.sum(shift_a_grad, axis=0),
-            jnp.sum(scale_a_grad, axis=0),
-            jnp.sum(gate_a_grad, axis=0),
-            jnp.sum(shift_b_grad, axis=0),
-            jnp.sum(scale_b_grad, axis=0),
-            jnp.sum(gate_b_grad, axis=0),
-        ]
-    )
-    vectors = jnp.concatenate([vectors, expand_bias_part.transpose(1, 0, 2).reshape(-1, width)])
-    count = vectors.shape[0]
-    vectors = jnp.pad(vectors.T, ((0, 0), (0, 128 - count))).astype(BF)
-    middle_y = sum_y(pos, *middle_core, nf, waits=(block_out,))
-    input_halves = wgrad(pos, [([norm_a], [projected_grad])], nf, extra=vectors, waits=(middle_y[0],))
-    contract_out = jnp.concatenate(
-        [g[:, j * width : (j + 1) * width] for g in contract_sp for j in range(contract_sp[0].shape[1] // width)], axis=0
-    )
-    expand_out = jnp.stack(
-        [g.reshape(rows, parts, nf, block).transpose(0, 2, 1, 3) for g in expand_sp], axis=2
-    ).reshape(rows, -1)
-    input_core = sum_core(pos, *input_halves, nf)
-    cross_own = sum_z(cross_y_sum, nf, waits=(input_core[0],))
-    latent_grad = last_backward(*norm_a_terms, latent_tokens, mods, attn_stream_grad, (cross_own,))
-    middle_own = sum_z(middle_y, nf, waits=(latent_grad, contract_out, expand_out))
-    input_y = sum_y(pos, *input_core, nf, waits=(middle_own,))
-
-    cross_sum = sum_sp(cross_own, nsp)
-    xquery_out, xoutput_out = cross_sum[:, :width], cross_sum[:, width:]
-    output_out, keyvals = merge_sp(middle_own, [(0, width)], [(width, width + 2 * own)], nsp, sp)
-    keyval_out = jnp.concatenate([g[:, p * own : (p + 1) * own] for p in range(2) for g in keyvals], axis=1)
-    input_own = sum_z(input_y, nf, waits=(xquery_out, xoutput_out, output_out, keyval_out))
-    owned, inputs = merge_sp(
-        input_own, [(input_own.shape[1] - 128, input_own.shape[1])], [(0, 3 * own)], nsp, sp
-    )
-    input_out = jnp.concatenate([g[:, p * own : (p + 1) * own] for p in range(3) for g in inputs], axis=1)
+    projected_grad = self_backward(qkv, mixed_grads, lse, (outer_core[0],))
+    input_out = input_backward(projected_grad, stream_swap, first)
+    norm_a_terms = scatter_tokens(list(input_out[:-2]), nsp)
+    shift_a_grad, scale_a_grad = input_out[-2][:, 0], input_out[-2][:, 1]
+    if nsp == 2 and block == rows:
+        vector_parts = vector_halves(
+            pos, sums, input_out[-2], gate_b_grad[:, None], input_out[-1], xvalue_bgrad[None], fed_sums[0],
+            hidden_sums, parts, nf,
+        )
+    else:
+
+        def spread(x):
+            return jnp.where(jnp.arange(nsp)[:, None] == sp, x[None], 0.0).reshape(nsp * x.shape[0])
+
+        qkv_bgrad = column_sum(input_out[-1])
+        expand_bias_part = jnp.where(
+            jnp.arange(nsp)[None, :, None, None] == sp,
+            expand_bgrad.reshape(parts, nf, block).transpose(1, 0, 2)[:, None],
+            0.0,
+        ).reshape(nf, -1, rows)
+        vectors = jnp.stack(
+            [
+                spread(qkv_bgrad[:own]),
+                spread(qkv_bgrad[2 * own :]),
+                jnp.sum(sums[:, 5], axis=0),
+                jnp.sum(sums[:, 4], axis=0),
+                spread(xvalue_bgrad),
+                jnp.sum(sums[:, 3], axis=0),
+                contract_bgrad,
+                jnp.sum(shift_a_grad, axis=0),
+                jnp.sum(scale_a_grad, axis=0),
+                jnp.sum(gate_a_grad, axis=0),
+                jnp.sum(shift_b_grad, axis=0),
+                jnp.sum(scale_b_grad, axis=0),
+                jnp.sum(gate_b_grad, axis=0),
+            ]
+        )
+        vectors = jnp.concatenate([vectors, expand_bias_part.transpose(1, 0, 2).reshape(-1, width)])
+        vectors = jnp.pad(vectors.T, ((0, 0), (0, 128 - vectors.shape[0]))).astype(BF)
+        vectors = vectors.reshape(nf // 2, 2, rows, 128)
+        vector_parts = (pick(vectors, core, 1), pick(vectors, 1 - core, 1))
+    count = 13 + hidden_rows // rows
+    input_own, input_other = wgrad(
+        pos, [([caption_all], [keyval_grad]), ([norm_a], [projected_grad])], nf, (vector_parts[0], fed_terms[1])
+    )
+    outer_y = sum_y(pos, *outer_core, nf, waits=(input_own[0],))
+    input_core = sum_core(
+        pos, input_own + [vector_parts[0]], input_other + [vector_parts[1]], nf, waits=(outer_y[0],)
+    )
+    outer_own = sum_z(outer_y, nf, waits=(input_core[0], norm_a_terms[1]))
+    input_y = sum_y(pos, *input_core, nf, waits=(outer_own,))
+    latent_grad, *tokens = last_backward(*norm_a_terms, latent_tokens, mods, attn_stream_grad, (input_y[0],))
+    block_out, token = finish_forward(*fed_terms, after_cross, mods, vecs, waits=(input_y[0],))
+    tokens.append(token)
+
+    if nsp == 2 and block == rows:
+        contract_out, expand_out, token = ff_outputs(pos, ff_own, parts, width, nf, (input_y[0],))
+        tokens.append(token)
+    else:
+        contract_out = jnp.concatenate(
+            [
+                g[:, j * width : (j + 1) * width]
+                for g in contract_sp
+                for j in range(contract_sp[0].shape[1] // width)
+            ],
+            axis=0,
+        )
+        expand_out = jnp.stack(
+            [g.reshape(rows, parts, nf, block).transpose(0, 2, 1, 3) for g in expand_sp], axis=2
+        ).reshape(rows, -1)
+    embed_part = jnp.stack(
+        [shift_a_grad, scale_a_grad, gate_a_grad, shift_b_grad, scale_b_grad, gate_b_grad], axis=1
+    )
+    time_grad = sum_sp(embed_part.reshape(latents, 6 * width), nsp)
+    outer_sum = sum_sp(outer_own, nsp)
+    xquery_out, xoutput_out, output_out = [outer_sum[:, i * width : (i + 1) * width] for i in range(3)]
+    input_own = sum_z(input_y, nf, waits=(*tokens, time_grad))
+    if nsp == 2:
+        keyval_out, input_wout, owned = last_outputs(pos, input_own, own)
+    else:
+        inputs = list(lax.all_gather(input_own[:, : 5 * own], "sp").astype(F32))
+        keyval_out = jnp.concatenate([g[:, p * own : (p + 1) * own] for p in range(2) for g in inputs], axis=1)
+        input_wout = jnp.concatenate([g[:, p * own : (p + 1) * own] for p in range(2, 5) for g in inputs], axis=1)
+        owned = sum_sp(input_own[:, 5 * own :], nsp)
     owned = owned[:, :count].T
     expand_bout = owned[13:count].reshape(hidden_rows)
 
-    embed_part = jnp.stack(
-        [shift_a_grad, scale_a_grad, gate_a_grad, shift_b_grad, scale_b_grad, gate_b_grad], axis=1
-    )
-    time_grad = sum_sp(embed_part.reshape(latents, 6 * width), nsp)
     table_out = owned[7:13]
     return (
         block_out,
@@ -972,7 +1150,7 @@
         caption_grad,
         time_grad,
         table_out,
-        input_out,
+        input_wout,
         owned[0],
         owned[1],
         output_out,

time: 558 us -> 533 us (0.955)
  local copies, waits for them, and re-layouts: 86.9 us -> 51.5 us
  waiting for transfers between devices: 168 us -> 193 us
  other arithmetic: 28.2 us -> 12.8 us
    ppermute x19 -> x17, waiting for transfers between devices: 39 us -> 57.9 us  [swap(): return lax.ppermute(x, 'sp', [(0, 1), (1, 0)])]
    ppermute x7 -> x6, waiting for transfers between devices: 19.7 us -> 9.63 us  [cross_y(): return lax.ppermute(x, 'fsdp', [(i, i ^ 2) for i in range(nf)])]
    unnamed x221 -> x165, local copies, waits for them, and re-layouts: 43.5 us -> 34.2 us
    reshape x6 -> x0, local copies, waits for them, and re-layouts: 9.23 us -> none  [the longest x4 4.7 us: on_device(): g.reshape(rows, parts, nf, block).transpose(0, 2, 1, 3)]
    ppermute x12 -> x9, waiting for transfers between devices: 68.9 us -> 77.3 us  [shift_z(): return lax.ppermute(x, 'fsdp', [(i, (i + 4 * d) % nf) for i in range(nf)])]
    all_gather x1, waiting for transfers between devices: 36.9 us -> 43.4 us  [on_device(): whole_expand = lax.all_gather(after(last, mine), 'fsdp', axis=0, tiled=True)]
    pallas_call x27 -> x26, Pallas kernels: 199 us -> 203 us  [call(): pl.pallas_call(body, name=(kernel.func if isinstance(kernel, partial) els...]
    ppermute x12 -> x9, starting transfers between devices: 17.4 us -> 13.8 us  [shift_z(): return lax.ppermute(x, 'fsdp', [(i, (i + 4 * d) % nf) for i in range(nf)])]
  transfers between devices with their start and end apart: 45 -> 43, of which waited for: 21 -> 23; matrix products, arithmetic and copies ran while one was open for 13% -> 6% of each run, Pallas kernels for 32% -> 33%
where the time goes in v3:
time: 533 us; the launch traced here: 525 us
  Pallas kernels  203 us (38%)
  waiting for transfers between devices  193 us (36%)
  local copies, waits for them, and re-layouts  51.5 us (10%)
  starting transfers between devices  43.8 us (8%)
  between operations  15.8 us (3%)
  other arithmetic  12.8 us (2%)
    pallas_call x26, Pallas kernels, call(): pl.pallas_call(body, name=(kernel.func if isinstance(kernel, partial) els...  203 us
    ppermute x9, waiting for transfers between devices, shift_z(): return lax.ppermute(x, 'fsdp', [(i, (i + 4 * d) % nf) for i in range(nf)])  77.3 us
    ppermute x17, waiting for transfers between devices, swap(): return lax.ppermute(x, 'sp', [(0, 1), (1, 0)])  57.9 us
    all_gather x1, waiting for transfers between devices, on_device(): whole_expand = lax.all_gather(after(last, mine), 'fsdp', axis=0, tiled=True)  43.4 us
    unnamed x165, local copies, waits for them, and re-layouts  34.2 us
    ppermute x17, starting transfers between devices, swap(): return lax.ppermute(x, 'sp', [(0, 1), (1, 0)])  22.1 us
    ppermute x9, starting transfers between devices, shift_z(): return lax.ppermute(x, 'fsdp', [(i, (i + 4 * d) % nf) for i in range(nf)])  13.8 us
  transfers between devices with their start and end apart: 43, of which 23 were waited for; matrix products, arithmetic and copies ran while one was open for 6% of the time, Pallas kernels for 33%

profile of v3, /device:TPU:8, one launch (start us, length us, event | category | flops | bytes accessed | tf_op | source)
XLA Modules:
  0.0 525.5 jit_solution(10122253830539144957)
XLA Ops:
  11.6 3.0 collective-permute-start.2
  28.7 15.4 %collective-permute-done.2.refs_3_ = bf16[72,1856]{1,0:T(8,128)(2,1)} collective-permute-done((bf16[72,1856]{1,0:T(8,128)(2,1)}, bf16[72,1856]{1,0:T(8,128)(2,1)}, u32[]{:S(2)}, u32[]{:S(2)}) %collective-permute-start.2) | collective-permute-done | bytes 267296 | tf_op jit(solution)/shard_map/ppermute | solution.py:716
  45.9 13.8 %collective-permute-done.1.refs_2_ = bf16[72,1856]{1,0:T(8,128)(2,1)} collective-permute-done((bf16[72,1856]{1,0:T(8,128)(2,1)}, bf16[72,1856]{1,0:T(8,128)(2,1)}, u32[]{:S(2)}, u32[]{:S(2)}) %collective-permute-start.1) | collective-permute-done | bytes 267296 | tf_op jit(solution)/shard_map/ppermute | solution.py:716
  62.7 3.7 collective-permute-done.5.refs_6_
  83.1 10.3 %qkv_kernel.1 = (bf16[1,1024,1152]{2,1,0:T(8,128)(2,1)}, bf16[1,1024,1728]{2,1,0:T(8,128)(2,1)}) custom-call(bf16[1,1024,1152]{2,1,0:T(8,128)(2,1)} %copy-done.3, f32[1,8,1152]{2,1,0:T(8,128)} %pad.9.refs_1_.refs_2_.refs_5_.refs_3_, f32[1,1728]{1,0:T(1,128)} %reshape.377.refs_2_, bf16[1152,1856]{1,0:T(8,128)(2,1)} %bitcast.81), custom_call_target="tpu_custom_call" | custom-call | bytes 1048576 | tf_op jit(solution)/shard_map/qkv_kernel/pallas_call | solution.py:58
  93.4 5.1 collective-permute-done.10.refs_1_.refs_3_
  101.0 15.0 %self_fwd_kernel.1 = (bf16[1,1024,576]{2,1,0:T(8,128)(2,1)S(1)}, f32[1,8,1024]{2,1,0:T(8,128)S(1)}) custom-call(bf16[1,1024,1728]{2,1,0:T(8,128)(2,1)S(1)} %copy-done.4, bf16[1,512,1152]{2,1,0:T(8,128)(2,1)S(1)} %collective-permute-done.10.refs_1_.refs_3_), custom_call_target="tpu_custom_call" | custom-call | bytes 1048576 | tf_op jit(solution)/shard_map/self_fwd_kernel/pallas_call | solution.py:58
  123.0 13.4 %collective-permute-done.12 = bf16[1,120,576]{2,1,0:T(8,128)(2,1)S(1)} collective-permute-done((bf16[1,120,576]{2,1,0:T(8,128)(2,1)S(1)}, bf16[1,120,576]{2,1,0:T(8,128)(2,1)S(1)}, u32[]{:S(2)}, u32[]{:S(2)}) %collective-permute-start.12) | collective-permute-done | bytes 138272 | tf_op jit(solution)/shard_map/ppermute | solution.py:754
  142.4 17.1 %middle_fwd_kernel.1 = (bf16[1,512,1152]{2,1,0:T(8,128)(2,1)}, bf16[1,512,1152]{2,1,0:T(8,128)(2,1)}, bf16[1,512,1152]{2,1,0:T(8,128)(2,1)}, f32[1,16,512]{2,1,0...) custom-call(bf16[1,512,1152]{2,1,0:T(8,128)(2,1)} %maximum_select_fusion.refs_0_, ...), custom_call_target="tpu_custom_call" | custom-call | bytes 1048576 | tf_op jit(solution)/shard_map/middle_fwd_kernel/pallas_call | solution.py:58
  162.2 43.4 %all-gather.5.cloned.1.call-done.refs_3_.refs_4_.refs_5_ = bf16[1152,4608]{1,0:T(8,128)(2,1)} async-done(((bf16[72,4608]{1,0:T(8,128)(2,1)}), bf16[1152,4608]{1,0:T(8,128)(2,1)}) %all-gather.5.cloned.1.call-update) | async-done | bytes 10616848 | tf_op jit(solution)/shard_map/all_gather | solution.py:968
  206.4 16.2 %ff_kernel.2 = (bf16[1,512,2304]{2,1,0:T(8,128)(2,1)S(1)}, bf16[1,512,2304]{2,1,0:T(8,128)(2,1)S(1)}, bf16[1,512,1152]{2,1,0:T(8,128)(2,1)S(1)}, bf16[1,512,1152...) custom-call(bf16[1,512,1152]{2,1,0:T(8,128)(2,1)S(1)} %collective-permute-done.14.refs_0_, ...), custom_call_target="tpu_custom_call" | custom-call | bytes 1048576 | tf_op jit(solution)/shard_map/ff_kernel/pallas_call | solution.py:58
  224.2 15.3 %ff_kernel.3 = (bf16[1,512,2304]{2,1,0:T(8,128)(2,1)S(1)}, bf16[1,512,2304]{2,1,0:T(8,128)(2,1)}, bf16[1,512,1152]{2,1,0:T(8,128)(2,1)S(1)}, bf16[1,512,1152]{2,...) custom-call(bf16[1,512,1152]{2,1,0:T(8,128)(2,1)S(1)} %copy-done.28, ...), custom_call_target="tpu_custom_call" | custom-call | bytes 1048576 | tf_op jit(solution)/shard_map/ff_kernel/pallas_call | solution.py:58
  240.6 8.6 %columns_kernel.2.refs_4_ = bf16[1152,4608]{1,0:T(8,128)(2,1)} custom-call(bf16[512,2304]{1,0:T(8,128)(2,1)S(1)} %bitcast.85, bf16[512,2304]{1,0:T(8,128)(2,1)S(1)} %bitcast.84, bf16[512,1152]{1,0:T(8,128)(2,1)S(1)} %bitcast.94, bf16[512,1152]{1,0:T(8,128)(2,1)S(1)} %bitcast.93), custom_call_target="tpu_custom_call" | custom-call | bytes 1048576 | tf_op jit(solution)/shard_map/columns_kernel/pallas_call | solution.py:58
  251.1 8.6 %columns_kernel.3.refs_15_ = bf16[1152,4608]{1,0:T(8,128)(2,1)} custom-call(bf16[512,1152]{1,0:T(8,128)(2,1)S(1)} %bitcast.88, bf16[512,1152]{1,0:T(8,128)(2,1)S(1)} %bitcast.86, bf16[512,2304]{1,0:T(8,128)(2,1)S(1)} %bitcast.91, bf16[512,2304]{1,0:T(8,128)(2,1)S(1)} %bitcast.90, ...), custom_call_target="tpu_custom_call", output_to_operand_aliasing={{}: (4, {})} | custom-call | bytes 1048576 | tf_op jit(solution)/shard_map/columns_kernel/pallas_call | solution.py:58
  266.1 24.7 %middle_bwd_kernel.1 = (bf16[1,512,1152]{2,1,0:T(8,128)(2,1)S(1)}, bf16[1,512,1152]{2,1,0:T(8,128)(2,1)S(1)}, bf16[1,512,1152]{2,1,0:T(8,128)(2,1)S(1)}, f32[1,5...) custom-call(s32[4]{0:T(128)S(1)} %pad_add_fusion.1.refs_0_, ...), custom_call_target="tpu_custom_call" | custom-call | bytes 1048576 | tf_op jit(solution)/shard_map/middle_bwd_kernel/pallas_call | solution.py:58
  299.1 8.4 %fed_kernel.1 = (bf16[1,512,1152]{2,1,0:T(8,128)(2,1)S(1)}, bf16[1,512,1152]{2,1,0:T(8,128)(2,1)}, f32[1,1,1152]{2,1,0:T(1,128)S(1)}) custom-call(bf16[1,512,2304]{2,1,0:T(8,128)(2,1)S(1)} %copy-done.13, bf16[1,512,2304]{2,1,0:T(8,128)(2,1)S(1)} %copy-done.11, bf16[1,512,1152]{2,1,0:T(8,128)(2,1)S(1)} %copy-done.9, bf16[1,512,1152]{2,1,0:T(8,128)(2,1)S(1)} %copy-done.6, ...), custom_call_target="tpu_custom_call" | custom-call | bytes 1048576 | tf_op jit(solution)/shard_map/fed_kernel/pallas_call | solution.py:58
  307.7 5.2 collective-permute-done.18.refs_8_.refs_2_
  314.4 6.4 %wgrad_kernel.2 = (bf16[8,72,1152]{2,1,0:T(8,128)(2,1)S(1)}, bf16[8,72,1152]{2,1,0:T(8,128)(2,1)S(1)}, bf16[8,72,1152]{2,1,0:T(8,128)(2,1)S(1)}, bf16[8,72,1152]...) custom-call(s32[4]{0:T(128)S(1)} %pad_add_fusion.1.refs_0_, ...), custom_call_target="tpu_custom_call" | custom-call | bytes 1048576 | tf_op jit(solution)/shard_map/wgrad_kernel/pallas_call | solution.py:58
  327.9 3.0 core_sum_kernel.2
  332.8 30.4 %self_bwd_kernel.1.refs_0_.refs_1_ = bf16[1,1024,1728]{2,1,0:T(8,128)(2,1)} custom-call(bf16[1,1024,1728]{2,1,0:T(8,128)(2,1)} %get-tuple-element.98.refs_0_, bf16[1,256,1152]{2,1,0:T(8,128)(2,1)} %copy-done.47, bf16[1,256,1152]{2,1,0:T(8,128)(2,1)} %copy-done.35, f32[1,8,1024]{2,1,0:T(8,128)} %copy-done.51, bf16[4,72,3456]{2,1,0:T(8,128)(2,1)} %copy-done.17), custom_call_target="tpu_custom_call" | custom-call | bytes 1048576 | tf_op jit(solution)/shard_map/self_bwd_kernel/pallas_call | solution.py:58
  363.3 11.2 %input_bwd_kernel.1 = (bf16[1,512,1152]{2,1,0:T(8,128)(2,1)}, bf16[1,512,1152]{2,1,0:T(8,128)(2,1)}, f32[1,8,1152]{2,1,0:T(8,128)}, f32[1,1,1728]{2,1,0:T(1,128)}) custom-call(bf16[1,1024,1728]{2,1,0:T(8,128)(2,1)} %self_bwd_kernel.1.refs_0_.refs_1_, bf16[1,1024,1728]{2,1,0:T(8,128)(2,1)} %self_bwd_kernel.1.refs_0_.refs_1_, bf16[1,512,1152]{2,1,0:T(8,128)(2,1)} %refs_2_.5, ...), custom_call_target="tpu_custom_call" | custom-call | bytes 1048576 | tf_op jit(solution)/shard_map/input_bwd_kernel/pallas_call | solution.py:58
  378.0 8.0 %wgrad_kernel.3 = (bf16[8,72,1152]{2,1,0:T(8,128)(2,1)S(1)}, bf16[8,72,1152]{2,1,0:T(8,128)(2,1)S(1)}, bf16[8,72,576]{2,1,0:T(8,128)(2,1)S(1)}, bf16[8,72,1152]{...) custom-call(s32[4]{0:T(128)S(1)} %pad_add_fusion.1.refs_0_, ...), custom_call_target="tpu_custom_call" | custom-call | bytes 1048576 | tf_op jit(solution)/shard_map/wgrad_kernel/pallas_call | solution.py:58
  388.1 5.9 %collective-permute-done.26.refs_2_ = bf16[4,72,3456]{2,1,0:T(8,128)(2,1)} collective-permute-done((bf16[4,72,3456]{2,1,0:T(8,128)(2,1)}, bf16[4,72,3456]{2,1,0:T(8,128)(2,1)}, u32[]{:S(2)}, u32[]{:S(2)}) %collective-permute-start.26) | collective-permute-done | bytes 1990688 | tf_op jit(solution)/shard_map/ppermute | solution.py:720
  407.4 7.5 %collective-permute-done.31.refs_5_.refs_1_ = bf16[1,512,1152]{2,1,0:T(8,128)(2,1)S(1)} collective-permute-done((bf16[1,512,1152]{2,1,0:T(8,128)(2,1)S(1)}, bf16[1,512,1152]{2,1,0:T(8,128)(2,1)S(1)}, u32[]{:S(2)}, u32[]{:S(2)}) %collective-permute-start.31) | collective-permute-done | bytes 1179680 | tf_op jit(solution)/shard_map/ppermute | solution.py:754
  416.5 17.9 %collective-permute-done.28.refs_1_ = bf16[72,3456]{1,0:T(8,128)(2,1)S(1)} collective-permute-done((bf16[72,3456]{1,0:T(8,128)(2,1)S(1)}, bf16[72,3456]{1,0:T(8,128)(2,1)S(1)}, u32[]{:S(2)}, u32[]{:S(2)}) %collective-permute-start.28) | collective-permute-done | bytes 497696 | tf_op jit(solution)/shard_map/ppermute | solution.py:716
  434.3 9.9 %collective-permute-done.29.refs_2_ = bf16[72,3456]{1,0:T(8,128)(2,1)S(1)} collective-permute-done((bf16[72,3456]{1,0:T(8,128)(2,1)S(1)}, bf16[72,3456]{1,0:T(8,128)(2,1)S(1)}, u32[]{:S(2)}, u32[]{:S(2)}) %collective-permute-start.29) | collective-permute-done | bytes 497696 | tf_op jit(solution)/shard_map/ppermute | solution.py:716
  449.8 10.0 %collective-permute-done.33 = f32[1,6912]{1,0:T(1,128)S(1)} collective-permute-done((f32[1,6912]{1,0:T(1,128)S(1)}, f32[1,6912]{1,0:T(1,128)S(1)}, u32[]{:S(2)}, u32[]{:S(2)}) %collective-permute-start.33) | collective-permute-done | bytes 27680 | tf_op jit(solution)/shard_map/ppermute | solution.py:754
  473.1 2.8 last_kernel.1
  475.9 3.9 collective-permute-done.37.refs_2_
  482.5 9.1 %collective-permute-done.34.refs_1_ = bf16[72,3008]{1,0:T(8,128)(2,1)} collective-permute-done((bf16[72,3008]{1,0:T(8,128)(2,1)}, bf16[72,3008]{1,0:T(8,128)(2,1)}, u32[]{:S(2)}, u32[]{:S(2)}) %collective-permute-start.34) | collective-permute-done | bytes 433184 | tf_op jit(solution)/shard_map/ppermute | solution.py:716
  491.6 7.3 %collective-permute-done.35.refs_2_ = bf16[72,3008]{1,0:T(8,128)(2,1)} collective-permute-done((bf16[72,3008]{1,0:T(8,128)(2,1)}, bf16[72,3008]{1,0:T(8,128)(2,1)}, u32[]{:S(2)}, u32[]{:S(2)}) %collective-permute-start.35) | collective-permute-done | bytes 433184 | tf_op jit(solution)/shard_map/ppermute | solution.py:716
  504.8 9.6 %collective-permute-done.38.refs_2_ = bf16[72,3008]{1,0:T(8,128)(2,1)S(1)} collective-permute-done((bf16[72,3008]{1,0:T(8,128)(2,1)S(1)}, bf16[72,3008]{1,0:T(8,128)(2,1)S(1)}, u32[]{:S(2)}, u32[]{:S(2)}) %collective-permute-start.38) | collective-permute-done | bytes 433184 | tf_op jit(solution)/shard_map/ppermute | solution.py:754
  (321 shorter events, 139.2 us)
Async XLA Ops:
  7.2 111.1 %all-gather.3.cloned.1.call-start = ((), (), s32[]{:S(2)}) async-start(), calls=%async_computation.1 | async-start | bytes 11280384 | tf_op jit(solution)/shard_map/all_gather | solution.py:961
  9.7 195.8 %all-gather.5.cloned.1.call-start = ((), (), s32[]{:S(2)}) async-start(), calls=%async_computation.2 | async-start | bytes 11280384 | tf_op jit(solution)/shard_map/all_gather | solution.py:968
  11.6 16.6 %collective-permute-start.3 = (bf16[72,1856]{1,0:T(8,128)(2,1)}, bf16[72,1856]{1,0:T(8,128)(2,1)}, u32[]{:S(2)}, u32[]{:S(2)}) collective-permute-start(bf16[72,1856]{1,0:T(8,128)(2,1)} %fusion.4.refs_1_), channel_id=1, source_target_pairs={{0,24},{2,26},{4,28},{6,30},{8,0},{10,2},{12,4},{14,6},{16,8},{18,... | collective-permute-start | bytes 801800 | tf_op jit(solution)/shard_map/ppermute | solution.py:716
  11.6 32.6 %collective-permute-start.2 = (bf16[72,1856]{1,0:T(8,128)(2,1)}, bf16[72,1856]{1,0:T(8,128)(2,1)}, u32[]{:S(2)}, u32[]{:S(2)}) collective-permute-start(bf16[72,1856]{1,0:T(8,128)(2,1)} %fusion.4.refs_1_), channel_id=1, source_target_pairs={{0,16},{2,18},{4,20},{6,22},{8,24},{10,26},{12,28},{14,30},{16,0},... | collective-permute-start | bytes 801800 | tf_op jit(solution)/shard_map/ppermute | solution.py:716
  14.6 45.1 %collective-permute-start.1 = (bf16[72,1856]{1,0:T(8,128)(2,1)}, bf16[72,1856]{1,0:T(8,128)(2,1)}, u32[]{:S(2)}, u32[]{:S(2)}) collective-permute-start(bf16[72,1856]{1,0:T(8,128)(2,1)} %fusion.4.refs_1_), channel_id=1, source_target_pairs={{0,8},{2,10},{4,12},{6,14},{8,16},{10,18},{12,20},{14,22},{16,24},... | collective-permute-start | bytes 801800 | tf_op jit(solution)/shard_map/ppermute | solution.py:716
  18.6 42.6 %collective-permute-start = (bf16[1,512,1152]{2,1,0:T(8,128)(2,1)S(1)}, bf16[1,512,1152]{2,1,0:T(8,128)(2,1)}, u32[]{:S(2)}, u32[]{:S(2)}) collective-permute-start(bf16[1,512,1152]{2,1,0:T(8,128)(2,1)S(1)} %copy-done.1), channel_id=1, source_target_pairs={{0,1},{1,0},{2,3},{3,2},{4,5},{5,4},{6,7},{7,6},{8,9},{9,8},{10,11... | collective-permute-start | bytes 3538952 | tf_op jit(solution)/shard_map/ppermute | solution.py:754
  25.3 37.4 %collective-permute-start.4 = (bf16[72,1856]{1,0:T(8,128)(2,1)}, bf16[72,1856]{1,0:T(8,128)(2,1)S(1)}, u32[]{:S(2)}, u32[]{:S(2)}) collective-permute-start(bf16[72,1856]{1,0:T(8,128)(2,1)} %fusion.4.refs_1_), channel_id=1, source_target_pairs={{0,4},{2,6},{4,0},{6,2},{8,12},{10,14},{12,8},{14,10},{16,20},{18,... | collective-permute-start | bytes 801800 | tf_op jit(solution)/shard_map/ppermute | solution.py:720
  28.2 34.5 %collective-permute-start.7 = (bf16[72,1856]{1,0:T(8,128)(2,1)}, bf16[72,1856]{1,0:T(8,128)(2,1)S(1)}, u32[]{:S(2)}, u32[]{:S(2)}) collective-permute-start(bf16[72,1856]{1,0:T(8,128)(2,1)} %collective-permute-done.3.refs_4_), channel_id=1, source_target_pairs={{0,4},{2,6},{4,0},{6,2},{8,12},{10,14},{12,8},{14,10},{16,20},{18,... | collective-permute-start | bytes 801800 | tf_op jit(solution)/shard_map/ppermute | solution.py:720
  44.1 18.6 %collective-permute-start.6 = (bf16[72,1856]{1,0:T(8,128)(2,1)}, bf16[72,1856]{1,0:T(8,128)(2,1)S(1)}, u32[]{:S(2)}, u32[]{:S(2)}) collective-permute-start(bf16[72,1856]{1,0:T(8,128)(2,1)} %collective-permute-done.2.refs_3_), channel_id=1, source_target_pairs={{0,4},{2,6},{4,0},{6,2},{8,12},{10,14},{12,8},{14,10},{16,20},{18,... | collective-permute-start | bytes 801800 | tf_op jit(solution)/shard_map/ppermute | solution.py:720
  69.8 395.3 %reduce-scatter.2.cloned.1.call-start = ((), (), s32[]{:S(2)}) async-start(), calls=%async_computation.3 | async-start | bytes 11280384 | tf_op jit(solution)/shard_map/reduce_scatter | solution.py:1022
  69.9 28.6 %collective-permute-start.10 = (bf16[1,512,1152]{2,1,0:T(8,128)(2,1)}, bf16[1,512,1152]{2,1,0:T(8,128)(2,1)S(1)}, u32[]{:S(2)}, u32[]{:S(2)}) collective-permute-start(bf16[1,512,1152]{2,1,0:T(8,128)(2,1)} %refs_2_.3), channel_id=1, source_target_pairs={{0,1},{1,0},{2,3},{3,2},{4,5},{5,4},{6,7},{7,6},{8,9},{9,8},{10,11... | collective-permute-start | bytes 3538952 | tf_op jit(solution)/shard_map/ppermute | solution.py:754
  116.8 22.4 %collective-permute-start.11 = (bf16[1,512,576]{1,2,0:T(8,128)(2,1)S(1)}, bf16[1,512,576]{1,2,0:T(8,128)(2,1)}, u32[]{:S(2)}, u32[]{:S(2)}) collective-permute-start(bf16[1,512,576]{1,2,0:T(8,128)(2,1)S(1)} %copy.73), channel_id=1, source_target_pairs={{0,1},{1,0},{2,3},{3,2},{4,5},{5,4},{6,7},{7,6},{8,9},{9,8},{10,11... | collective-permute-start | bytes 1769480 | tf_op jit(solution)/shard_map/ppermute | solution.py:754
  120.7 15.7 %collective-permute-start.12 = (bf16[1,120,576]{2,1,0:T(8,128)(2,1)S(1)}, bf16[1,120,576]{2,1,0:T(8,128)(2,1)S(1)}, u32[]{:S(2)}, u32[]{:S(2)}) collective-permute-start(bf16[1,120,576]{2,1,0:T(8,128)(2,1)S(1)} %slice.216), channel_id=1, source_target_pairs={{0,1},{1,0},{2,3},{3,2},{4,5},{5,4},{6,7},{7,6},{8,9},{9,8},{10,11... | collective-permute-start | bytes 414728 | tf_op jit(solution)/shard_map/ppermute | solution.py:754
  121.5 16.9 %collective-permute-start.13 = (bf16[1,120,576]{2,1,0:T(8,128)(2,1)S(1)}, bf16[1,120,576]{2,1,0:T(8,128)(2,1)S(1)}, u32[]{:S(2)}, u32[]{:S(2)}) collective-permute-start(bf16[1,120,576]{2,1,0:T(8,128)(2,1)S(1)} %fusion.3), channel_id=1, source_target_pairs={{0,1},{1,0},{2,3},{3,2},{4,5},{5,4},{6,7},{7,6},{8,9},{9,8},{10,11... | collective-permute-start | bytes 414728 | tf_op jit(solution)/shard_map/ppermute | solution.py:754
  159.5 46.1 %collective-permute-start.14 = (bf16[1,512,1152]{2,1,0:T(8,128)(2,1)}, bf16[1,512,1152]{2,1,0:T(8,128)(2,1)S(1)}, u32[]{:S(2)}, u32[]{:S(2)}) collective-permute-start(bf16[1,512,1152]{2,1,0:T(8,128)(2,1)} %get-tuple-element.103.refs_0_), channel_id=1, source_target_pairs={{0,1},{1,0},{2,3},{3,2},{4,5},{5,4},{6,7},{7,6},{8,9},{9,8},{10,11... | collective-permute-start | bytes 3538952 | tf_op jit(solution)/shard_map/ppermute | solution.py:754
  222.7 28.4 %collective-permute-start.15 = (bf16[1,512,1152]{2,1,0:T(8,128)(2,1)}, bf16[1,512,1152]{2,1,0:T(8,128)(2,1)S(1)}, u32[]{:S(2)}, u32[]{:S(2)}) collective-permute-start(bf16[1,512,1152]{2,1,0:T(8,128)(2,1)} %get-tuple-element.105.refs_7_), channel_id=1, source_target_pairs={{0,1},{1,0},{2,3},{3,2},{4,5},{5,4},{6,7},{7,6},{8,9},{9,8},{10,11... | collective-permute-start | bytes 3538952 | tf_op jit(solution)/shard_map/ppermute | solution.py:754
  292.5 15.1 %collective-permute-start.17 = (bf16[1,120,1152]{2,1,0:T(8,128)(2,1)}, bf16[1,120,1152]{2,1,0:T(8,128)(2,1)S(1)}, u32[]{:S(2)}, u32[]{:S(2)}) collective-permute-start(bf16[1,120,1152]{2,1,0:T(8,128)(2,1)} %get-tuple-element.121), channel_id=1, source_target_pairs={{0,1},{1,0},{2,3},{3,2},{4,5},{5,4},{6,7},{7,6},{8,9},{9,8},{10,11... | collective-permute-start | bytes 829448 | tf_op jit(solution)/shard_map/ppermute | solution.py:754
  293.9 19.0 %collective-permute-start.18 = (bf16[1,256,1152]{2,1,0:T(8,128)(2,1)}, bf16[1,256,1152]{2,1,0:T(8,128)(2,1)S(1)}, u32[]{:S(2)}, u32[]{:S(2)}) collective-permute-start(bf16[1,256,1152]{2,1,0:T(8,128)(2,1)} %copy-done.60), channel_id=1, source_target_pairs={{0,1},{1,0},{2,3},{3,2},{4,5},{5,4},{6,7},{7,6},{8,9},{9,8},{10,11... | collective-permute-start | bytes 1769480 | tf_op jit(solution)/shard_map/ppermute | solution.py:754
  321.4 55.4 %collective-permute-start.16 = (bf16[1,512,1152]{2,1,0:T(8,128)(2,1)}, bf16[1,512,1152]{2,1,0:T(8,128)(2,1)S(1)}, u32[]{:S(2)}, u32[]{:S(2)}) collective-permute-start(bf16[1,512,1152]{2,1,0:T(8,128)(2,1)} %get-tuple-element.119), channel_id=1, source_target_pairs={{0,1},{1,0},{2,3},{3,2},{4,5},{5,4},{6,7},{7,6},{8,9},{9,8},{10,11... | collective-permute-start | bytes 3538952 | tf_op jit(solution)/shard_map/ppermute | solution.py:754
  332.2 61.9 %collective-permute-start.26 = (bf16[4,72,3456]{2,1,0:T(8,128)(2,1)}, bf16[4,72,3456]{2,1,0:T(8,128)(2,1)}, u32[]{:S(2)}, u32[]{:S(2)}) collective-permute-start(bf16[4,72,3456]{2,1,0:T(8,128)(2,1)} %get-tuple-element.152), channel_id=1, source_target_pairs={{0,4},{2,6},{4,0},{6,2},{8,12},{10,14},{12,8},{14,10},{16,20},{18,... | collective-permute-start | bytes 5971976 | tf_op jit(solution)/shard_map/ppermute | solution.py:720
  386.6 28.3 %collective-permute-start.31 = (bf16[1,512,1152]{2,1,0:T(8,128)(2,1)S(1)}, bf16[1,512,1152]{2,1,0:T(8,128)(2,1)S(1)}, u32[]{:S(2)}, u32[]{:S(2)}) collective-permute-start(bf16[1,512,1152]{2,1,0:T(8,128)(2,1)S(1)} %copy-done.76), channel_id=1, source_target_pairs={{0,1},{1,0},{2,3},{3,2},{4,5},{5,4},{6,7},{7,6},{8,9},{9,8},{10,11... | collective-permute-start | bytes 3538952 | tf_op jit(solution)/shard_map/ppermute | solution.py:754
  398.3 61.6 %collective-permute-start.27 = (bf16[4,72,3008]{2,1,0:T(8,128)(2,1)S(1)}, bf16[4,72,3008]{2,1,0:T(8,128)(2,1)S(1)}, u32[]{:S(2)}, u32[]{:S(2)}) collective-permute-start(bf16[4,72,3008]{2,1,0:T(8,128)(2,1)S(1)} %get-tuple-element.155), channel_id=1, source_target_pairs={{0,4},{2,6},{4,0},{6,2},{8,12},{10,14},{12,8},{14,10},{16,20},{18,... | collective-permute-start | bytes 5197832 | tf_op jit(solution)/shard_map/ppermute | solution.py:720
  398.9 35.4 %collective-permute-start.28 = (bf16[72,3456]{1,0:T(8,128)(2,1)S(1)}, bf16[72,3456]{1,0:T(8,128)(2,1)S(1)}, u32[]{:S(2)}, u32[]{:S(2)}) collective-permute-start(bf16[72,3456]{1,0:T(8,128)(2,1)S(1)} %get-tuple-element.156), channel_id=1, source_target_pairs={{0,8},{2,10},{4,12},{6,14},{8,16},{10,18},{12,20},{14,22},{16,24},... | collective-permute-start | bytes 1493000 | tf_op jit(solution)/shard_map/ppermute | solution.py:716
  401.3 43.0 %collective-permute-start.29 = (bf16[72,3456]{1,0:T(8,128)(2,1)S(1)}, bf16[72,3456]{1,0:T(8,128)(2,1)S(1)}, u32[]{:S(2)}, u32[]{:S(2)}) collective-permute-start(bf16[72,3456]{1,0:T(8,128)(2,1)S(1)} %get-tuple-element.157), channel_id=1, source_target_pairs={{0,16},{2,18},{4,20},{6,22},{8,24},{10,26},{12,28},{14,30},{16,0},... | collective-permute-start | bytes 1493000 | tf_op jit(solution)/shard_map/ppermute | solution.py:716
  403.6 42.7 %collective-permute-start.30 = (bf16[72,3456]{1,0:T(8,128)(2,1)S(1)}, bf16[72,3456]{1,0:T(8,128)(2,1)S(1)}, u32[]{:S(2)}, u32[]{:S(2)}) collective-permute-start(bf16[72,3456]{1,0:T(8,128)(2,1)S(1)} %get-tuple-element.158), channel_id=1, source_target_pairs={{0,24},{2,26},{4,28},{6,30},{8,0},{10,2},{12,4},{14,6},{16,8},{18,... | collective-permute-start | bytes 1493000 | tf_op jit(solution)/shard_map/ppermute | solution.py:716
  415.0 33.8 %collective-permute-start.32 = (bf16[1,60,1152]{2,1,0:T(8,128)(2,1)S(1)}, bf16[1,60,1152]{2,1,0:T(8,128)(2,1)S(1)}, u32[]{:S(2)}, u32[]{:S(2)}) collective-permute-start(bf16[1,60,1152]{2,1,0:T(8,128)(2,1)S(1)} %select_convert_fusion), channel_id=1, source_target_pairs={{0,1},{1,0},{2,3},{3,2},{4,5},{5,4},{6,7},{7,6},{8,9},{9,8},{10,11... | collective-permute-start | bytes 414728 | tf_op jit(solution)/shard_map/ppermute | solution.py:754
  446.6 20.0 %collective-permute-start.39 = (bf16[72,3456]{1,0:T(8,128)(2,1)S(1)}, bf16[72,3456]{1,0:T(8,128)(2,1)}, u32[]{:S(2)}, u32[]{:S(2)}) collective-permute-start(bf16[72,3456]{1,0:T(8,128)(2,1)S(1)} %z_sum_kernel.2.refs_3_), channel_id=1, source_target_pairs={{0,1},{1,0},{2,3},{3,2},{4,5},{5,4},{6,7},{7,6},{8,9},{9,8},{10,11... | collective-permute-start | bytes 1493000 | tf_op jit(solution)/shard_map/ppermute | solution.py:754
  461.7 29.9 %collective-permute-start.34 = (bf16[72,3008]{1,0:T(8,128)(2,1)}, bf16[72,3008]{1,0:T(8,128)(2,1)}, u32[]{:S(2)}, u32[]{:S(2)}) collective-permute-start(bf16[72,3008]{1,0:T(8,128)(2,1)} %get-tuple-element.165), channel_id=1, source_target_pairs={{0,8},{2,10},{4,12},{6,14},{8,16},{10,18},{12,20},{14,22},{16,24},... | collective-permute-start | bytes 1299464 | tf_op jit(solution)/shard_map/ppermute | solution.py:716
  461.7 37.2 %collective-permute-start.35 = (bf16[72,3008]{1,0:T(8,128)(2,1)}, bf16[72,3008]{1,0:T(8,128)(2,1)}, u32[]{:S(2)}, u32[]{:S(2)}) collective-permute-start(bf16[72,3008]{1,0:T(8,128)(2,1)} %get-tuple-element.166), channel_id=1, source_target_pairs={{0,16},{2,18},{4,20},{6,22},{8,24},{10,26},{12,28},{14,30},{16,0},... | collective-permute-start | bytes 1299464 | tf_op jit(solution)/shard_map/ppermute | solution.py:716
  463.1 37.7 %collective-permute-start.36 = (bf16[72,3008]{1,0:T(8,128)(2,1)}, bf16[72,3008]{1,0:T(8,128)(2,1)}, u32[]{:S(2)}, u32[]{:S(2)}) collective-permute-start(bf16[72,3008]{1,0:T(8,128)(2,1)} %get-tuple-element.167), channel_id=1, source_target_pairs={{0,24},{2,26},{4,28},{6,30},{8,0},{10,2},{12,4},{14,6},{16,8},{18,... | collective-permute-start | bytes 1299464 | tf_op jit(solution)/shard_map/ppermute | solution.py:716
  465.1 14.8 %collective-permute-start.37 = (bf16[72,4608]{1,0:T(8,128)(2,1)}, bf16[72,4608]{1,0:T(8,128)(2,1)S(1)}, u32[]{:S(2)}, u32[]{:S(2)}) collective-permute-start(bf16[72,4608]{1,0:T(8,128)(2,1)} %reduce-scatter.2.cloned.1.call-done.refs_1_), channel_id=1, source_target_pairs={{0,1},{1,0},{2,3},{3,2},{4,5},{5,4},{6,7},{7,6},{8,9},{9,8},{10,11... | collective-permute-start | bytes 1990664 | tf_op jit(solution)/shard_map/ppermute | solution.py:754
  502.3 12.2 %collective-permute-start.38 = (bf16[72,3008]{1,0:T(8,128)(2,1)S(1)}, bf16[72,3008]{1,0:T(8,128)(2,1)S(1)}, u32[]{:S(2)}, u32[]{:S(2)}) collective-permute-start(bf16[72,3008]{1,0:T(8,128)(2,1)S(1)} %z_sum_kernel.3.refs_1_), channel_id=1, source_target_pairs={{0,1},{1,0},{2,3},{3,2},{4,5},{5,4},{6,7},{7,6},{8,9},{9,8},{10,11... | collective-permute-start | bytes 1299464 | tf_op jit(solution)/shard_map/ppermute | solution.py:754
  (91 other events, 833.5 us)
Sparse Core Ops, SparseCore 0:
  10.9 104.6 all-gather.2
  118.5 87.0 all-gather.4
  260.8 134.9 reduce-scatter.1

commit v4 on v3

--- a/solution.py
+++ b/solution.py
@@ -625,7 +625,7 @@
     )
 
 
-def last_out_kernel(pos_ref, x_ref, got_ref, kv_ref, in_ref, vec_ref):
+def last_out_kernel(pos_ref, x_ref, got_ref, kv_ref, in_ref, table_ref, expand_ref, *vec_refs):
     first = pos_ref[0] == 0
     own = kv_ref.shape[1] // 4
     for p in range(5):
@@ -633,18 +633,22 @@
         ref, at = (kv_ref, p) if p < 2 else (in_ref, p - 2)
         ref[:, 2 * at * own : (2 * at + 1) * own] = jnp.where(first, x, got)
         ref[:, (2 * at + 1) * own : (2 * at + 2) * own] = jnp.where(first, got, x)
-    vec_ref[...] = x_ref[:, 5 * own :].astype(F32) + got_ref[:, 5 * own :].astype(F32)
-
-
-def last_outputs(pos, x, own):
+    vectors = (x_ref[:, 5 * own :].astype(F32) + got_ref[:, 5 * own :].astype(F32)).T
+    for i, ref in enumerate(vec_refs):
+        ref[...] = vectors[i : i + 1]
+    table_ref[...] = vectors[7:13]
+    expand_ref[...] = vectors[13 : 13 + expand_ref.shape[0]]
+
+
+def last_outputs(pos, x, own, expands):
     vmem = pl.BlockSpec(memory_space=pltpu.VMEM)
     r = x.shape[0]
     return call(
         last_out_kernel,
         (pos, x, swap(x)),
         [smem()] + [vmem] * 2,
-        [((r, 4 * own), F32), ((r, 6 * own), F32), ((r, 128), F32)],
-        [vmem] * 3,
+        [((r, 4 * own), F32), ((r, 6 * own), F32), ((6, r), F32), ((expands, r), F32)] + [((1, r), F32)] * 7,
+        [vmem] * 11,
         vmem=16 << 20,
     )
 
@@ -1105,7 +1109,11 @@
     input_core = sum_core(
         pos, input_own + [vector_parts[0]], input_other + [vector_parts[1]], nf, waits=(outer_y[0],)
     )
-    outer_own = sum_z(outer_y, nf, waits=(input_core[0], norm_a_terms[1]))
+    embed_part = jnp.stack(
+        [shift_a_grad, scale_a_grad, gate_a_grad, shift_b_grad, scale_b_grad, gate_b_grad], axis=1
+    )
+    time_grad = sum_sp(embed_part.reshape(latents, 6 * width), nsp)
+    outer_own = sum_z(outer_y, nf, waits=(input_core[0], norm_a_terms[1], time_grad))
     input_y = sum_y(pos, *input_core, nf, waits=(outer_own,))
     latent_grad, *tokens = last_backward(*norm_a_terms, latent_tokens, mods, attn_stream_grad, (input_y[0],))
     block_out, token = finish_forward(*fed_terms, after_cross, mods, vecs, waits=(input_y[0],))
@@ -1126,24 +1134,20 @@
         expand_out = jnp.stack(
             [g.reshape(rows, parts, nf, block).transpose(0, 2, 1, 3) for g in expand_sp], axis=2
         ).reshape(rows, -1)
-    embed_part = jnp.stack(
-        [shift_a_grad, scale_a_grad, gate_a_grad, shift_b_grad, scale_b_grad, gate_b_grad], axis=1
-    )
-    time_grad = sum_sp(embed_part.reshape(latents, 6 * width), nsp)
     outer_sum = sum_sp(outer_own, nsp)
     xquery_out, xoutput_out, output_out = [outer_sum[:, i * width : (i + 1) * width] for i in range(3)]
-    input_own = sum_z(input_y, nf, waits=(*tokens, time_grad))
+    input_own = sum_z(input_y, nf, waits=tuple(tokens))
     if nsp == 2:
-        keyval_out, input_wout, owned = last_outputs(pos, input_own, own)
+        keyval_out, input_wout, table_out, expand_bout, *owned = last_outputs(pos, input_own, own, count - 13)
+        owned = [x.reshape(rows) for x in owned]
+        expand_bout = expand_bout.reshape(hidden_rows)
     else:
         inputs = list(lax.all_gather(input_own[:, : 5 * own], "sp").astype(F32))
         keyval_out = jnp.concatenate([g[:, p * own : (p + 1) * own] for p in range(2) for g in inputs], axis=1)
         input_wout = jnp.concatenate([g[:, p * own : (p + 1) * own] for p in range(2, 5) for g in inputs], axis=1)
-        owned = sum_sp(input_own[:, 5 * own :], nsp)
-    owned = owned[:, :count].T
-    expand_bout = owned[13:count].reshape(hidden_rows)
-
-    table_out = owned[7:13]
+        owned = sum_sp(input_own[:, 5 * own :], nsp)[:, :count].T
+        expand_bout = owned[13:count].reshape(hidden_rows)
+        table_out = owned[7:13]
     return (
         block_out,
         latent_grad,

time: 533 us -> 524 us (0.983)
  waiting for transfers between devices: 193 us -> 186 us
    ppermute x9, waiting for transfers between devices: 77.3 us -> 67.1 us  [shift_z(): return lax.ppermute(x, 'fsdp', [(i, (i + 4 * d) % nf) for i in range(nf)])]
    unnamed x165 -> x164, local copies, waits for them, and re-layouts: 34.2 us -> 33.6 us
  transfers between devices with their start and end apart: 43 -> 43, of which waited for: 23 -> 23; matrix products, arithmetic and copies ran while one was open for 6% -> 6% of each run, Pallas kernels for 33% -> 34%
where the time goes in v4:
time: 524 us; the launch traced here: 517 us
  Pallas kernels  203 us (39%)
  waiting for transfers between devices  186 us (35%)
  local copies, waits for them, and re-layouts  49.8 us (10%)
  starting transfers between devices  44.6 us (9%)
  between operations  15.8 us (3%)
  other arithmetic  12.8 us (2%)
    pallas_call x26, Pallas kernels, call(): pl.pallas_call(body, name=(kernel.func if isinstance(kernel, partial) els...  203 us
    ppermute x9, waiting for transfers between devices, shift_z(): return lax.ppermute(x, 'fsdp', [(i, (i + 4 * d) % nf) for i in range(nf)])  67.1 us
    ppermute x17, waiting for transfers between devices, swap(): return lax.ppermute(x, 'sp', [(0, 1), (1, 0)])  59.4 us
    all_gather x1, waiting for transfers between devices, on_device(): whole_expand = lax.all_gather(after(last, mine), 'fsdp', axis=0, tiled=True)  43.3 us
    unnamed x164, local copies, waits for them, and re-layouts  33.6 us
    ppermute x17, starting transfers between devices, swap(): return lax.ppermute(x, 'sp', [(0, 1), (1, 0)])  20.1 us
    ppermute x9, starting transfers between devices, shift_z(): return lax.ppermute(x, 'fsdp', [(i, (i + 4 * d) % nf) for i in range(nf)])  16.1 us
    ppermute x6, waiting for transfers between devices, cross_y(): return lax.ppermute(x, 'fsdp', [(i, i ^ 2) for i in range(nf)])  10.7 us
  transfers between devices with their start and end apart: 43, of which 23 were waited for; matrix products, arithmetic and copies ran while one was open for 6% of the time, Pallas kernels for 34%

profile of v4, /device:TPU:8, one launch (start us, length us, event | category | flops | bytes accessed | tf_op | source)
XLA Modules:
  0.0 516.9 jit_solution(11228750925528679188)
XLA Ops:
  11.6 3.0 collective-permute-start.2
  28.7 15.4 %collective-permute-done.2.refs_3_ = bf16[72,1856]{1,0:T(8,128)(2,1)} collective-permute-done((bf16[72,1856]{1,0:T(8,128)(2,1)}, bf16[72,1856]{1,0:T(8,128)(2,1)}, u32[]{:S(2)}, u32[]{:S(2)}) %collective-permute-start.2) | collective-permute-done | bytes 267296 | tf_op jit(solution)/shard_map/ppermute | solution.py:720
  45.9 13.8 %collective-permute-done.1.refs_2_ = bf16[72,1856]{1,0:T(8,128)(2,1)} collective-permute-done((bf16[72,1856]{1,0:T(8,128)(2,1)}, bf16[72,1856]{1,0:T(8,128)(2,1)}, u32[]{:S(2)}, u32[]{:S(2)}) %collective-permute-start.1) | collective-permute-done | bytes 267296 | tf_op jit(solution)/shard_map/ppermute | solution.py:720
  62.7 3.7 collective-permute-done.5.refs_6_
  83.1 10.3 %qkv_kernel.1 = (bf16[1,1024,1152]{2,1,0:T(8,128)(2,1)}, bf16[1,1024,1728]{2,1,0:T(8,128)(2,1)}) custom-call(bf16[1,1024,1152]{2,1,0:T(8,128)(2,1)} %copy-done.3, f32[1,8,1152]{2,1,0:T(8,128)} %pad.9.refs_1_.refs_2_.refs_5_.refs_3_, f32[1,1728]{1,0:T(1,128)} %reshape.398.refs_2_, bf16[1152,1856]{1,0:T(8,128)(2,1)} %bitcast.86), custom_call_target="tpu_custom_call" | custom-call | bytes 1048576 | tf_op jit(solution)/shard_map/qkv_kernel/pallas_call | solution.py:58
  93.5 5.1 collective-permute-done.10.refs_1_.refs_3_
  101.0 15.0 %self_fwd_kernel.1 = (bf16[1,1024,576]{2,1,0:T(8,128)(2,1)S(1)}, f32[1,8,1024]{2,1,0:T(8,128)S(1)}) custom-call(bf16[1,1024,1728]{2,1,0:T(8,128)(2,1)S(1)} %copy-done.4, bf16[1,512,1152]{2,1,0:T(8,128)(2,1)S(1)} %collective-permute-done.10.refs_1_.refs_3_), custom_call_target="tpu_custom_call" | custom-call | bytes 1048576 | tf_op jit(solution)/shard_map/self_fwd_kernel/pallas_call | solution.py:58
  123.1 13.4 %collective-permute-done.12 = bf16[1,120,576]{2,1,0:T(8,128)(2,1)S(1)} collective-permute-done((bf16[1,120,576]{2,1,0:T(8,128)(2,1)S(1)}, bf16[1,120,576]{2,1,0:T(8,128)(2,1)S(1)}, u32[]{:S(2)}, u32[]{:S(2)}) %collective-permute-start.12) | collective-permute-done | bytes 138272 | tf_op jit(solution)/shard_map/ppermute | solution.py:758
  142.5 17.1 %middle_fwd_kernel.1 = (bf16[1,512,1152]{2,1,0:T(8,128)(2,1)}, bf16[1,512,1152]{2,1,0:T(8,128)(2,1)}, bf16[1,512,1152]{2,1,0:T(8,128)(2,1)}, f32[1,16,512]{2,1,0...) custom-call(bf16[1,512,1152]{2,1,0:T(8,128)(2,1)} %maximum_select_fusion.refs_0_, ...), custom_call_target="tpu_custom_call" | custom-call | bytes 1048576 | tf_op jit(solution)/shard_map/middle_fwd_kernel/pallas_call | solution.py:58
  162.3 43.3 %all-gather.5.cloned.1.call-done.refs_3_.refs_4_.refs_5_ = bf16[1152,4608]{1,0:T(8,128)(2,1)} async-done(((bf16[72,4608]{1,0:T(8,128)(2,1)}), bf16[1152,4608]{1,0:T(8,128)(2,1)}) %all-gather.5.cloned.1.call-update) | async-done | bytes 10616848 | tf_op jit(solution)/shard_map/all_gather | solution.py:972
  206.4 16.3 %ff_kernel.2 = (bf16[1,512,2304]{2,1,0:T(8,128)(2,1)S(1)}, bf16[1,512,2304]{2,1,0:T(8,128)(2,1)S(1)}, bf16[1,512,1152]{2,1,0:T(8,128)(2,1)S(1)}, bf16[1,512,1152...) custom-call(bf16[1,512,1152]{2,1,0:T(8,128)(2,1)S(1)} %collective-permute-done.14.refs_0_, ...), custom_call_target="tpu_custom_call" | custom-call | bytes 1048576 | tf_op jit(solution)/shard_map/ff_kernel/pallas_call | solution.py:58
  224.2 15.3 %ff_kernel.3 = (bf16[1,512,2304]{2,1,0:T(8,128)(2,1)S(1)}, bf16[1,512,2304]{2,1,0:T(8,128)(2,1)}, bf16[1,512,1152]{2,1,0:T(8,128)(2,1)S(1)}, bf16[1,512,1152]{2,...) custom-call(bf16[1,512,1152]{2,1,0:T(8,128)(2,1)S(1)} %copy-done.28, ...), custom_call_target="tpu_custom_call" | custom-call | bytes 1048576 | tf_op jit(solution)/shard_map/ff_kernel/pallas_call | solution.py:58
  240.6 8.5 %columns_kernel.2.refs_4_ = bf16[1152,4608]{1,0:T(8,128)(2,1)} custom-call(bf16[512,2304]{1,0:T(8,128)(2,1)S(1)} %bitcast.90, bf16[512,2304]{1,0:T(8,128)(2,1)S(1)} %bitcast.89, bf16[512,1152]{1,0:T(8,128)(2,1)S(1)} %bitcast.99, bf16[512,1152]{1,0:T(8,128)(2,1)S(1)} %bitcast.98), custom_call_target="tpu_custom_call" | custom-call | bytes 1048576 | tf_op jit(solution)/shard_map/columns_kernel/pallas_call | solution.py:58
  251.1 8.6 %columns_kernel.3.refs_15_ = bf16[1152,4608]{1,0:T(8,128)(2,1)} custom-call(bf16[512,1152]{1,0:T(8,128)(2,1)S(1)} %bitcast.93, bf16[512,1152]{1,0:T(8,128)(2,1)S(1)} %bitcast.91, bf16[512,2304]{1,0:T(8,128)(2,1)S(1)} %bitcast.96, bf16[512,2304]{1,0:T(8,128)(2,1)S(1)} %bitcast.95, ...), custom_call_target="tpu_custom_call", output_to_operand_aliasing={{}: (4, {})} | custom-call | bytes 1048576 | tf_op jit(solution)/shard_map/columns_kernel/pallas_call | solution.py:58
  266.1 24.7 %middle_bwd_kernel.1 = (bf16[1,512,1152]{2,1,0:T(8,128)(2,1)S(1)}, bf16[1,512,1152]{2,1,0:T(8,128)(2,1)S(1)}, bf16[1,512,1152]{2,1,0:T(8,128)(2,1)S(1)}, f32[1,5...) custom-call(s32[4]{0:T(128)S(1)} %pad_add_fusion.1.refs_0_, ...), custom_call_target="tpu_custom_call" | custom-call | bytes 1048576 | tf_op jit(solution)/shard_map/middle_bwd_kernel/pallas_call | solution.py:58
  299.1 8.4 %fed_kernel.1 = (bf16[1,512,1152]{2,1,0:T(8,128)(2,1)S(1)}, bf16[1,512,1152]{2,1,0:T(8,128)(2,1)}, f32[1,1,1152]{2,1,0:T(1,128)S(1)}) custom-call(bf16[1,512,2304]{2,1,0:T(8,128)(2,1)S(1)} %copy-done.13, bf16[1,512,2304]{2,1,0:T(8,128)(2,1)S(1)} %copy-done.11, bf16[1,512,1152]{2,1,0:T(8,128)(2,1)S(1)} %copy-done.9, bf16[1,512,1152]{2,1,0:T(8,128)(2,1)S(1)} %copy-done.6, ...), custom_call_target="tpu_custom_call" | custom-call | bytes 1048576 | tf_op jit(solution)/shard_map/fed_kernel/pallas_call | solution.py:58
  307.6 5.3 %collective-permute-done.18.refs_8_.refs_2_ = bf16[1,256,1152]{2,1,0:T(8,128)(2,1)S(1)} collective-permute-done((bf16[1,256,1152]{2,1,0:T(8,128)(2,1)}, bf16[1,256,1152]{2,1,0:T(8,128)(2,1)S(1)}, u32[]{:S(2)}, u32[]{:S(2)}) %collective-permute-start.18) | collective-permute-done | bytes 589856 | tf_op jit(solution)/shard_map/ppermute | solution.py:758
  314.4 6.4 %wgrad_kernel.2 = (bf16[8,72,1152]{2,1,0:T(8,128)(2,1)S(1)}, bf16[8,72,1152]{2,1,0:T(8,128)(2,1)S(1)}, bf16[8,72,1152]{2,1,0:T(8,128)(2,1)S(1)}, bf16[8,72,1152]...) custom-call(s32[4]{0:T(128)S(1)} %pad_add_fusion.1.refs_0_, ...), custom_call_target="tpu_custom_call" | custom-call | bytes 1048576 | tf_op jit(solution)/shard_map/wgrad_kernel/pallas_call | solution.py:58
  327.9 3.0 core_sum_kernel.2
  332.9 30.4 %self_bwd_kernel.1.refs_0_.refs_1_ = bf16[1,1024,1728]{2,1,0:T(8,128)(2,1)} custom-call(bf16[1,1024,1728]{2,1,0:T(8,128)(2,1)} %get-tuple-element.106.refs_0_, bf16[1,256,1152]{2,1,0:T(8,128)(2,1)} %copy-done.47, bf16[1,256,1152]{2,1,0:T(8,128)(2,1)} %copy-done.35, f32[1,8,1024]{2,1,0:T(8,128)} %copy-done.51, bf16[4,72,3456]{2,1,0:T(8,128)(2,1)} %copy-done.17), custom_call_target="tpu_custom_call" | custom-call | bytes 1048576 | tf_op jit(solution)/shard_map/self_bwd_kernel/pallas_call | solution.py:58
  363.3 11.2 %input_bwd_kernel.1 = (bf16[1,512,1152]{2,1,0:T(8,128)(2,1)}, bf16[1,512,1152]{2,1,0:T(8,128)(2,1)}, f32[1,8,1152]{2,1,0:T(8,128)}, f32[1,1,1728]{2,1,0:T(1,128)}) custom-call(bf16[1,1024,1728]{2,1,0:T(8,128)(2,1)} %self_bwd_kernel.1.refs_0_.refs_1_, bf16[1,1024,1728]{2,1,0:T(8,128)(2,1)} %self_bwd_kernel.1.refs_0_.refs_1_, bf16[1,512,1152]{2,1,0:T(8,128)(2,1)} %refs_2_.5, ...), custom_call_target="tpu_custom_call" | custom-call | bytes 1048576 | tf_op jit(solution)/shard_map/input_bwd_kernel/pallas_call | solution.py:58
  378.0 8.0 %wgrad_kernel.3 = (bf16[8,72,1152]{2,1,0:T(8,128)(2,1)S(1)}, bf16[8,72,1152]{2,1,0:T(8,128)(2,1)S(1)}, bf16[8,72,576]{2,1,0:T(8,128)(2,1)S(1)}, bf16[8,72,1152]{...) custom-call(s32[4]{0:T(128)S(1)} %pad_add_fusion.1.refs_0_, ...), custom_call_target="tpu_custom_call" | custom-call | bytes 1048576 | tf_op jit(solution)/shard_map/wgrad_kernel/pallas_call | solution.py:58
  387.1 6.9 %collective-permute-done.26.refs_2_ = bf16[4,72,3456]{2,1,0:T(8,128)(2,1)} collective-permute-done((bf16[4,72,3456]{2,1,0:T(8,128)(2,1)}, bf16[4,72,3456]{2,1,0:T(8,128)(2,1)}, u32[]{:S(2)}, u32[]{:S(2)}) %collective-permute-start.26) | collective-permute-done | bytes 1990688 | tf_op jit(solution)/shard_map/ppermute | solution.py:724
  409.3 13.0 %collective-permute-done.32 = f32[1,6912]{1,0:T(1,128)S(1)} collective-permute-done((f32[1,6912]{1,0:T(1,128)S(1)}, f32[1,6912]{1,0:T(1,128)S(1)}, u32[]{:S(2)}, u32[]{:S(2)}) %collective-permute-start.32) | collective-permute-done | bytes 27680 | tf_op jit(solution)/shard_map/ppermute | solution.py:758
  426.4 13.8 %collective-permute-done.28.refs_1_ = bf16[72,3456]{1,0:T(8,128)(2,1)S(1)} collective-permute-done((bf16[72,3456]{1,0:T(8,128)(2,1)S(1)}, bf16[72,3456]{1,0:T(8,128)(2,1)S(1)}, u32[]{:S(2)}, u32[]{:S(2)}) %collective-permute-start.28) | collective-permute-done | bytes 497696 | tf_op jit(solution)/shard_map/ppermute | solution.py:720
  440.1 8.7 %collective-permute-done.29.refs_2_ = bf16[72,3456]{1,0:T(8,128)(2,1)S(1)} collective-permute-done((bf16[72,3456]{1,0:T(8,128)(2,1)S(1)}, bf16[72,3456]{1,0:T(8,128)(2,1)S(1)}, u32[]{:S(2)}, u32[]{:S(2)}) %collective-permute-start.29) | collective-permute-done | bytes 497696 | tf_op jit(solution)/shard_map/ppermute | solution.py:720
  459.5 6.2 %collective-permute-done.39 = bf16[72,3456]{1,0:T(8,128)(2,1)} collective-permute-done((bf16[72,3456]{1,0:T(8,128)(2,1)S(1)}, bf16[72,3456]{1,0:T(8,128)(2,1)}, u32[]{:S(2)}, u32[]{:S(2)}) %collective-permute-start.39) | collective-permute-done | bytes 497696 | tf_op jit(solution)/shard_map/ppermute | solution.py:758
  472.2 2.8 last_kernel.1
  475.0 2.9 collective-permute-done.37.refs_2_
  480.5 4.7 collective-permute-done.34.refs_1_
  485.2 7.7 %collective-permute-done.35.refs_2_ = bf16[72,3008]{1,0:T(8,128)(2,1)} collective-permute-done((bf16[72,3008]{1,0:T(8,128)(2,1)}, bf16[72,3008]{1,0:T(8,128)(2,1)}, u32[]{:S(2)}, u32[]{:S(2)}) %collective-permute-start.35) | collective-permute-done | bytes 433184 | tf_op jit(solution)/shard_map/ppermute | solution.py:720
  497.0 10.6 %collective-permute-done.38.refs_2_ = bf16[72,3008]{1,0:T(8,128)(2,1)S(1)} collective-permute-done((bf16[72,3008]{1,0:T(8,128)(2,1)S(1)}, bf16[72,3008]{1,0:T(8,128)(2,1)S(1)}, u32[]{:S(2)}, u32[]{:S(2)}) %collective-permute-start.38) | collective-permute-done | bytes 433184 | tf_op jit(solution)/shard_map/ppermute | solution.py:758
  (315 shorter events, 137.6 us)
Async XLA Ops:
  7.2 111.2 %all-gather.3.cloned.1.call-start = ((), (), s32[]{:S(2)}) async-start(), calls=%async_computation.1 | async-start | bytes 11280384 | tf_op jit(solution)/shard_map/all_gather | solution.py:965
  9.7 195.8 %all-gather.5.cloned.1.call-start = ((), (), s32[]{:S(2)}) async-start(), calls=%async_computation.2 | async-start | bytes 11280384 | tf_op jit(solution)/shard_map/all_gather | solution.py:972
  11.6 16.6 %collective-permute-start.3 = (bf16[72,1856]{1,0:T(8,128)(2,1)}, bf16[72,1856]{1,0:T(8,128)(2,1)}, u32[]{:S(2)}, u32[]{:S(2)}) collective-permute-start(bf16[72,1856]{1,0:T(8,128)(2,1)} %fusion.4.refs_1_), channel_id=1, source_target_pairs={{0,24},{2,26},{4,28},{6,30},{8,0},{10,2},{12,4},{14,6},{16,8},{18,... | collective-permute-start | bytes 801800 | tf_op jit(solution)/shard_map/ppermute | solution.py:720
  11.6 32.6 %collective-permute-start.2 = (bf16[72,1856]{1,0:T(8,128)(2,1)}, bf16[72,1856]{1,0:T(8,128)(2,1)}, u32[]{:S(2)}, u32[]{:S(2)}) collective-permute-start(bf16[72,1856]{1,0:T(8,128)(2,1)} %fusion.4.refs_1_), channel_id=1, source_target_pairs={{0,16},{2,18},{4,20},{6,22},{8,24},{10,26},{12,28},{14,30},{16,0},... | collective-permute-start | bytes 801800 | tf_op jit(solution)/shard_map/ppermute | solution.py:720
  14.6 45.1 %collective-permute-start.1 = (bf16[72,1856]{1,0:T(8,128)(2,1)}, bf16[72,1856]{1,0:T(8,128)(2,1)}, u32[]{:S(2)}, u32[]{:S(2)}) collective-permute-start(bf16[72,1856]{1,0:T(8,128)(2,1)} %fusion.4.refs_1_), channel_id=1, source_target_pairs={{0,8},{2,10},{4,12},{6,14},{8,16},{10,18},{12,20},{14,22},{16,24},... | collective-permute-start | bytes 801800 | tf_op jit(solution)/shard_map/ppermute | solution.py:720
  18.6 42.6 %collective-permute-start = (bf16[1,512,1152]{2,1,0:T(8,128)(2,1)S(1)}, bf16[1,512,1152]{2,1,0:T(8,128)(2,1)}, u32[]{:S(2)}, u32[]{:S(2)}) collective-permute-start(bf16[1,512,1152]{2,1,0:T(8,128)(2,1)S(1)} %copy-done.1), channel_id=1, source_target_pairs={{0,1},{1,0},{2,3},{3,2},{4,5},{5,4},{6,7},{7,6},{8,9},{9,8},{10,11... | collective-permute-start | bytes 3538952 | tf_op jit(solution)/shard_map/ppermute | solution.py:758
  25.3 37.4 %collective-permute-start.4 = (bf16[72,1856]{1,0:T(8,128)(2,1)}, bf16[72,1856]{1,0:T(8,128)(2,1)S(1)}, u32[]{:S(2)}, u32[]{:S(2)}) collective-permute-start(bf16[72,1856]{1,0:T(8,128)(2,1)} %fusion.4.refs_1_), channel_id=1, source_target_pairs={{0,4},{2,6},{4,0},{6,2},{8,12},{10,14},{12,8},{14,10},{16,20},{18,... | collective-permute-start | bytes 801800 | tf_op jit(solution)/shard_map/ppermute | solution.py:724
  28.2 34.5 %collective-permute-start.7 = (bf16[72,1856]{1,0:T(8,128)(2,1)}, bf16[72,1856]{1,0:T(8,128)(2,1)S(1)}, u32[]{:S(2)}, u32[]{:S(2)}) collective-permute-start(bf16[72,1856]{1,0:T(8,128)(2,1)} %collective-permute-done.3.refs_4_), channel_id=1, source_target_pairs={{0,4},{2,6},{4,0},{6,2},{8,12},{10,14},{12,8},{14,10},{16,20},{18,... | collective-permute-start | bytes 801800 | tf_op jit(solution)/shard_map/ppermute | solution.py:724
  44.1 18.6 %collective-permute-start.6 = (bf16[72,1856]{1,0:T(8,128)(2,1)}, bf16[72,1856]{1,0:T(8,128)(2,1)S(1)}, u32[]{:S(2)}, u32[]{:S(2)}) collective-permute-start(bf16[72,1856]{1,0:T(8,128)(2,1)} %collective-permute-done.2.refs_3_), channel_id=1, source_target_pairs={{0,4},{2,6},{4,0},{6,2},{8,12},{10,14},{12,8},{14,10},{16,20},{18,... | collective-permute-start | bytes 801800 | tf_op jit(solution)/shard_map/ppermute | solution.py:724
  69.9 389.0 %reduce-scatter.2.cloned.1.call-start = ((), (), s32[]{:S(2)}) async-start(), calls=%async_computation.3 | async-start | bytes 11280384 | tf_op jit(solution)/shard_map/reduce_scatter | solution.py:1026
  70.0 28.6 %collective-permute-start.10 = (bf16[1,512,1152]{2,1,0:T(8,128)(2,1)}, bf16[1,512,1152]{2,1,0:T(8,128)(2,1)S(1)}, u32[]{:S(2)}, u32[]{:S(2)}) collective-permute-start(bf16[1,512,1152]{2,1,0:T(8,128)(2,1)} %refs_2_.3), channel_id=1, source_target_pairs={{0,1},{1,0},{2,3},{3,2},{4,5},{5,4},{6,7},{7,6},{8,9},{9,8},{10,11... | collective-permute-start | bytes 3538952 | tf_op jit(solution)/shard_map/ppermute | solution.py:758
  116.9 22.4 %collective-permute-start.11 = (bf16[1,512,576]{1,2,0:T(8,128)(2,1)S(1)}, bf16[1,512,576]{1,2,0:T(8,128)(2,1)}, u32[]{:S(2)}, u32[]{:S(2)}) collective-permute-start(bf16[1,512,576]{1,2,0:T(8,128)(2,1)S(1)} %copy.70), channel_id=1, source_target_pairs={{0,1},{1,0},{2,3},{3,2},{4,5},{5,4},{6,7},{7,6},{8,9},{9,8},{10,11... | collective-permute-start | bytes 1769480 | tf_op jit(solution)/shard_map/ppermute | solution.py:758
  120.8 15.7 %collective-permute-start.12 = (bf16[1,120,576]{2,1,0:T(8,128)(2,1)S(1)}, bf16[1,120,576]{2,1,0:T(8,128)(2,1)S(1)}, u32[]{:S(2)}, u32[]{:S(2)}) collective-permute-start(bf16[1,120,576]{2,1,0:T(8,128)(2,1)S(1)} %slice.159), channel_id=1, source_target_pairs={{0,1},{1,0},{2,3},{3,2},{4,5},{5,4},{6,7},{7,6},{8,9},{9,8},{10,11... | collective-permute-start | bytes 414728 | tf_op jit(solution)/shard_map/ppermute | solution.py:758
  121.5 16.9 %collective-permute-start.13 = (bf16[1,120,576]{2,1,0:T(8,128)(2,1)S(1)}, bf16[1,120,576]{2,1,0:T(8,128)(2,1)S(1)}, u32[]{:S(2)}, u32[]{:S(2)}) collective-permute-start(bf16[1,120,576]{2,1,0:T(8,128)(2,1)S(1)} %fusion.3), channel_id=1, source_target_pairs={{0,1},{1,0},{2,3},{3,2},{4,5},{5,4},{6,7},{7,6},{8,9},{9,8},{10,11... | collective-permute-start | bytes 414728 | tf_op jit(solution)/shard_map/ppermute | solution.py:758
  159.6 46.0 %collective-permute-start.14 = (bf16[1,512,1152]{2,1,0:T(8,128)(2,1)}, bf16[1,512,1152]{2,1,0:T(8,128)(2,1)S(1)}, u32[]{:S(2)}, u32[]{:S(2)}) collective-permute-start(bf16[1,512,1152]{2,1,0:T(8,128)(2,1)} %get-tuple-element.111.refs_0_), channel_id=1, source_target_pairs={{0,1},{1,0},{2,3},{3,2},{4,5},{5,4},{6,7},{7,6},{8,9},{9,8},{10,11... | collective-permute-start | bytes 3538952 | tf_op jit(solution)/shard_map/ppermute | solution.py:758
  222.7 28.4 %collective-permute-start.15 = (bf16[1,512,1152]{2,1,0:T(8,128)(2,1)}, bf16[1,512,1152]{2,1,0:T(8,128)(2,1)S(1)}, u32[]{:S(2)}, u32[]{:S(2)}) collective-permute-start(bf16[1,512,1152]{2,1,0:T(8,128)(2,1)} %get-tuple-element.113.refs_7_), channel_id=1, source_target_pairs={{0,1},{1,0},{2,3},{3,2},{4,5},{5,4},{6,7},{7,6},{8,9},{9,8},{10,11... | collective-permute-start | bytes 3538952 | tf_op jit(solution)/shard_map/ppermute | solution.py:758
  292.4 15.1 %collective-permute-start.17 = (bf16[1,120,1152]{2,1,0:T(8,128)(2,1)}, bf16[1,120,1152]{2,1,0:T(8,128)(2,1)S(1)}, u32[]{:S(2)}, u32[]{:S(2)}) collective-permute-start(bf16[1,120,1152]{2,1,0:T(8,128)(2,1)} %get-tuple-element.129), channel_id=1, source_target_pairs={{0,1},{1,0},{2,3},{3,2},{4,5},{5,4},{6,7},{7,6},{8,9},{9,8},{10,11... | collective-permute-start | bytes 829448 | tf_op jit(solution)/shard_map/ppermute | solution.py:758
  293.9 19.0 %collective-permute-start.18 = (bf16[1,256,1152]{2,1,0:T(8,128)(2,1)}, bf16[1,256,1152]{2,1,0:T(8,128)(2,1)S(1)}, u32[]{:S(2)}, u32[]{:S(2)}) collective-permute-start(bf16[1,256,1152]{2,1,0:T(8,128)(2,1)} %copy-done.60), channel_id=1, source_target_pairs={{0,1},{1,0},{2,3},{3,2},{4,5},{5,4},{6,7},{7,6},{8,9},{9,8},{10,11... | collective-permute-start | bytes 1769480 | tf_op jit(solution)/shard_map/ppermute | solution.py:758
  321.4 55.4 %collective-permute-start.16 = (bf16[1,512,1152]{2,1,0:T(8,128)(2,1)}, bf16[1,512,1152]{2,1,0:T(8,128)(2,1)S(1)}, u32[]{:S(2)}, u32[]{:S(2)}) collective-permute-start(bf16[1,512,1152]{2,1,0:T(8,128)(2,1)} %get-tuple-element.127), channel_id=1, source_target_pairs={{0,1},{1,0},{2,3},{3,2},{4,5},{5,4},{6,7},{7,6},{8,9},{9,8},{10,11... | collective-permute-start | bytes 3538952 | tf_op jit(solution)/shard_map/ppermute | solution.py:758
  332.2 61.8 %collective-permute-start.26 = (bf16[4,72,3456]{2,1,0:T(8,128)(2,1)}, bf16[4,72,3456]{2,1,0:T(8,128)(2,1)}, u32[]{:S(2)}, u32[]{:S(2)}) collective-permute-start(bf16[4,72,3456]{2,1,0:T(8,128)(2,1)} %get-tuple-element.160), channel_id=1, source_target_pairs={{0,4},{2,6},{4,0},{6,2},{8,12},{10,14},{12,8},{14,10},{16,20},{18,... | collective-permute-start | bytes 5971976 | tf_op jit(solution)/shard_map/ppermute | solution.py:724
  394.0 30.8 %collective-permute-start.31 = (bf16[1,512,1152]{2,1,0:T(8,128)(2,1)S(1)}, bf16[1,512,1152]{2,1,0:T(8,128)(2,1)S(1)}, u32[]{:S(2)}, u32[]{:S(2)}) collective-permute-start(bf16[1,512,1152]{2,1,0:T(8,128)(2,1)S(1)} %copy-done.76), channel_id=1, source_target_pairs={{0,1},{1,0},{2,3},{3,2},{4,5},{5,4},{6,7},{7,6},{8,9},{9,8},{10,11... | collective-permute-start | bytes 3538952 | tf_op jit(solution)/shard_map/ppermute | solution.py:758
  399.7 54.0 %collective-permute-start.27 = (bf16[4,72,3008]{2,1,0:T(8,128)(2,1)S(1)}, bf16[4,72,3008]{2,1,0:T(8,128)(2,1)S(1)}, u32[]{:S(2)}, u32[]{:S(2)}) collective-permute-start(bf16[4,72,3008]{2,1,0:T(8,128)(2,1)S(1)} %get-tuple-element.163), channel_id=1, source_target_pairs={{0,4},{2,6},{4,0},{6,2},{8,12},{10,14},{12,8},{14,10},{16,20},{18,... | collective-permute-start | bytes 5197832 | tf_op jit(solution)/shard_map/ppermute | solution.py:724
  401.2 21.1 %collective-permute-start.32 = (f32[1,6912]{1,0:T(1,128)S(1)}, f32[1,6912]{1,0:T(1,128)S(1)}, u32[]{:S(2)}, u32[]{:S(2)}) collective-permute-start(f32[1,6912]{1,0:T(1,128)S(1)} %bitcast.107), channel_id=1, source_target_pairs={{0,1},{1,0},{2,3},{3,2},{4,5},{5,4},{6,7},{7,6},{8,9},{9,8},{10,11... | collective-permute-start | bytes 82952 | tf_op jit(solution)/shard_map/ppermute | solution.py:758
  404.6 35.5 %collective-permute-start.28 = (bf16[72,3456]{1,0:T(8,128)(2,1)S(1)}, bf16[72,3456]{1,0:T(8,128)(2,1)S(1)}, u32[]{:S(2)}, u32[]{:S(2)}) collective-permute-start(bf16[72,3456]{1,0:T(8,128)(2,1)S(1)} %get-tuple-element.164), channel_id=1, source_target_pairs={{0,8},{2,10},{4,12},{6,14},{8,16},{10,18},{12,20},{14,22},{16,24},... | collective-permute-start | bytes 1493000 | tf_op jit(solution)/shard_map/ppermute | solution.py:720
  407.0 41.9 %collective-permute-start.29 = (bf16[72,3456]{1,0:T(8,128)(2,1)S(1)}, bf16[72,3456]{1,0:T(8,128)(2,1)S(1)}, u32[]{:S(2)}, u32[]{:S(2)}) collective-permute-start(bf16[72,3456]{1,0:T(8,128)(2,1)S(1)} %get-tuple-element.165), channel_id=1, source_target_pairs={{0,16},{2,18},{4,20},{6,22},{8,24},{10,26},{12,28},{14,30},{16,0},... | collective-permute-start | bytes 1493000 | tf_op jit(solution)/shard_map/ppermute | solution.py:720
  422.3 28.6 %collective-permute-start.30 = (bf16[72,3456]{1,0:T(8,128)(2,1)S(1)}, bf16[72,3456]{1,0:T(8,128)(2,1)S(1)}, u32[]{:S(2)}, u32[]{:S(2)}) collective-permute-start(bf16[72,3456]{1,0:T(8,128)(2,1)S(1)} %get-tuple-element.166), channel_id=1, source_target_pairs={{0,24},{2,26},{4,28},{6,30},{8,0},{10,2},{12,4},{14,6},{16,8},{18,... | collective-permute-start | bytes 1493000 | tf_op jit(solution)/shard_map/ppermute | solution.py:720
  424.8 27.9 %collective-permute-start.33 = (bf16[1,60,1152]{2,1,0:T(8,128)(2,1)S(1)}, bf16[1,60,1152]{2,1,0:T(8,128)(2,1)S(1)}, u32[]{:S(2)}, u32[]{:S(2)}) collective-permute-start(bf16[1,60,1152]{2,1,0:T(8,128)(2,1)S(1)} %select_convert_fusion), channel_id=1, source_target_pairs={{0,1},{1,0},{2,3},{3,2},{4,5},{5,4},{6,7},{7,6},{8,9},{9,8},{10,11... | collective-permute-start | bytes 414728 | tf_op jit(solution)/shard_map/ppermute | solution.py:758
  451.2 14.5 %collective-permute-start.39 = (bf16[72,3456]{1,0:T(8,128)(2,1)S(1)}, bf16[72,3456]{1,0:T(8,128)(2,1)}, u32[]{:S(2)}, u32[]{:S(2)}) collective-permute-start(bf16[72,3456]{1,0:T(8,128)(2,1)S(1)} %z_sum_kernel.2.refs_3_), channel_id=1, source_target_pairs={{0,1},{1,0},{2,3},{3,2},{4,5},{5,4},{6,7},{7,6},{8,9},{9,8},{10,11... | collective-permute-start | bytes 1493000 | tf_op jit(solution)/shard_map/ppermute | solution.py:758
  455.5 29.8 %collective-permute-start.34 = (bf16[72,3008]{1,0:T(8,128)(2,1)}, bf16[72,3008]{1,0:T(8,128)(2,1)}, u32[]{:S(2)}, u32[]{:S(2)}) collective-permute-start(bf16[72,3008]{1,0:T(8,128)(2,1)} %get-tuple-element.173), channel_id=1, source_target_pairs={{0,8},{2,10},{4,12},{6,14},{8,16},{10,18},{12,20},{14,22},{16,24},... | collective-permute-start | bytes 1299464 | tf_op jit(solution)/shard_map/ppermute | solution.py:720
  455.5 37.5 %collective-permute-start.35 = (bf16[72,3008]{1,0:T(8,128)(2,1)}, bf16[72,3008]{1,0:T(8,128)(2,1)}, u32[]{:S(2)}, u32[]{:S(2)}) collective-permute-start(bf16[72,3008]{1,0:T(8,128)(2,1)} %get-tuple-element.174), channel_id=1, source_target_pairs={{0,16},{2,18},{4,20},{6,22},{8,24},{10,26},{12,28},{14,30},{16,0},... | collective-permute-start | bytes 1299464 | tf_op jit(solution)/shard_map/ppermute | solution.py:720
  456.9 37.0 %collective-permute-start.36 = (bf16[72,3008]{1,0:T(8,128)(2,1)}, bf16[72,3008]{1,0:T(8,128)(2,1)}, u32[]{:S(2)}, u32[]{:S(2)}) collective-permute-start(bf16[72,3008]{1,0:T(8,128)(2,1)} %get-tuple-element.175), channel_id=1, source_target_pairs={{0,24},{2,26},{4,28},{6,30},{8,0},{10,2},{12,4},{14,6},{16,8},{18,... | collective-permute-start | bytes 1299464 | tf_op jit(solution)/shard_map/ppermute | solution.py:720
  458.9 19.0 %collective-permute-start.37 = (bf16[72,4608]{1,0:T(8,128)(2,1)}, bf16[72,4608]{1,0:T(8,128)(2,1)S(1)}, u32[]{:S(2)}, u32[]{:S(2)}) collective-permute-start(bf16[72,4608]{1,0:T(8,128)(2,1)} %reduce-scatter.2.cloned.1.call-done.refs_1_), channel_id=1, source_target_pairs={{0,1},{1,0},{2,3},{3,2},{4,5},{5,4},{6,7},{7,6},{8,9},{9,8},{10,11... | collective-permute-start | bytes 1990664 | tf_op jit(solution)/shard_map/ppermute | solution.py:758
  (91 other events, 843.9 us)
Sparse Core Ops, SparseCore 0:
  10.9 104.6 all-gather.2
  118.5 87.0 all-gather.4
  260.8 134.9 reduce-scatter.1
